TPU v7x, 32 devices: a whole 2x2x4 slice. The times are simulated.
32 devices in a mesh: dp: 2 (over x), fsdp: 16 (over z, y, core).
Axes of the slice: x: 2, y: 2, z: 4, core: 2. Of those that a mesh axis runs over, the one named last changes fastest.
Arguments:
- hidden_in: bfloat16 [8192, 1536], P(('dp', 'fsdp')), may hold values from -6 to 6
- lengths: int32 [32], P(('dp', 'fsdp')), may hold values from 64 to 256, as said below
- cotangent: bfloat16 [8192, 1536], P(('dp', 'fsdp')), may hold values from -6 to 6
- pre_gain: float32 [1536], replicated, may hold values from 0.1 to 1.9
- in_weight: bfloat16 [1536, 6448], P(('dp', 'fsdp')), may hold values from -0.15625 to 0.15625
- conv_weight: float32 [4, 3328], replicated, may hold values from -3 to 3
- conv_bias: float32 [3328], replicated, may hold values from -3 to 3
- dt_bias: float32 [48], replicated, may hold values from -6.9 to -2.3
- a_log: float32 [48], replicated, may hold values from 0 to 2.77
- skip: float32 [48], replicated, may hold values from 0.5 to 2
- inner_gain: float32 [3072], replicated, may hold values from 0.1 to 1.9
- out_weight: bfloat16 [1536, 3072], P(('dp', 'fsdp')), may hold values from -0.109375 to 0.109375
Outputs:
- output: bfloat16 [8192, 1536], P(('dp', 'fsdp'))
- grad_hidden: bfloat16 [8192, 1536], P(('dp', 'fsdp'))
- grad_pre_gain: float32 [1536], replicated
- grad_in_weight: float32 [1536, 6448], P(('dp', 'fsdp'))
- grad_conv_weight: float32 [4, 3328], replicated
- grad_conv_bias: float32 [3328], replicated
- grad_dt_bias: float32 [48], replicated
- grad_a_log: float32 [48], replicated
- grad_skip: float32 [48], replicated
- grad_inner_gain: float32 [3072], replicated
- grad_out_weight: float32 [1536, 3072], P(('dp', 'fsdp'))
Inputs may be any that keep to these rules, and one draw needn't show every extreme that they name: lengths of the slots' sequences; in every draw one slot has exactly 256 and one exactly 64.
All inputs are finite; a program needn't handle non-finite values.
Results may differ from a plain program's by a relative error of at most 0.0075.
Values may be sent and summed in bfloat16 or wider, within the bound.
No kernel may reach another device: no remote copies, remote signals or barrier semaphores. Data moves between devices by JAX's collectives and lax.ppermute only.
A program may use at most 320 MiB of HBM per device.

v0:
```python
import jax
import jax.numpy as jnp
from jax import lax
from jax.sharding import PartitionSpec as P

SPAN = 256


EPSILON = 1e-05
PRECISE = lax.Precision.HIGHEST


def prenorm(stream, gain):
    return stream * lax.rsqrt(jnp.mean(stream * stream, axis=-1, keepdims=True) + EPSILON) * gain


def causal_conv(conv_input, taps_weight, taps_bias):
    seq_length = conv_input.shape[0]
    kernel_taps = taps_weight.shape[0]
    padded = jnp.concatenate(
        [jnp.zeros((kernel_taps - 1, conv_input.shape[1]), conv_input.dtype), conv_input], axis=0
    )
    summed = jnp.zeros_like(conv_input) + taps_bias[None, :]
    for tap in range(kernel_taps):
        summed = summed + taps_weight[tap][None, :] * padded[tap : tap + seq_length]
    return jax.nn.silu(summed)


def scan_states(values, b_rows, c_rows, step_size, decay_rate, skip):
    seq_length = values.shape[0]
    block_count = seq_length // SPAN
    head_count = values.shape[1]
    head_width = values.shape[2]
    state_width = b_rows.shape[1]
    causal = jnp.arange(SPAN)[:, None] >= jnp.arange(SPAN)[None, :]

    def step(carried_state, pieces):
        x_block, b_block, c_block, step_block = pieces
        cumulative = jnp.cumsum(step_block * decay_rate[None, :], axis=0)
        spread = jnp.where(causal[:, :, None], cumulative[:, None, :] - cumulative[None, :, :], 0.0)
        decays = jnp.where(causal[:, :, None], jnp.exp(spread), 0.0)
        scores = jnp.dot(c_block, b_block.T, precision=PRECISE)
        mixing = scores[:, :, None] * decays * step_block[None, :, :]
        within = jnp.einsum("tsh,shp->thp", mixing, x_block, precision=PRECISE)
        carried = (
            jnp.einsum("tn,hpn->thp", c_block, carried_state, precision=PRECISE)
            * jnp.exp(cumulative)[:, :, None]
        )
        tail_decay = jnp.exp(cumulative[-1][None, :] - cumulative) * step_block
        weighted = tail_decay[:, :, None] * x_block
        fresh_state = jnp.einsum("shp,sn->hpn", weighted, b_block, precision=PRECISE)
        carried_state = carried_state * jnp.exp(cumulative[-1])[:, None, None] + fresh_state
        return (carried_state, within + carried + skip[None, :, None] * x_block)

    initial = jnp.zeros((head_count, head_width, state_width), jnp.float32)
    pieces = (
        values.reshape(block_count, SPAN, head_count, head_width),
        b_rows.reshape(block_count, SPAN, state_width),
        c_rows.reshape(block_count, SPAN, state_width),
        step_size.reshape(block_count, SPAN, head_count),
    )
    final_state, outputs = lax.scan(jax.checkpoint(step), initial, pieces)
    return outputs.reshape(seq_length, head_count * head_width)


def mixer(gate_part, conv_out, step_raw, dt_bias, a_log, skip, inner_gain):
    inner_width = gate_part.shape[1]
    head_count = step_raw.shape[1]
    state_width = (conv_out.shape[1] - inner_width) // 2
    values = conv_out[:, :inner_width].reshape(
        conv_out.shape[0], head_count, inner_width // head_count
    )
    b_rows = conv_out[:, inner_width : inner_width + state_width]
    c_rows = conv_out[:, inner_width + state_width :]
    step_size = jax.nn.softplus(step_raw + dt_bias[None, :])
    decay_rate = -jnp.exp(a_log)
    scanned = scan_states(values, b_rows, c_rows, step_size, decay_rate, skip)
    gated_out = scanned * jax.nn.silu(gate_part)
    return (
        gated_out
        * lax.rsqrt(jnp.mean(gated_out * gated_out, axis=-1, keepdims=True) + EPSILON)
        * inner_gain
    )


def fetch(in_weight, out_weight):
    return (
        lax.all_gather(in_weight, ("dp", "fsdp"), axis=0, tiled=True),
        lax.all_gather(out_weight, ("dp", "fsdp"), axis=0, tiled=True),
    )


def spread_gradients(grad_in_weight, grad_out_weight):
    outer_count = lax.axis_size("dp")
    inner_count = lax.axis_size("fsdp")
    row_count = grad_in_weight.shape[0] // (outer_count * inner_count)
    shaped_in = grad_in_weight.reshape(outer_count, inner_count, row_count, grad_in_weight.shape[1])
    shaped_out = grad_out_weight.reshape(
        outer_count, inner_count, row_count, grad_out_weight.shape[1]
    )
    moved_in, moved_out = (
        lax.all_to_all(
            shaped_in.astype(jnp.bfloat16), "fsdp", split_axis=1, concat_axis=0, tiled=True
        ).astype(shaped_in.dtype),
        lax.all_to_all(
            shaped_out.astype(jnp.bfloat16), "fsdp", split_axis=1, concat_axis=0, tiled=True
        ).astype(shaped_out.dtype),
    )
    group_in = jnp.sum(
        moved_in.reshape(inner_count, outer_count, row_count, grad_in_weight.shape[1]), axis=0
    )
    group_out = jnp.sum(
        moved_out.reshape(inner_count, outer_count, row_count, grad_out_weight.shape[1]), axis=0
    )
    crossed_in, crossed_out = (
        lax.all_to_all(
            group_in.astype(jnp.bfloat16), "dp", split_axis=0, concat_axis=0, tiled=True
        ).astype(group_in.dtype),
        lax.all_to_all(
            group_out.astype(jnp.bfloat16), "dp", split_axis=0, concat_axis=0, tiled=True
        ).astype(group_out.dtype),
    )
    owned_in = jnp.sum(crossed_in, axis=0)
    owned_out = jnp.sum(crossed_out, axis=0)
    return (owned_in, owned_out)


def body(
    hidden_in,
    lengths,
    cotangent,
    pre_gain,
    in_weight,
    conv_weight,
    conv_bias,
    dt_bias,
    a_log,
    skip,
    inner_gain,
    out_weight,
):
    whole_in, whole_out = fetch(in_weight, out_weight)
    stream = hidden_in.astype(jnp.float32)
    seq_length = stream.shape[0]
    valid_mask = (jnp.arange(seq_length) < lengths[0]).astype(jnp.float32)[:, None]
    normed, pull_norm = jax.vjp(prenorm, stream, pre_gain)
    normed_low = normed.astype(jnp.bfloat16)
    projected = jnp.dot(normed_low, whole_in, preferred_element_type=jnp.float32)
    inner_width = whole_out.shape[1]
    head_count = dt_bias.shape[0]
    proj_width = projected.shape[1]
    gate_part = projected[:, :inner_width]
    conv_input = projected[:, inner_width : proj_width - head_count]
    step_raw = projected[:, proj_width - head_count :]
    conv_out, pull_conv = jax.vjp(causal_conv, conv_input, conv_weight, conv_bias)
    conv_low = lax.optimization_barrier(conv_out.astype(jnp.bfloat16)).astype(jnp.float32)
    mixed_out, pull_mix = jax.vjp(
        mixer, gate_part, conv_low, step_raw, dt_bias, a_log, skip, inner_gain
    )
    mixed_low = mixed_out.astype(jnp.bfloat16)
    branch = lax.dot_general(
        mixed_low, whole_out, (((1,), (1,)), ((), ())), preferred_element_type=jnp.float32
    )
    output = (valid_mask * (stream + branch)).astype(jnp.bfloat16)
    back_in, back_out = fetch(in_weight, out_weight)
    upstream = cotangent * valid_mask.astype(jnp.bfloat16)
    grad_out_weight = lax.dot_general(
        upstream, mixed_low, (((0,), (0,)), ((), ())), preferred_element_type=jnp.float32
    )
    grad_mixed = jnp.dot(upstream, back_out, preferred_element_type=jnp.float32)
    (
        grad_gate,
        grad_conv_out,
        grad_step_raw,
        grad_dt_bias,
        grad_a_log,
        grad_skip,
        grad_inner_gain,
    ) = pull_mix(grad_mixed)
    grad_conv_input, grad_conv_weight, grad_conv_bias = pull_conv(grad_conv_out)
    grad_projected = jnp.concatenate([grad_gate, grad_conv_input, grad_step_raw], axis=1).astype(
        jnp.bfloat16
    )
    grad_in_weight = lax.dot_general(
        normed_low, grad_projected, (((0,), (0,)), ((), ())), preferred_element_type=jnp.float32
    )
    grad_normed = lax.dot_general(
        grad_projected, back_in, (((1,), (1,)), ((), ())), preferred_element_type=jnp.float32
    )
    grad_stream, grad_pre_gain = pull_norm(grad_normed)
    grad_hidden = (upstream.astype(jnp.float32) + grad_stream).astype(jnp.bfloat16)
    owned_in, owned_out = spread_gradients(grad_in_weight, grad_out_weight)
    small_sums = lax.psum(
        (
            grad_pre_gain,
            grad_conv_weight,
            grad_conv_bias,
            grad_dt_bias,
            grad_a_log,
            grad_skip,
            grad_inner_gain,
        ),
        ("dp", "fsdp"),
    )
    return (
        output,
        grad_hidden,
        small_sums[0],
        owned_in,
        small_sums[1],
        small_sums[2],
        small_sums[3],
        small_sums[4],
        small_sums[5],
        small_sums[6],
        owned_out,
    )


def solution(mesh):
    in_specs = (
        P(("dp", "fsdp"), None),
        P(("dp", "fsdp")),
        P(("dp", "fsdp"), None),
        P(),
        P(("dp", "fsdp"), None),
        P(),
        P(),
        P(),
        P(),
        P(),
        P(),
        P(("dp", "fsdp"), None),
    )
    out_specs = (
        P(("dp", "fsdp"), None),
        P(("dp", "fsdp"), None),
        P(),
        P(("dp", "fsdp"), None),
        P(),
        P(),
        P(),
        P(),
        P(),
        P(),
        P(("dp", "fsdp"), None),
    )
    return jax.shard_map(body, mesh=mesh, in_specs=in_specs, out_specs=out_specs, check_vma=False)
```

profile of v0, /device:TPU:16, one launch (start us, length us, event | category | flops | bytes accessed | tf_op | source)
XLA Modules:
  0.0 961.1 jit_solution(3690587650820404867)
XLA Ops:
  7.2 0.7 all-gather.3.cloned.1.call-update
  8.0 0.7 all-gather.5.cloned.1.call-update
  9.8 0.7 iota_compare_fusion
  10.5 1.1 slice_reduce_fusion.6
  11.6 1.4 fusion.56
  13.0 1.2 exponential_negate_fusion
  14.2 127.0 %all-gather.3.cloned.1.call-done = bf16[1536,6448]{1,0:T(8,128)(2,1)} async-done(((bf16[48,6448]{1,0:T(8,128)(2,1)}), bf16[1536,6448]{1,0:T(8,128)(2,1)}) %all-gather.3.cloned.1.call-update) | async-done | bytes 19808272 | tf_op jit(solution)/shard_map/all_gather | solution.py:88
  141.1 13.1 %fusion.76 = f32[256,6448]{0,1:T(8,128)S(1)} fusion(bf16[1536,6448]{1,0:T(8,128)(2,1)} %all-gather.3.cloned.1.call-done, bf16[256,1536]{1,0:T(8,128)(2,1)} %param.12, f32[1536]{0:T(1024)} %param.15, f32[256]{0:T(256)S(1)} %fusion.92), kind=kOutput, calls=%fused_computation.119 | convolution fusion | flops 5072486400 | bytes 27204608 | tf_op jit(solution)/shard_map/dot_general | solution.py:148
  154.5 2.6 copy-done.7
  157.1 6.9 multiply_convert_fusion
  163.9 1.4 slice.87.clone.1
  165.9 0.5 slice-done.4
  166.5 0.9 broadcast_multiply_fusion.5
  167.4 0.7 copy.124
  168.1 1.5 reduce-window.36
  169.8 0.7 copy.126
  170.7 1.2 fusion.87
  171.9 2.4 fusion.68
  174.3 9.8 %fusion.36 = f32[256,48,64]{0,2,1:T(8,128)S(1)} fusion(f32[256,48,64]{0,2,1:T(8,128)S(1)} %bitcast.130, f32[256,48,64]{0,2,1:T(8,128)S(1)} %fusion.68, bf16[256,48,64]{0,2,1:T(8,128)(2,1)S(1)} %bitcast.141, f32[256,48]{0,1:T(8,128)S(1)} %copy-done.37, f32[256,48]{0,1:T(8,128)S(1)} %bitcast_bitcast_fusion, f32[256,256]{1,0:T(8,128)S(1)} %fusion.87, ...), kind=kOutput, calls=%fused_computation.63 | convolution fusion | flops 2434793472 | bytes 11485376 | tf_op jit(solution)/shard_map/jvp()/while/body/eval_jaxpr/tsh,shp->thp/dot_general | solution.py:44
  184.2 1.1 multiply_reduce_fusion.10
  185.9 6.5 convolution_convert_fusion.1
  192.4 9.6 %copy.154 = bf16[2,16,48,3072]{3,2,0,1:T(8,128)(2,1)} copy(bf16[2,16,48,3072]{3,2,1,0:T(8,128)(2,1)} %bitcast.124) | data formatting | bytes 18874368 | tf_op jit(solution)/shard_map/convert_element_type | solution.py:106
  202.0 5.7 all-to-all-start.2
  207.7 67.3 %all-gather.5.cloned.1.call-done = bf16[1536,3072]{1,0:T(8,128)(2,1)} async-done(((bf16[48,3072]{1,0:T(8,128)(2,1)}), bf16[1536,3072]{1,0:T(8,128)(2,1)}) %all-gather.5.cloned.1.call-update) | async-done | bytes 9437200 | tf_op jit(solution)/shard_map/all_gather | solution.py:89
  275.0 8.8 multiply_reduce_fusion.5
  283.8 0.9 fusion.105
  284.7 5.3 fusion.32
  290.3 4.2 multiply_reduce_fusion.7
  294.7 0.6 reduce-window.38
  296.3 21.8 %fusion.14 = (f32[256,48]{0,1:T(8,128)S(1)}, f32[256,48]{0,1:T(8,128)S(1)}, f32[256,48]{0,1:T(8,128)S(1)}, f32[256,256]{1,0:T(8,128)S(1)}) fusion(f32[256,256]{1,0:T(8,128)S(1)} %fusion.106, f32[256,48]{0,1:T(8,128)S(1)} %copy.133, f32[256,48]{0,1:T(8,128)S(1)} %copy.132, pred[256,256]{1,0:T(8,128)(4,1)S(1)} %copy-done.28, f32[256,48,64]{0,2,1:T(8,128)} %bitcast.131, ...), kind=kOutput, calls=%fused_computation.20 | convolution fusion | flops 2463002624 | bytes 7127040 | tf_op jit(solution)/shard_map/transpose(jvp())/while/body/eval_jaxpr/checkpoint/tsh,shp->thp/dot_general | solution.py:44
  318.4 6.8 multiply_reduce_fusion.6
  326.4 2.7 reduce-window.40
  329.5 1.5 fusion.101
  331.1 5.0 fusion.65
  336.5 2.9 fusion.62
  339.9 12.5 %bitcast_add_fusion = f32[256,48,64]{0,2,1:T(8,128)} fusion(f32[256,48,64]{0,2,1:T(8,128)S(1)} %copy-done.13, f32[256,48,64]{0,2,1:T(8,128)S(1)} %bitcast.129, f32[256,256]{1,0:T(8,128)S(1)} %copy-done.20, f32[256,48]{0,1:T(8,128)S(1)} %copy-done.36, f32[256,48]{0,1:T(8,128)S(1)} %copy-done.34, pred[256,256]{1,0:T(8,128)(4,1)S(1)} %copy-done.29, ...), kind=kOutput, calls=%fused_computation.56 | convolution fusion | flops 2434793472 | bytes 9912512 | tf_op jit(solution)/shard_map/transpose(jvp())/while/body/eval_jaxpr/checkpoint/tsh,shp->thp/dot_general | solution.py:44
  352.4 9.2 multiply_reduce_fusion.3
  361.6 4.1 broadcast_multiply_fusion
  365.8 2.7 fusion.29
  368.6 11.1 %convolution_convert_fusion = bf16[1536,6448]{0,1:T(8,128)(2,1)} fusion(bf16[256,48]{0,1:T(8,128)(2,1)S(1)} %copy.150, bf16[256,3328]{0,1:T(8,128)(2,1)S(1)} %fusion.29, bf16[256,3072]{0,1:T(8,128)(2,1)} %get-tuple-element.217, bf16[256,1536]{1,0:T(8,128)(2,1)S(1)} %copy-done.14, f32[1536]{0:T(1024)S(1)} %copy-done.43, f32[256]{0:T(256)S(1)} %copy-done.49), kind=kOutput, calls=%fused_computation | convolution fusion | flops 5092294656 | bytes 23903232 | tf_op jit(solution)/shard_map/dot_general | solution.py:184
  379.6 24.4 %copy.151 = bf16[1536,6448]{1,0:T(8,128)(2,1)} copy(bf16[1536,6448]{0,1:T(8,128)(2,1)} %convolution_convert_fusion) | data formatting | bytes 39616512 | tf_op jit(solution)/shard_map/convert_element_type | solution.py:103
  404.1 17.3 %copy.152 = bf16[2,16,48,6448]{3,2,0,1:T(8,128)(2,1)} copy(bf16[2,16,48,6448]{3,2,1,0:T(8,128)(2,1)} %bitcast.123) | data formatting | bytes 39616512 | tf_op jit(solution)/shard_map/convert_element_type | solution.py:103
  421.4 1.3 all-to-all-done.2
  422.8 9.3 all-to-all-start
  432.7 0.7 pad_add_fusion.3
  433.4 12.0 %fusion.53 = (f32[1536]{0:T(1024)}, f32[256]{0:T(256)S(1)}, f32[256,1536]{1,0:T(8,128)}) fusion(bf16[256,1536]{1,0:T(8,128)(2,1)S(1)} %copy-done.14, f32[256]{0:T(256)S(1)} %copy-done.49, f32[1536]{0:T(1024)S(1)} %copy-done.43, bf16[1536,6448]{1,0:T(8,128)(2,1)} %all-gather.3.cloned.1.call-done, bf16[256,48]{0,1:T(8,128)(2,1)S(1)} %copy.150, ...), kind=kOutput, calls=%fused_computation.93 | convolution fusion | flops 5083568128 | bytes 25483264 | tf_op jit(solution)/shard_map/dot_general | solution.py:187
  445.4 6.7 reduce_sum.341
  452.1 413.9 %all-to-all-done = bf16[2,16,48,6448]{3,2,0,1:T(8,128)(2,1)} async-done(((bf16[2,16,48,6448]{3,2,0,1:T(8,128)(2,1)}), bf16[2,16,48,6448]{3,2,0,1:T(8,128)(2,1)}, u32[]{:S(2)}, u32[]{:S(2)}) %all-to-all-start) | async-done | bytes 19808288 | tf_op jit(solution)/shard_map/all_to_all | solution.py:102
  866.0 4.2 all-to-all-start.3
  870.3 7.9 fusion.43
  878.2 11.8 %reduce_sum.321 = bf16[2,48,6448]{2,1,0:T(8,128)(2,1)} reduce(bf16[2,16,48,6448]{3,2,0,1:T(8,128)(2,1)} %all-to-all-done, bf16[]{:T(256)} %constant.89.clone.1), dimensions={1}, to_apply=%region_20.21 | reduce | flops 9285120 | bytes 21046274 | tf_op jit(solution)/shard_map/reduce_sum | solution.py:109
  890.0 3.6 all-to-all-start.1
  893.7 2.9 fusion.55
  896.5 2.0 convert_reduce_fusion.1
  898.6 11.0 %all-to-all-done.1 = bf16[2,48,6448]{2,1,0:T(8,128)(2,1)S(1)} async-done(((bf16[2,48,6448]{2,1,0:T(8,128)(2,1)}), bf16[2,48,6448]{2,1,0:T(8,128)(2,1)S(1)}, u32[]{:S(2)}, u32[]{:S(2)}) %all-to-all-start.1) | async-done | bytes 1238048 | tf_op jit(solution)/shard_map/all_to_all | solution.py:116
  909.6 1.2 convert_reduce_fusion
  910.8 34.5 %all-reduce.17.cloned.1.call-done = (f32[1536]{0:T(1024)}, f32[4,3328]{1,0:T(4,128)}, f32[3328]{0:T(1024)}, f32[48]{0:T(128)}, f32[48]{0:T(128)}, /*index=5*/f32[48]{0:T(128)}, f32[3072]{0:T(1024)}) async-done(((f32[1536]{0:T(1024)}, f32[4,3328]{1,0:T(4,128)}, f32[3328]{0:T(1024)}, f32[48]{0:T(128)}, f32[48]{0:T(128)}, /*index=5*/f32[48]{0:T(128)}, f32[3072]{0:T(1024)}), (f32[1536]{0:T(1024)}, ...) | async-done | bytes 85584 | tf_op jit(solution)/shard_map/psum | solution.py:193
  945.3 1.3 copy.181
  946.6 1.4 copy.182
  948.1 1.3 copy.183
  949.4 1.1 copy.184
  950.5 1.1 copy.185
  951.6 1.1 copy.186
  952.8 1.3 copy.187
  (171 shorter events, 7.3 us)
Async XLA Ops:
  7.2 134.0 %all-gather.3.cloned.1.call-start = ((), (), s32[]{:S(2)}) async-start(), calls=%async_computation.4 | async-start | bytes 20680704 | tf_op jit(solution)/shard_map/all_gather | solution.py:88
  7.9 267.1 %all-gather.5.cloned.1.call-start = ((), (), s32[]{:S(2)}) async-start(), calls=%async_computation.5 | async-start | bytes 9732096 | tf_op jit(solution)/shard_map/all_gather | solution.py:89
  11.6 145.5 %copy-start.21 = (f32[3328]{0:T(1024)}, f32[3328]{0:T(1024)S(1)}, u32[]{:S(2)}) copy-start(f32[3328]{0:T(1024)S(1)} %get-tuple-element.198) | copy-start | bytes 39940
  11.6 145.4 %copy-start.23 = (f32[3328]{0:T(1024)}, f32[3328]{0:T(1024)S(1)}, u32[]{:S(2)}) copy-start(f32[3328]{0:T(1024)S(1)} %get-tuple-element.199) | copy-start | bytes 39940
  11.6 145.4 %copy-start.25 = (f32[3328]{0:T(1024)}, f32[3328]{0:T(1024)S(1)}, u32[]{:S(2)}) copy-start(f32[3328]{0:T(1024)S(1)} %get-tuple-element.200) | copy-start | bytes 39940
  13.0 141.2 %copy-start.41 = (f32[256]{0:T(256)}, f32[256]{0:T(256)S(1)}, u32[]{:S(2)}) copy-start(f32[256]{0:T(256)S(1)} %fusion.56) | copy-start | bytes 3076
  14.2 140.1 %copy-start.48 = (f32[256]{0:T(256)}, f32[256]{0:T(256)S(1)}, u32[]{:S(2)}) copy-start(f32[256]{0:T(256)S(1)} %fusion.92) | copy-start | bytes 3076
  154.2 2.8 copy-start.7
  154.2 2.8 copy-start.38
  157.0 6.9 copy-start.1
  163.9 1.7 copy-start.6
  165.6 0.8 slice-start.4
  166.4 7.8 copy-start.5
  166.5 17.6 %copy-start.17 = (f32[256,48]{1,0:T(8,128)}, f32[256,48]{1,0:T(8,128)S(1)}, u32[]{:S(2)}) copy-start(f32[256,48]{1,0:T(8,128)S(1)} %copy.168) | copy-start | bytes 147460
  168.1 6.1 copy-start.27
  168.1 6.2 copy-start.50
  170.5 3.7 copy-start.16
  170.5 3.8 copy-start.37
  171.9 12.3 %slice-start = ((s8[6602752]{0:T(1024)(128)(4,1)}), s8[4194304]{0:T(1024)(128)(4,1)S(1)}, s32[]{:S(2)}) async-start(s8[6602752]{0:T(1024)(128)(4,1)} %bitcast.134), calls=%async_computation.7 | async-start | bytes 8388608
  174.3 9.8 %slice-start.1 = ((s8[6602752]{0:T(1024)(128)(4,1)}), s8[2408448]{0:T(1024)(128)(4,1)S(1)}, s32[]{:S(2)}) async-start(s8[6602752]{0:T(1024)(128)(4,1)} %bitcast.134), calls=%async_computation.8 | async-start | bytes 4816896
  184.2 1.6 copy-start.9
  184.2 1.7 copy-start.11
  184.2 1.7 copy-start.30
  184.2 1.7 copy-start.46
  185.8 98.9 %copy-start.3 = (f32[256,3072]{0,1:T(8,128)}, f32[256,3072]{0,1:T(8,128)S(1)}, u32[]{:S(2)}) copy-start(f32[256,3072]{0,1:T(8,128)S(1)} %get-tuple-element.214) | copy-start | bytes 9437188
  185.8 89.2 %copy-start.39 = (f32[256]{0:T(256)}, f32[256]{0:T(256)S(1)}, u32[]{:S(2)}) copy-start(f32[256]{0:T(256)S(1)} %fusion.93) | copy-start | bytes 3076
  202.0 220.8 %all-to-all-start.2 = ((bf16[2,16,48,3072]{3,2,0,1:T(8,128)(2,1)}), bf16[2,16,48,3072]{3,2,0,1:T(8,128)(2,1)}, u32[]{:S(2)}, u32[]{:S(2)}) async-start(bf16[2,16,48,3072]{3,2,0,1:T(8,128)(2,1)} %copy.154), calls=%async_computation.2 | async-start | bytes 18874368 | tf_op jit(solution)/shard_map/all_to_all | solution.py:105
  275.0 9.7 %copy-start.10 = (f32[256,48,64]{0,2,1:T(8,128)S(1)}, f32[256,48,64]{0,2,1:T(8,128)}, u32[]{:S(2)}) copy-start(f32[256,48,64]{0,2,1:T(8,128)} %copy-done.9) | copy-start | bytes 9437188
  275.0 9.7 %copy-start.31 = (f32[3072]{0:T(1024)S(1)}, f32[3072]{0:T(1024)}, u32[]{:S(2)}) copy-start(f32[3072]{0:T(1024)} %param.22) | copy-start | bytes 36868
  290.0 6.2 copy-start.33
  290.0 4.6 copy-start.44
  290.2 6.0 copy-start.28
  295.8 22.3 %copy-start.35 = (f32[256,48]{0,1:T(8,128)}, f32[256,48]{0,1:T(8,128)S(1)}, u32[]{:S(2)}) copy-start(f32[256,48]{0,1:T(8,128)S(1)} %copy.133) | copy-start | bytes 147460
  296.2 21.8 %copy-start.19 = (f32[256,256]{1,0:T(8,128)}, f32[256,256]{1,0:T(8,128)S(1)}, u32[]{:S(2)}) copy-start(f32[256,256]{1,0:T(8,128)S(1)} %fusion.106) | copy-start | bytes 786436
  325.2 4.3 copy-start.18
  331.1 5.4 copy-start
  336.1 3.7 copy-start.13
  336.1 3.7 copy-start.20
  336.1 3.7 copy-start.29
  336.1 3.7 copy-start.34
  336.1 3.7 copy-start.36
  336.1 3.7 copy-start.51
  336.5 15.9 %slice-start.2 = ((s8[6602752]{0:T(1024)(128)(4,1)}), s8[4194304]{0:T(1024)(128)(4,1)S(1)}, s32[]{:S(2)}) async-start(s8[6602752]{0:T(1024)(128)(4,1)} %bitcast.136), calls=%async_computation.9 | async-start | bytes 8388608
  339.9 12.5 %copy-start.2 = (f32[256,3328]{0,1:T(8,128)S(1)}, f32[256,3328]{0,1:T(8,128)}, u32[]{:S(2)}) copy-start(f32[256,3328]{0,1:T(8,128)} %copy-done.1) | copy-start | bytes 10223620
  339.9 12.5 %slice-start.3 = ((s8[6602752]{0:T(1024)(128)(4,1)}), s8[2408448]{0:T(1024)(128)(4,1)S(1)}, s32[]{:S(2)}) async-start(s8[6602752]{0:T(1024)(128)(4,1)} %bitcast.136), calls=%async_computation.10 | async-start | bytes 4816896
  339.9 12.5 %copy-start.8 = (f32[256,3328]{0,1:T(8,128)S(1)}, f32[256,3328]{0,1:T(8,128)}, u32[]{:S(2)}) copy-start(f32[256,3328]{0,1:T(8,128)} %get-tuple-element.216) | copy-start | bytes 10223620
  352.4 9.2 copy-start.22
  352.4 9.2 copy-start.24
  352.4 9.2 copy-start.26
  365.8 2.7 copy-start.14
  365.8 2.7 copy-start.43
  365.8 2.7 copy-start.49
  421.4 10.8 %copy-start.52 = (f32[48]{0:T(128)S(1)}, f32[48]{0:T(128)}, u32[]{:S(2)}) copy-start(f32[48]{0:T(128)} %param.20) | copy-start | bytes 580
  422.8 443.2 %all-to-all-start = ((bf16[2,16,48,6448]{3,2,0,1:T(8,128)(2,1)}), bf16[2,16,48,6448]{3,2,0,1:T(8,128)(2,1)}, u32[]{:S(2)}, u32[]{:S(2)}) async-start(bf16[2,16,48,6448]{3,2,0,1:T(8,128)(2,1)} %copy.152), calls=%async_computation | async-start | bytes 40108032 | tf_op jit(solution)/shard_map/all_to_all | solution.py:102
  432.1 513.3 %all-reduce.17.cloned.1.call-start = ((), (), s32[]{:S(2)}) async-start(), calls=%async_computation.6 | async-start | bytes 183296 | tf_op jit(solution)/shard_map/psum | solution.py:193
  445.4 424.8 %copy-start.4 = (f32[256,3072]{0,1:T(8,128)S(1)}, f32[256,3072]{0,1:T(8,128)}, u32[]{:S(2)}) copy-start(f32[256,3072]{0,1:T(8,128)} %copy-done.3) | copy-start | bytes 9437188
  445.4 424.8 %copy-start.32 = (f32[3072]{0:T(1024)S(1)}, f32[3072]{0:T(1024)}, u32[]{:S(2)}) copy-start(f32[3072]{0:T(1024)} %param.22) | copy-start | bytes 36868
  445.4 424.8 %copy-start.40 = (f32[256]{0:T(256)S(1)}, f32[256]{0:T(256)}, u32[]{:S(2)}) copy-start(f32[256]{0:T(256)} %copy-done.39) | copy-start | bytes 3076
  866.0 24.0 %all-to-all-start.3 = ((bf16[2,48,3072]{2,1,0:T(8,128)(2,1)}), bf16[2,48,3072]{2,1,0:T(8,128)(2,1)}, u32[]{:S(2)}, u32[]{:S(2)}) async-start(bf16[2,48,3072]{2,1,0:T(8,128)(2,1)} %reduce_sum.341), calls=%async_computation.3 | async-start | bytes 1179648 | tf_op jit(solution)/shard_map/all_to_all | solution.py:119
  870.2 7.9 copy-start.42
  878.2 15.5 %copy-start.12 = (bf16[256,1536]{1,0:T(8,128)(2,1)S(1)}, bf16[256,1536]{1,0:T(8,128)(2,1)}, u32[]{:S(2)}) copy-start(bf16[256,1536]{1,0:T(8,128)(2,1)} %param.14) | copy-start | bytes 2359300
  878.2 15.5 %copy-start.15 = (bf16[256,1536]{1,0:T(8,128)(2,1)S(1)}, bf16[256,1536]{1,0:T(8,128)(2,1)}, u32[]{:S(2)}) copy-start(bf16[256,1536]{1,0:T(8,128)(2,1)} %param.12) | copy-start | bytes 2359300
  878.2 15.4 %copy-start.47 = (bf16[256]{0:T(256)(128)(2,1)S(1)}, bf16[256]{0:T(256)(128)(2,1)}, u32[]{:S(2)}) copy-start(bf16[256]{0:T(256)(128)(2,1)} %fusion.94) | copy-start | bytes 1540
  890.0 19.5 %all-to-all-start.1 = ((bf16[2,48,6448]{2,1,0:T(8,128)(2,1)}), bf16[2,48,6448]{2,1,0:T(8,128)(2,1)S(1)}, u32[]{:S(2)}, u32[]{:S(2)}) async-start(bf16[2,48,6448]{2,1,0:T(8,128)(2,1)} %reduce_sum.321), calls=%async_computation.1 | async-start | bytes 2506752 | tf_op jit(solution)/shard_map/all_to_all | solution.py:116
  (1 other events, 0.5 us)
Sparse Core Ops, SparseCore 0:
  10.9 130.1 all-gather.2
  144.0 130.8 all-gather.4
  445.5 499.7 all-reduce.16
where the time goes:
time: 969 us; the launch traced here: 961 us
  waiting for transfers between devices  656 us (68%)
  matrix products  127 us (13%)
  local copies, waits for them, and re-layouts  72.1 us (7%)
  other arithmetic  66.9 us (7%)
  starting transfers between devices  22.9 us (2%)
  between operations  15.9 us (2%)
    all_to_all x1, waiting for transfers between devices, spread_gradients(): lax.all_to_all(shaped_in.astype(jnp.bfloat16), 'fsdp', split_axis=1, conc...  414 us
    all_gather x1, waiting for transfers between devices, fetch(): lax.all_gather(in_weight, ('dp', 'fsdp'), axis=0, tiled=True)  127 us
    all_gather x1, waiting for transfers between devices, fetch(): lax.all_gather(out_weight, ('dp', 'fsdp'), axis=0, tiled=True)  67.3 us
    dot_general x3, matrix products, step(): within = jnp.einsum('tsh,shp->thp', mixing, x_block, precision=PRECISE)  44.1 us
    convert_element_type x2, local copies, waits for them, and re-layouts, spread_gradients(): shaped_in.astype(jnp.bfloat16)  41.8 us
    psum x1, waiting for transfers between devices, body(): lax.psum((grad_pre_gain, grad_conv_weight, grad_conv_bias, grad_dt_bias,...  34.5 us
  transfers between devices with their start and end apart: 7, of which 6 were waited for; matrix products, arithmetic and copies ran while one was open for 26% of the time, Pallas kernels for 0%

commit v1 on v0

v1 whole, which is shorter than its diff:
```python
import functools

import jax
import jax.numpy as jnp
from jax import lax
from jax.experimental import pallas as pl
from jax.experimental.pallas import tpu as pltpu
from jax.sharding import Mesh
from jax.sharding import PartitionSpec as P

EPSILON = 1e-05
PRECISE = lax.Precision.HIGHEST
LANES = 128
LOW = jnp.bfloat16

PLANE = ("xi", "yi", "c")
LINE = ("xo", "zo")
EVERY = ("xo", "xi", "zo", "yi", "c")


def swap(value):
    return lax.ppermute(value, "c", [(0, 1), (1, 0)])


def cross(value, axes, distance, count):
    return lax.ppermute(value, axes, [(i, i ^ distance) for i in range(count)])


def shift_down(value, rows):
    if rows == 0:
        return value
    index = lax.broadcasted_iota(jnp.int32, value.shape, 0)
    return jnp.where(index >= rows, pltpu.roll(value, rows, 0), 0.0)


def shift_up(value, rows):
    if rows == 0:
        return value
    length = value.shape[0]
    index = lax.broadcasted_iota(jnp.int32, value.shape, 0)
    return jnp.where(index < length - rows, pltpu.roll(value, length - rows, 0), 0.0)


def softplus(value):
    return jnp.maximum(value, 0.0) + jnp.log1p(jnp.exp(-jnp.abs(value)))


def dot_f32(left, right):
    return jnp.dot(left, right, precision=PRECISE, preferred_element_type=jnp.float32)


def dot_low(left, right):
    return jnp.dot(left, right, preferred_element_type=jnp.float32)


def dot_nt(left, right):
    return lax.dot_general(left, right, (((1,), (1,)), ((), ())), preferred_element_type=jnp.float32)


def convolve(conv_input, taps, bias):
    kernel_taps = taps.shape[0]
    summed = bias
    for tap in range(kernel_taps):
        summed = summed + taps[tap : tap + 1] * shift_down(conv_input, kernel_taps - 1 - tap)
    return summed


def triangle(length, lower):
    row = lax.broadcasted_iota(jnp.int32, (length, length), 0)
    column = lax.broadcasted_iota(jnp.int32, (length, length), 1)
    return row >= column if lower else row <= column


def head_lanes(step, head_count, inner):
    head = lax.broadcasted_iota(jnp.int32, (LANES, inner), 0)
    lane = lax.broadcasted_iota(jnp.int32, (LANES, inner), 1)
    spread = (lane // (inner // head_count) == head).astype(jnp.float32)
    return dot_f32(step, spread)


def lanes_sum(value, head_count):
    inner = value.shape[1]
    lane = lax.broadcasted_iota(jnp.int32, (inner, LANES), 0)
    head = lax.broadcasted_iota(jnp.int32, (inner, LANES), 1)
    return dot_f32(value, (lane // (inner // head_count) == head).astype(jnp.float32))


def scan_forward(heads, part_ref, taps_ref, bias_ref, dt_ref, alog_ref, skip_ref, out_ref):
    inner = out_ref.shape[1]
    length = out_ref.shape[0]
    width = taps_ref.shape[1]
    states = (width - inner) // 2
    conv_low = jax.nn.silu(convolve(part_ref[:, :width], taps_ref[...], bias_ref[...])).astype(LOW)
    step = softplus(part_ref[:, width:] + dt_ref[...])
    lower = triangle(length, True)
    cumulative = dot_f32(lower.astype(jnp.float32), step * -jnp.exp(alog_ref[...]))
    across = cumulative.T
    scores = dot_nt(conv_low[:, inner + states :], conv_low[:, inner : inner + states])
    scores = jnp.where(lower, scores, 0.0)
    values = conv_low[:, :inner].astype(jnp.float32)
    scaled = (values * head_lanes(step, heads, inner)).astype(LOW)
    first = lax.broadcasted_iota(jnp.int32, (length, LANES), 1) < inner // heads
    for pair in range(heads // 2):
        lanes = slice(pair * LANES, (pair + 1) * LANES)
        sums = []
        for head in (2 * pair, 2 * pair + 1):
            spread = cumulative[:, head : head + 1] - across[head : head + 1, :]
            mixing = scores * jnp.exp(jnp.where(lower, spread, 0.0))
            sums.append(dot_low(mixing.astype(LOW), scaled[:, lanes]))
        out_ref[:, lanes] = jnp.where(first, sums[0], sums[1]) + skip_ref[:, lanes] * values[:, lanes]


def scan_backward(
    heads,
    part_ref,
    grad_ref,
    scanned_ref,
    taps_ref,
    bias_ref,
    dt_ref,
    alog_ref,
    skip_ref,
    out_ref,
    small_ref,
):
    inner = grad_ref.shape[1]
    length = grad_ref.shape[0]
    width = taps_ref.shape[1]
    states = (width - inner) // 2
    kernel_taps = taps_ref.shape[0]
    conv_input = part_ref[:, :width]
    summed = convolve(conv_input, taps_ref[...], bias_ref[...])
    gate = jax.nn.sigmoid(summed)
    conv_low = (summed * gate).astype(LOW)
    slope = gate * (1.0 + summed * (1.0 - gate))
    raw = part_ref[:, width:] + dt_ref[...]
    step = softplus(raw)
    decay = -jnp.exp(alog_ref[...])
    lower = triangle(length, True)
    cumulative = dot_f32(lower.astype(jnp.float32), step * decay)
    across = cumulative.T
    b_rows = conv_low[:, inner : inner + states]
    c_rows = conv_low[:, inner + states :]
    scores = jnp.where(lower, dot_nt(c_rows, b_rows), 0.0)
    values = conv_low[:, :inner].astype(jnp.float32)
    steps = head_lanes(step, heads, inner)
    scaled = (values * steps).astype(LOW)
    grad = grad_ref[...]
    grad_low = grad.astype(LOW)
    grad_across = grad.T.astype(LOW)
    half = inner // heads
    first = lax.broadcasted_iota(jnp.int32, (length, LANES), 1) < half
    upper_rows = lax.broadcasted_iota(jnp.int32, (LANES, length), 0) < half
    grad_scores = jnp.zeros((length, length), jnp.float32)
    moved = []
    for pair in range(heads // 2):
        lanes = slice(pair * LANES, (pair + 1) * LANES)
        sums = []
        for head in (2 * pair, 2 * pair + 1):
            spread = cumulative[:, head : head + 1] - across[head : head + 1, :]
            decays = jnp.where(lower, jnp.exp(jnp.where(lower, spread, 0.0)), 0.0)
            mixing = (scores * decays).astype(LOW)
            own = first if head % 2 == 0 else jnp.logical_not(first)
            grad_own = jnp.where(own, grad[:, lanes], 0.0).astype(LOW)
            grad_scores = grad_scores + dot_nt(grad_own, scaled[:, lanes]) * decays
            sums.append(dot_low(grad_across[lanes], mixing))
        moved.append(jnp.where(upper_rows, sums[0], sums[1]).T)
    grad_scaled = jnp.concatenate(moved, axis=1)
    within = scanned_ref[...] - skip_ref[...] * values
    grad_cumulative = lanes_sum(
        grad_low.astype(jnp.float32) * within - scaled.astype(jnp.float32) * grad_scaled, heads
    )
    grad_rate = dot_f32(triangle(length, False).astype(jnp.float32), grad_cumulative)
    grad_step = grad_rate * decay + lanes_sum(values * grad_scaled, heads)
    grad_raw = grad_step * jax.nn.sigmoid(raw)
    grad_values = steps * grad_scaled + skip_ref[...] * grad
    scores_low = grad_scores.astype(LOW)
    grad_c = dot_low(scores_low, b_rows)
    grad_b = dot_low(c_rows.T, scores_low).T
    grad_summed = jnp.concatenate([grad_values, grad_b, grad_c], axis=1) * slope
    grad_input = jnp.zeros_like(grad_summed)
    rows = []
    for tap in range(kernel_taps):
        away = kernel_taps - 1 - tap
        grad_input = grad_input + taps_ref[tap : tap + 1, :] * shift_up(grad_summed, away)
        rows.append(jnp.sum(grad_summed * shift_down(conv_input, away), axis=0, keepdims=True))
    rows.append(jnp.sum(grad_summed, axis=0, keepdims=True))
    out_ref[:, :width] = grad_input.astype(LOW)
    out_ref[:, width:] = grad_raw.astype(LOW)

    @pl.when(pl.program_id(0) == 0)
    def _():
        small_ref[...] = jnp.zeros_like(small_ref)

    for index, row in enumerate(rows):
        small_ref[index : index + 1, :width] += row
    small_ref[5:6, :inner] += jnp.sum(grad * values, axis=0, keepdims=True)
    small_ref[5:6, width:] += jnp.sum(grad_raw, axis=0, keepdims=True)
    small_ref[6:7, width:] += jnp.sum(grad_rate * step, axis=0, keepdims=True) * decay


def row_block(length, width):
    return pl.BlockSpec((length, width), lambda slot: (slot, 0))


def whole_block(array):
    return pl.BlockSpec(array.shape, lambda slot: (0,) * array.ndim)


def run_forward(slots, heads, part, taps, bias, dt_row, alog_row, skip_row):
    length = part.shape[0] // slots
    inner = skip_row.shape[1]
    weights = (taps, bias, dt_row, alog_row, skip_row)
    return pl.pallas_call(
        functools.partial(scan_forward, heads),
        grid=(slots,),
        in_specs=[row_block(length, part.shape[1])] + [whole_block(w) for w in weights],
        out_specs=row_block(length, inner),
        out_shape=jax.ShapeDtypeStruct((part.shape[0], inner), jnp.float32),
        compiler_params=pltpu.CompilerParams(vmem_limit_bytes=32 << 20),
    )(part, *weights)


def run_backward(slots, heads, part, grad, scanned, taps, bias, dt_row, alog_row, skip_row):
    length = part.shape[0] // slots
    weights = (taps, bias, dt_row, alog_row, skip_row)
    return pl.pallas_call(
        functools.partial(scan_backward, heads),
        grid=(slots,),
        in_specs=[
            row_block(length, part.shape[1]),
            row_block(length, grad.shape[1]),
            row_block(length, grad.shape[1]),
        ]
        + [whole_block(w) for w in weights],
        out_specs=[
            row_block(length, part.shape[1]),
            pl.BlockSpec((8, part.shape[1]), lambda slot: (0, 0)),
        ],
        out_shape=[
            jax.ShapeDtypeStruct(part.shape, LOW),
            jax.ShapeDtypeStruct((8, part.shape[1]), jnp.float32),
        ],
        compiler_params=pltpu.CompilerParams(vmem_limit_bytes=32 << 20),
    )(part, grad, scanned, *weights)


def body(
    sizes,
    hidden_in,
    lengths,
    cotangent,
    pre_gain,
    in_weight,
    conv_weight,
    conv_bias,
    dt_bias,
    a_log,
    skip,
    inner_gain,
    out_weight,
):
    length, model = hidden_in.shape
    rows = in_weight.shape[0]
    inner_all = out_weight.shape[1]
    heads_all = dt_bias.shape[0]
    states = (conv_weight.shape[1] - inner_all) // 2
    ranks = sizes["xi"] * sizes["yi"] * sizes["c"]
    lines = sizes["xo"] * sizes["zo"]
    inner = inner_all // ranks
    heads = heads_all // ranks
    head_width = inner // heads
    core = lax.axis_index("c")
    rank = (lax.axis_index("xi") * sizes["yi"] + lax.axis_index("yi")) * sizes["c"] + core
    place = lax.axis_index("xo") * sizes["zo"] + lax.axis_index("zo")
    by_plane = (sizes["xo"], sizes["xi"], sizes["zo"], sizes["yi"] * sizes["c"] * rows)
    from_plane = (sizes["xo"], sizes["zo"], sizes["xi"], sizes["yi"] * sizes["c"] * rows)

    def to_lines(value):
        return value.reshape(-1, *by_plane).transpose(0, 1, 3, 2, 4).reshape(-1, model)

    def from_lines(value):
        return value.reshape(-1, *from_plane).transpose(0, 1, 3, 2, 4).reshape(-1, model)

    def gather_rows(piece):
        if lines != 4:
            return lax.all_gather(piece, LINE, axis=0, tiled=True)
        pieces = [piece] + [cross(piece, LINE, away, lines) for away in range(1, lines)]
        whole = jnp.zeros((lines * piece.shape[0], piece.shape[1]), piece.dtype)
        for away, part in enumerate(pieces):
            whole = lax.dynamic_update_slice(whole, part, ((place ^ away) * piece.shape[0], 0))
        return whole

    def scatter_rows(whole):
        count = whole.shape[0] // lines
        if lines != 4:
            moved = lax.all_to_all(whole.astype(LOW), LINE, split_axis=0, concat_axis=0, tiled=True)
            return jnp.sum(moved.reshape(lines, count, -1).astype(jnp.float32), axis=0)

        def part(away):
            return lax.dynamic_slice(whole, ((place ^ away) * count, 0), (count, whole.shape[1]))

        total = part(0).astype(jnp.float32)
        for away in (2, 3, 1):
            total = total + cross(part(away).astype(LOW), LINE, away, lines).astype(jnp.float32)
        return total

    def exchange(value):
        return lax.all_to_all(value, PLANE, split_axis=0, concat_axis=0, tiled=True)

    def gather_tokens(value):
        near = [value] + [cross(value, ("xi", "yi"), away, 4) for away in range(1, 4)]
        return jnp.concatenate(near + [swap(block) for block in near], axis=0)

    def scatter_tokens(value):
        half = value.shape[0] // 2
        total = value[:half].astype(jnp.float32) + swap(value[half:].astype(LOW)).astype(jnp.float32)
        total = total.reshape(4, length, -1)
        own = total[0]
        for away in range(1, 4):
            own = own + cross(total[away].astype(LOW), ("xi", "yi"), away, 4).astype(jnp.float32)
        return own

    def by_rank(columns):
        return columns.reshape(rows, ranks, -1).transpose(1, 0, 2)

    first_conv = inner_all
    first_state = 2 * inner_all
    first_step = first_state + 2 * states
    state_columns = in_weight[:, first_state:first_step].reshape(rows, 2, states).transpose(1, 0, 2)
    packed_conv = jnp.concatenate(
        [
            by_rank(in_weight[:, first_conv:first_state]),
            jnp.tile(state_columns, (ranks // 2, 1, 1)),
            jnp.pad(by_rank(in_weight[:, first_step:]), ((0, 0), (0, 0), (0, LANES - heads))),
        ],
        axis=2,
    )
    packed_gate = by_rank(in_weight[:, :inner_all])
    packed_out = by_rank(out_weight)
    plane_rows = ranks * rows
    conv_columns = gather_rows(exchange(packed_conv).reshape(plane_rows, -1))
    gate_columns = gather_rows(exchange(packed_gate).reshape(plane_rows, -1))
    out_columns = gather_rows(exchange(packed_out).reshape(plane_rows, -1))
    own_states = conv_columns[:, inner : inner + states]
    other_states = swap(own_states)
    conv_columns = jnp.concatenate(
        [
            conv_columns[:, :inner],
            jnp.where(core == 0, own_states, other_states),
            jnp.where(core == 0, other_states, own_states),
            conv_columns[:, inner + states :],
        ],
        axis=1,
    )

    stream = hidden_in.astype(jnp.float32)
    scale = lax.rsqrt(jnp.mean(stream * stream, axis=-1, keepdims=True) + EPSILON)
    valid = (jnp.arange(length) < lengths[0])[:, None]
    own_upstream = jnp.where(valid, cotangent, jnp.zeros_like(cotangent))
    normed = gather_tokens(to_lines((stream * scale * pre_gain).astype(LOW)))
    upstream = gather_tokens(to_lines(own_upstream))
    slots = normed.shape[0] // length

    def of_rank(value, count):
        return lax.dynamic_slice_in_dim(value, rank * count, count, axis=-1)

    taps = jnp.concatenate(
        [of_rank(conv_weight[:, :inner_all], inner), conv_weight[:, inner_all:]], axis=1
    )
    bias = jnp.concatenate([of_rank(conv_bias[:inner_all], inner), conv_bias[inner_all:]])[None]
    dt_row = jnp.pad(of_rank(dt_bias, heads), (0, LANES - heads))[None]
    alog_row = jnp.pad(of_rank(a_log, heads), (0, LANES - heads))[None]
    skip_row = jnp.repeat(of_rank(skip, heads), head_width)[None]
    gain_row = of_rank(inner_gain, inner)[None]

    conv_part = dot_low(normed, conv_columns)
    scanned = run_forward(slots, heads, conv_part, taps, bias, dt_row, alog_row, skip_row)
    gate_part = dot_low(normed, gate_columns)
    gate_sigmoid = jax.nn.sigmoid(gate_part)
    gate_silu = gate_part * gate_sigmoid
    gated = scanned * gate_silu
    gained_low = (gated * gain_row).astype(LOW)
    branch = dot_nt(gained_low, out_columns)
    grad_mixed = dot_low(upstream, out_columns)
    grad_gained = grad_mixed * gain_row
    stats = jnp.stack([jnp.sum(gated * gated, axis=1), jnp.sum(grad_gained * gated, axis=1)])
    stats = stats.reshape(2, 2, 4, length)
    stats = stats + swap(stats[:, ::-1])
    stats = stats.reshape(2, 2, 2, 2, length)
    far = [
        cross(jnp.flip(stats, axes), ("xi", "yi"), away, 4)
        for axes, away in (((2, 3), 3), ((3,), 1), ((2,), 2))
    ]
    stats = ((stats + far[0]) + (far[1] + far[2])).reshape(2, -1)
    inner_scale = lax.rsqrt(stats[0] / inner_all + EPSILON)[:, None]
    slope = inner_scale**3 * stats[1][:, None] / inner_all
    branch_own = scatter_tokens(branch.astype(LOW))
    branch_own = from_lines(branch_own * inner_scale[:length])
    output = jnp.where(valid, stream + branch_own, 0.0).astype(LOW)

    mixed_low = (gated * inner_scale * gain_row).astype(LOW)
    grad_out_columns = lax.dot_general(
        upstream, mixed_low, (((0,), (0,)), ((), ())), preferred_element_type=jnp.float32
    )
    grad_inner_gain = jnp.sum(grad_mixed * gated * inner_scale, axis=0)
    grad_gated = grad_gained * inner_scale - gated * slope
    grad_gate = (grad_gated * scanned * (gate_sigmoid * (1.0 + gate_part * (1.0 - gate_sigmoid)))).astype(LOW)
    grad_scanned = grad_gated * gate_silu
    grad_gate_columns = lax.dot_general(
        normed, grad_gate, (((0,), (0,)), ((), ())), preferred_element_type=jnp.float32
    )
    grad_conv, small = run_backward(
        slots, heads, conv_part, grad_scanned, scanned, taps, bias, dt_row, alog_row, skip_row
    )
    grad_conv_columns = lax.dot_general(
        normed, grad_conv, (((0,), (0,)), ((), ())), preferred_element_type=jnp.float32
    )
    grad_normed = dot_nt(grad_gate, gate_columns) + dot_nt(grad_conv, conv_columns)
    gain_lines = to_lines(pre_gain[None])
    grad_pre_gain = jnp.sum(grad_normed * normed.astype(jnp.float32), axis=0, keepdims=True) / gain_lines
    grad_pre_gain = from_lines(grad_pre_gain)[0]
    grad_own = from_lines(scatter_tokens(grad_normed.astype(LOW))) * pre_gain
    along = jnp.mean(grad_own * stream, axis=-1, keepdims=True)
    grad_stream = grad_own * scale - stream * (scale**3 * along)
    grad_hidden = (own_upstream.astype(jnp.float32) + grad_stream).astype(LOW)

    def to_owners(value):
        return exchange(value.astype(LOW).reshape(ranks, rows, -1)).astype(jnp.float32)

    grad_b = grad_conv_columns[:, inner : inner + states]
    grad_c = grad_conv_columns[:, inner + states : inner + 2 * states]
    kept = jnp.where(core == 0, grad_b, grad_c)
    given = jnp.where(core == 0, grad_c, grad_b)
    kept = kept + swap(given.astype(LOW)).astype(jnp.float32)
    conv_back = jnp.concatenate(
        [grad_conv_columns[:, :inner], kept, grad_conv_columns[:, inner + 2 * states :]], axis=1
    )
    owned_out = to_owners(scatter_rows(grad_out_columns)).transpose(1, 0, 2).reshape(rows, inner_all)
    owned_gate = to_owners(scatter_rows(grad_gate_columns)).transpose(1, 0, 2).reshape(rows, inner_all)
    owned_conv = to_owners(scatter_rows(conv_back))
    owned_states = jnp.sum(
        owned_conv[:, :, inner : inner + states].reshape(ranks // 2, 2, rows, states), axis=0
    )
    owned_in = jnp.concatenate(
        [
            owned_gate,
            owned_conv[:, :, :inner].transpose(1, 0, 2).reshape(rows, inner_all),
            owned_states.transpose(1, 0, 2).reshape(rows, 2 * states),
            owned_conv[:, :, inner + states : inner + states + heads].transpose(1, 0, 2).reshape(rows, heads_all),
        ],
        axis=1,
    )

    def place_rank(value, total):
        blank = jnp.zeros(value.shape[:-1] + (total,), jnp.float32)
        return lax.dynamic_update_slice_in_dim(blank, value, rank * value.shape[-1], axis=-1)

    taps_count = conv_weight.shape[0]
    width = taps.shape[1]
    conv_small = small[: taps_count + 1, :width]
    conv_small = jnp.concatenate(
        [place_rank(conv_small[:, :inner], inner_all), conv_small[:, inner:]], axis=1
    )
    head_small = jnp.stack(
        [
            small[5, width : width + heads],
            small[6, width : width + heads],
            jnp.sum(small[5, :inner].reshape(heads, head_width), axis=1),
        ]
    )
    head_small = jnp.pad(place_rank(head_small, heads_all), ((0, 0), (0, LANES - heads_all)))
    pieces = (grad_pre_gain, conv_small, place_rank(grad_inner_gain, inner_all), head_small)
    flat = jnp.concatenate([piece.reshape(-1, LANES) for piece in pieces], axis=0)
    flat = flat + swap(flat)
    far = [cross(flat, ("xi", "yi"), away, 4) for away in (3, 1, 2)]
    flat = (flat + far[0]) + (far[1] + far[2])
    if lines == 4:
        far = [cross(flat, LINE, away, 4) for away in (3, 1, 2)]
        flat = (flat + far[0]) + (far[1] + far[2])
    else:
        flat = lax.psum(flat, LINE)
    sums = []
    start = 0
    for piece in pieces:
        count = piece.size // LANES
        sums.append(flat[start : start + count].reshape(piece.shape))
        start += count
    return (
        output,
        grad_hidden,
        sums[0],
        owned_in,
        sums[1][:taps_count],
        sums[1][taps_count],
        sums[3][0, :heads_all],
        sums[3][1, :heads_all],
        sums[3][2, :heads_all],
        sums[2],
        owned_out,
    )


def solution(mesh):
    dp, fsdp = mesh.shape["dp"], mesh.shape["fsdp"]
    shape = (dp // 2, 2, fsdp // 4, 2, 2)
    fine = Mesh(mesh.devices.reshape(shape), EVERY)
    split, kept = P(EVERY, None), P()
    in_specs = (split, P(EVERY), split, kept, split, kept, kept, kept, kept, kept, kept, split)
    out_specs = (split, split, kept, split, kept, kept, kept, kept, kept, kept, split)
    return jax.shard_map(
        functools.partial(body, dict(zip(EVERY, shape))),
        mesh=fine,
        in_specs=in_specs,
        out_specs=out_specs,
        check_vma=False,
    )
```

time: 969 us -> 507 us (0.52)
  waiting for transfers between devices: 656 us -> 238 us
  matrix products: 127 us -> 62.3 us
  starting transfers between devices: 22.9 us -> 77.7 us
  Pallas kernels: 0 us -> 40.2 us
  other arithmetic: 66.9 us -> 29 us
  local copies, waits for them, and re-layouts: 72.1 us -> 50.6 us
  between operations: 15.9 us -> 3.15 us
    all_to_all x4 -> x6, waiting for transfers between devices: 426 us -> 27 us  [exchange(): return lax.all_to_all(value, PLANE, split_axis=0, concat_axis=0, tiled=True)]
    ppermute x0 -> x53, waiting for transfers between devices: none -> 211 us  [the longest x39 209 us: cross(): return lax.ppermute(value, axes, [(i, i ^ distance) for i in range(count)])]
    all_gather x2 -> x0, waiting for transfers between devices: 194 us -> none  [the longest x1 127 us: fetch(): lax.all_gather(in_weight, ('dp', 'fsdp'), axis=0, tiled=True)]
    dot_general x17 -> x8, matrix products: 120 us -> 54.4 us  [the longest x3 25.1 us: dot_nt(): lax.dot_general(left, right, (((1,), (1,)), ((), ())), preferred_element_...]
    ppermute x0 -> x53, starting transfers between devices: none -> 54.4 us  [the longest x39 51.3 us: cross(): return lax.ppermute(value, axes, [(i, i ^ distance) for i in range(count)])]
    convert_element_type x3 -> x4, local copies, waits for them, and re-layouts: 51.4 us -> 4.53 us  [the longest x3 3.53 us: scatter_rows(): part(away).astype(LOW)]
    pallas_call x0 -> x2, Pallas kernels: none -> 40.2 us  [the longest x1 28.5 us: run_backward(): pl.pallas_call(functools.partial(scan_backward, heads), grid=(slots,), in...]
    psum x1 -> x0, waiting for transfers between devices: 34.5 us -> none  [body(): lax.psum((grad_pre_gain, grad_conv_weight, grad_conv_bias, grad_dt_bias,...]
  transfers between devices with their start and end apart: 7 -> 59, of which waited for: 6 -> 26; matrix products, arithmetic and copies ran while one was open for 26% -> 24% of each run, Pallas kernels for 0% -> 8%
where the time goes in v1:
time: 507 us; the launch traced here: 501 us
  waiting for transfers between devices  238 us (47%)
  starting transfers between devices  77.7 us (15%)
  matrix products  62.3 us (12%)
  local copies, waits for them, and re-layouts  50.6 us (10%)
  Pallas kernels  40.2 us (8%)
  other arithmetic  29 us (6%)
    ppermute x39, waiting for transfers between devices, cross(): return lax.ppermute(value, axes, [(i, i ^ distance) for i in range(count)])  209 us
    ppermute x39, starting transfers between devices, cross(): return lax.ppermute(value, axes, [(i, i ^ distance) for i in range(count)])  51.3 us
    pallas_call x1, Pallas kernels, run_backward(): pl.pallas_call(functools.partial(scan_backward, heads), grid=(slots,), in...  28.5 us
    all_to_all x6, waiting for transfers between devices, exchange(): return lax.all_to_all(value, PLANE, split_axis=0, concat_axis=0, tiled=True)  27 us
    dot_general x3, matrix products, dot_nt(): lax.dot_general(left, right, (((1,), (1,)), ((), ())), preferred_element_...  25.1 us
    all_to_all x6, starting transfers between devices, exchange(): return lax.all_to_all(value, PLANE, split_axis=0, concat_axis=0, tiled=True)  23.3 us
    dot_general x3, matrix products, dot_low(): return jnp.dot(left, right, preferred_element_type=jnp.float32)  17.1 us
    unnamed x139, local copies, waits for them, and re-layouts  15.5 us
  transfers between devices with their start and end apart: 59, of which 26 were waited for; matrix products, arithmetic and copies ran while one was open for 24% of the time, Pallas kernels for 8%

profile of v1, /device:TPU:16, one launch (start us, length us, event | category | flops | bytes accessed | tf_op | source)
XLA Modules:
  0.0 500.5 jit_solution(11537308843082552047)
XLA Ops:
  3.7 1.6 collective-permute-start
  7.7 4.1 all-to-all-start.1
  15.1 12.4 %all-to-all-done.1 = bf16[8,48,384]{2,1,0:T(8,128)(2,1)} async-done(((bf16[8,48,384]{2,1,0:T(8,128)(2,1)}), bf16[8,48,384]{2,1,0:T(8,128)(2,1)}, u32[]{:S(2)}, u32[]{:S(2)}) %all-to-all-start.1) | async-done | bytes 294944 | tf_op jit(solution)/shard_map/all_to_all | solution.py:309
  27.5 4.1 all-to-all-start.2
  34.6 3.4 all-to-all-done.2
  38.0 3.8 all-to-all-start
  42.7 1.6 collective-permute-start.11
  47.4 1.7 constant_dynamic-update-slice_fusion.21
  52.5 4.6 collective-permute-done.11
  57.0 2.3 collective-permute-start.15
  60.4 7.7 %collective-permute-done.14 = bf16[384,384]{1,0:T(8,128)(2,1)} collective-permute-done((bf16[384,384]{1,0:T(8,128)(2,1)}, bf16[384,384]{1,0:T(8,128)(2,1)}, u32[]{:S(2)}, u32[]{:S(2)}) %collective-permute-start.14) | collective-permute-done | bytes 294944 | tf_op jit(solution)/shard_map/ppermute | solution.py:26
  68.6 1.7 constant_dynamic-update-slice_fusion.20
  72.9 12.6 %collective-permute-done.15 = bf16[384,384]{1,0:T(8,128)(2,1)S(1)} collective-permute-done((bf16[384,384]{1,0:T(8,128)(2,1)}, bf16[384,384]{1,0:T(8,128)(2,1)S(1)}, u32[]{:S(2)}, u32[]{:S(2)}) %collective-permute-start.15) | collective-permute-done | bytes 294944 | tf_op jit(solution)/shard_map/ppermute | solution.py:26
  85.5 1.8 collective-permute-start.2
  88.0 6.4 %collective-permute-done.13 = bf16[384,384]{1,0:T(8,128)(2,1)S(1)} collective-permute-done((bf16[384,384]{1,0:T(8,128)(2,1)}, bf16[384,384]{1,0:T(8,128)(2,1)S(1)}, u32[]{:S(2)}, u32[]{:S(2)}) %collective-permute-start.13) | collective-permute-done | bytes 294944 | tf_op jit(solution)/shard_map/ppermute | solution.py:26
  94.5 4.5 collective-permute-done.16
  106.4 1.7 collective-permute-start.7
  108.2 9.6 %collective-permute-done.21 = bf16[256,1536]{0,1:T(8,128)(2,1)S(1)} collective-permute-done((bf16[256,1536]{0,1:T(8,128)(2,1)S(1)}, bf16[256,1536]{0,1:T(8,128)(2,1)S(1)}, u32[]{:S(2)}, u32[]{:S(2)}) %collective-permute-start.21) | collective-permute-done | bytes 786464 | tf_op jit(solution)/shard_map/ppermute | solution.py:26
  117.8 5.7 %collective-permute-start.8 = (bf16[384,640]{0,1:T(8,128)(2,1)S(1)}, bf16[384,640]{0,1:T(8,128)(2,1)S(1)}, u32[]{:S(2)}, u32[]{:S(2)}) collective-permute-start(bf16[384,640]{0,1:T(8,128)(2,1)S(1)} %copy.120), channel_id=1, source_target_pairs={{0,8},{4,12},{8,0},{12,4},{1,9},{5,13},{9,1},{13,5},{2,10},{6,14},... | collective-permute-start | bytes 1474568 | tf_op jit(solution)/shard_map/ppermute | solution.py:26
  123.6 1.9 collective-permute-start.9
  125.7 29.6 %collective-permute-done.8 = bf16[384,640]{0,1:T(8,128)(2,1)S(1)} collective-permute-done((bf16[384,640]{0,1:T(8,128)(2,1)S(1)}, bf16[384,640]{0,1:T(8,128)(2,1)S(1)}, u32[]{:S(2)}, u32[]{:S(2)}) %collective-permute-start.8) | collective-permute-done | bytes 491552 | tf_op jit(solution)/shard_map/ppermute | solution.py:26
  155.4 11.0 %collective-permute-done.9 = bf16[384,640]{0,1:T(8,128)(2,1)S(1)} collective-permute-done((bf16[384,640]{0,1:T(8,128)(2,1)S(1)}, bf16[384,640]{0,1:T(8,128)(2,1)S(1)}, u32[]{:S(2)}, u32[]{:S(2)}) %collective-permute-start.9) | collective-permute-done | bytes 491552 | tf_op jit(solution)/shard_map/ppermute | solution.py:26
  167.6 1.7 collective-permute-done.10
  170.6 5.5 %fusion.24.part_ref = f32[2048,768]{1,0:T(8,128)S(1)} fusion(bf16[2048,1536]{0,1:T(8,128)(2,1)S(1)} %constant_dynamic-update-slice_fusion, bf16[1536,128]{0,1:T(8,128)(2,1)S(1)} %get-tuple-element.90, bf16[1536,128]{0,1:T(8,128)(2,1)S(1)} %get-tuple-element.89, bf16[1536,128]{0,1:T(8,128)(2,1)S(1)} %get-tuple-element.88, bf16[1536,384]{0,1:T(8,128)(2,1)S(1)} %slice.210), kind=kOutput, calls=%fused_computation.67 | convolution fusion | flops 4841275392 | bytes 14942208 | tf_op jit(solution)/shard_map/dot_general | solution.py:53
  176.2 11.7 %shard_map.203.scanned_ref = f32[2048,384]{1,0:T(8,128)S(1)} custom-call(f32[2048,768]{1,0:T(8,128)S(1)} %fusion.24.part_ref, f32[4,640]{1,0:T(4,128)S(1)} %pad_maximum_fusion.6.taps_ref, f32[1,640]{1,0:T(1,128)S(1)} %broadcast_in_dim.55.bias_ref, f32[1,128]{1,0:T(1,128)S(1)} %get-tuple-element.103.dt_ref, f32[1,128]{1,0:T(1,128)S(1)} %get-tuple-element.102.alog_ref, ...), custom_call_target="tpu_custom_call" | custom-call | tf_op jit(solution)/shard_map/pallas_call | solution.py:214
  187.9 3.5 fusion.40
  191.6 8.1 %multiply_reduce_fusion.2 = (f32[2048]{0:T(1024)S(1)}, f32[2048]{0:T(1024)S(1)}, f32[2048,384]{1,0:T(8,128)}, f32[2048,384]{1,0:T(8,128)}) fusion(f32[384]{0:T(512)S(1)} %dynamic_slice.59, f32[2048,384]{1,0:T(8,128)S(1)} %shard_map.203.scanned_ref, f32[2048,384]{1,0:T(8,128)S(1)} %fusion.40, bf16[2048,1536]{0,1:T(8,128)(2,1)S(1)} %constant_dynamic-update-slice_fusion.8, ...), kind=kOutput, calls=%fused_computation.10 | convolution fusion | flops 2423779328 | bytes 20071936 | tf_op jit(solution)/shard_map/dot_general | solution.py:53
  201.4 3.0 collective-permute-start.29
  205.0 5.7 %convolution_convert_fusion = bf16[2048,1536]{0,1:T(8,128)(2,1)S(1)} fusion(bf16[1536,384]{1,0:T(8,128)(2,1)} %constant_dynamic-update-slice_fusion.18, f32[2048,384]{1,0:T(8,128)} %get-tuple-element.61, f32[384]{0:T(512)S(1)} %dynamic_slice.59), kind=kOutput, calls=%fused_computation.2 | convolution fusion | flops 2420637696 | bytes 10618368 | tf_op jit(solution)/shard_map/dot_general | solution.py:57
  210.7 2.0 slice.214
  212.7 2.2 copy-done.9
  215.0 7.9 %fusion.10 = f32[1536,384]{1,0:T(8,128)} fusion(bf16[2048,1536]{0,1:T(8,128)(2,1)} %copy-done.38, f32[2048,384]{1,0:T(8,128)S(1)} %copy-done.17, f32[2048]{0:T(1024)S(1)} %bitcast.148, f32[384]{0:T(512)S(1)} %dynamic_slice.59), kind=kOutput, calls=%fused_computation.30 | convolution fusion | flops 2418278400 | bytes 11806208 | tf_op jit(solution)/shard_map/dot_general | solution.py:403
  222.9 3.7 multiply_convert_fusion.1
  226.6 28.5 %shard_map.204 = (bf16[2048,768]{1,0:T(8,128)(2,1)S(1)}, f32[8,768]{1,0:T(8,128)S(1)}) custom-call(f32[2048,768]{1,0:T(8,128)S(1)} %bitcast.111, f32[2048,384]{1,0:T(8,128)S(1)} %get-tuple-element.65.grad_ref, f32[2048,384]{1,0:T(8,128)S(1)} %shard_map.203.scanned_ref, f32[4,640]{1,0:T(4,128)S(1)} %pad_maximum_fusion.6.taps_ref, ...), custom_call_target="tpu_custom_call" | custom-call | tf_op jit(solution)/shard_map/pallas_call | solution.py:227
  255.8 7.2 %fusion.42 = f32[1536,768]{0,1:T(8,128)} fusion(bf16[2048,1536]{0,1:T(8,128)(2,1)S(1)} %bitcast.117, bf16[2048,768]{1,0:T(8,128)(2,1)S(1)} %get-tuple-element.13), kind=kOutput, calls=%fused_computation.144 | convolution fusion | flops 4831838208 | bytes 14155776 | tf_op jit(solution)/shard_map/dot_general | solution.py:416
  263.0 8.2 %fusion.23 = f32[2048,1536]{0,1:T(8,128)} fusion(bf16[2048,768]{1,0:T(8,128)(2,1)S(1)} %get-tuple-element.13, bf16[1536,128]{0,1:T(8,128)(2,1)S(1)} %copy-done.33, bf16[1536,128]{0,1:T(8,128)(2,1)S(1)} %copy-done.31, bf16[1536,128]{0,1:T(8,128)(2,1)S(1)} %copy-done.29, bf16[1536,384]{0,1:T(8,128)(2,1)S(1)} %copy-done.22), kind=kOutput, calls=%fused_computation.66 | convolution fusion | flops 4841275392 | bytes 18087936 | tf_op jit(solution)/shard_map/dot_general | solution.py:57
  271.3 5.0 fusion.41
  277.6 11.3 %multiply_reduce_fusion = (f32[1536]{0:T(1024)}, bf16[2048,1536]{0,1:T(8,128)(2,1)}) fusion(bf16[2048,1536]{0,1:T(8,128)(2,1)} %copy-done.6, f32[2048,1536]{0,1:T(8,128)} %fusion.23, bf16[2048,384]{1,0:T(8,128)(2,1)} %copy-done.10, bf16[1536,384]{1,0:T(8,128)(2,1)S(1)} %copy-done.13), kind=kOutput, calls=%fused_computation | convolution fusion | flops 2431646208 | bytes 27924480 | tf_op jit(solution)/shard_map/dot_general | solution.py:57
  295.9 2.9 collective-permute-start.37
  299.7 2.2 slice.223
  301.9 1.7 collective-permute-done.38
  303.6 1.8 collective-permute-start.40
  307.5 2.2 dynamic-slice_convert_fusion.8
  309.8 17.6 %collective-permute-done.40 = f32[169,128]{1,0:T(8,128)S(1)} collective-permute-done((f32[169,128]{1,0:T(8,128)S(1)}, f32[169,128]{1,0:T(8,128)S(1)}, u32[]{:S(2)}, u32[]{:S(2)}) %collective-permute-start.40) | collective-permute-done | bytes 86560 | tf_op jit(solution)/shard_map/ppermute | solution.py:26
  329.6 3.1 collective-permute-start.43
  334.2 1.9 copy-done.4
  337.9 2.0 collective-permute-start.47
  339.9 12.4 %collective-permute-done.43 = bf16[384,384]{1,0:T(8,128)(2,1)S(1)} collective-permute-done((bf16[384,384]{1,0:T(8,128)(2,1)S(1)}, bf16[384,384]{1,0:T(8,128)(2,1)S(1)}, u32[]{:S(2)}, u32[]{:S(2)}) %collective-permute-start.43) | collective-permute-done | bytes 294944 | tf_op jit(solution)/shard_map/ppermute | solution.py:26
  353.6 27.7 %collective-permute-done.44 = bf16[384,384]{1,0:T(8,128)(2,1)S(1)} collective-permute-done((bf16[384,384]{1,0:T(8,128)(2,1)S(1)}, bf16[384,384]{1,0:T(8,128)(2,1)S(1)}, u32[]{:S(2)}, u32[]{:S(2)}) %collective-permute-start.44) | collective-permute-done | bytes 294944 | tf_op jit(solution)/shard_map/ppermute | solution.py:26
  382.2 3.8 all-to-all-start.5
  387.7 2.1 add_convert_fusion.2
  389.8 2.6 all-to-all-done.5
  392.4 3.4 all-to-all-start.3
  395.9 6.5 %collective-permute-done.48 = bf16[384,640]{0,1:T(8,128)(2,1)} collective-permute-done((bf16[384,640]{0,1:T(8,128)(2,1)}, bf16[384,640]{0,1:T(8,128)(2,1)}, u32[]{:S(2)}, u32[]{:S(2)}) %collective-permute-start.48) | collective-permute-done | bytes 491552 | tf_op jit(solution)/shard_map/ppermute | solution.py:26
  402.3 1.9 add_convert_fusion
  405.2 4.1 all-to-all-start.4
  410.3 7.5 %all-to-all-done.4 = bf16[8,48,640]{2,1,0:T(8,128)(2,1)S(1)} async-done(((bf16[8,48,640]{2,1,0:T(8,128)(2,1)}), bf16[8,48,640]{2,1,0:T(8,128)(2,1)S(1)}, u32[]{:S(2)}, u32[]{:S(2)}) %all-to-all-start.4) | async-done | bytes 491552 | tf_op jit(solution)/shard_map/all_to_all | solution.py:309
  419.1 4.7 fusion.33
  428.3 3.6 fusion.34
  434.2 26.9 %collective-permute-done.18 = bf16[256,1536]{0,1:T(8,128)(2,1)} collective-permute-done((bf16[256,1536]{0,1:T(8,128)(2,1)}, bf16[256,1536]{0,1:T(8,128)(2,1)}, u32[]{:S(2)}, u32[]{:S(2)}) %collective-permute-start.18) | collective-permute-done | bytes 786464 | tf_op jit(solution)/shard_map/ppermute | solution.py:26
  463.8 2.0 fusion.15
  465.9 12.6 %collective-permute-done.33 = bf16[256,1536]{0,1:T(8,128)(2,1)S(1)} collective-permute-done((bf16[256,1536]{0,1:T(8,128)(2,1)S(1)}, bf16[256,1536]{0,1:T(8,128)(2,1)S(1)}, u32[]{:S(2)}, u32[]{:S(2)}) %collective-permute-start.33) | collective-permute-done | bytes 786464 | tf_op jit(solution)/shard_map/ppermute | solution.py:26
  478.5 2.0 collective-permute-done.34
  480.5 15.2 %collective-permute-done.35 = bf16[256,1536]{0,1:T(8,128)(2,1)S(1)} collective-permute-done((bf16[256,1536]{0,1:T(8,128)(2,1)S(1)}, bf16[256,1536]{0,1:T(8,128)(2,1)S(1)}, u32[]{:S(2)}, u32[]{:S(2)}) %collective-permute-start.35) | collective-permute-done | bytes 786464 | tf_op jit(solution)/shard_map/ppermute | solution.py:26
  (350 shorter events, 74.2 us)
Async XLA Ops:
  3.7 97.3 %collective-permute-start = (bf16[256,1536]{0,1:T(8,128)(2,1)S(1)}, bf16[256,1536]{0,1:T(8,128)(2,1)}, u32[]{:S(2)}, u32[]{:S(2)}) collective-permute-start(bf16[256,1536]{0,1:T(8,128)(2,1)S(1)} %bitcast.120), channel_id=1, source_target_pairs={{0,2},{2,0},{16,18},{18,16},{1,3},{3,1},{17,19},{19,17},{4,6},{6,4... | collective-permute-start | bytes 2359304 | tf_op jit(solution)/shard_map/ppermute | solution.py:26
  5.3 98.5 %collective-permute-start.1 = (bf16[256,1536]{0,1:T(8,128)(2,1)S(1)}, bf16[256,1536]{0,1:T(8,128)(2,1)}, u32[]{:S(2)}, u32[]{:S(2)}) collective-permute-start(bf16[256,1536]{0,1:T(8,128)(2,1)S(1)} %bitcast.121), channel_id=1, source_target_pairs={{0,16},{2,18},{16,0},{18,2},{1,17},{3,19},{17,1},{19,3},{4,20},{6,... | collective-permute-start | bytes 2359304 | tf_op jit(solution)/shard_map/ppermute | solution.py:26
  7.7 19.9 %all-to-all-start.1 = ((bf16[8,48,384]{2,1,0:T(8,128)(2,1)}), bf16[8,48,384]{2,1,0:T(8,128)(2,1)}, u32[]{:S(2)}, u32[]{:S(2)}) async-start(bf16[8,48,384]{2,1,0:T(8,128)(2,1)} %copy.124), calls=%async_computation.1 | async-start | bytes 589824 | tf_op jit(solution)/shard_map/all_to_all | solution.py:309
  27.5 10.5 %all-to-all-start.2 = ((bf16[8,48,384]{2,1,0:T(8,128)(2,1)}), bf16[8,48,384]{2,1,0:T(8,128)(2,1)}, u32[]{:S(2)}, u32[]{:S(2)}) async-start(bf16[8,48,384]{2,1,0:T(8,128)(2,1)} %copy.127), calls=%async_computation.2 | async-start | bytes 589824 | tf_op jit(solution)/shard_map/all_to_all | solution.py:309
  38.0 12.2 %all-to-all-start = ((bf16[8,48,640]{2,1,0:T(8,128)(2,1)}), bf16[8,48,640]{2,1,0:T(8,128)(2,1)S(1)}, u32[]{:S(2)}, u32[]{:S(2)}) async-start(bf16[8,48,640]{2,1,0:T(8,128)(2,1)} %copy.119), calls=%async_computation | async-start | bytes 983040 | tf_op jit(solution)/shard_map/all_to_all | solution.py:309
  42.7 14.3 %collective-permute-start.11 = (bf16[384,384]{1,0:T(8,128)(2,1)}, bf16[384,384]{1,0:T(8,128)(2,1)}, u32[]{:S(2)}, u32[]{:S(2)}) collective-permute-start(bf16[384,384]{1,0:T(8,128)(2,1)} %bitcast.12), channel_id=1, source_target_pairs={{0,4},{4,0},{8,12},{12,8},{1,5},{5,1},{9,13},{13,9},{2,6},{6,2},{1... | collective-permute-start | bytes 884744 | tf_op jit(solution)/shard_map/ppermute | solution.py:26
  44.3 26.0 %collective-permute-start.12 = (bf16[384,384]{1,0:T(8,128)(2,1)}, bf16[384,384]{1,0:T(8,128)(2,1)}, u32[]{:S(2)}, u32[]{:S(2)}) collective-permute-start(bf16[384,384]{1,0:T(8,128)(2,1)} %bitcast.12), channel_id=1, source_target_pairs={{0,8},{4,12},{8,0},{12,4},{1,9},{5,13},{9,1},{13,5},{2,10},{6,14},... | collective-permute-start | bytes 884744 | tf_op jit(solution)/shard_map/ppermute | solution.py:26
  44.7 23.5 %collective-permute-start.14 = (bf16[384,384]{1,0:T(8,128)(2,1)}, bf16[384,384]{1,0:T(8,128)(2,1)}, u32[]{:S(2)}, u32[]{:S(2)}) collective-permute-start(bf16[384,384]{1,0:T(8,128)(2,1)} %bitcast.14), channel_id=1, source_target_pairs={{0,4},{4,0},{8,12},{12,8},{1,5},{5,1},{9,13},{13,9},{2,6},{6,2},{1... | collective-permute-start | bytes 884744 | tf_op jit(solution)/shard_map/ppermute | solution.py:26
  52.2 50.2 %copy-start.5 = (bf16[2048,1536]{0,1:T(8,128)(2,1)S(1)}, bf16[2048,1536]{0,1:T(8,128)(2,1)}, u32[]{:S(2)}) copy-start(bf16[2048,1536]{0,1:T(8,128)(2,1)} %constant_dynamic-update-slice_fusion.7) | copy-start | bytes 18874372
  57.0 28.4 %collective-permute-start.15 = (bf16[384,384]{1,0:T(8,128)(2,1)}, bf16[384,384]{1,0:T(8,128)(2,1)S(1)}, u32[]{:S(2)}, u32[]{:S(2)}) collective-permute-start(bf16[384,384]{1,0:T(8,128)(2,1)} %bitcast.14), channel_id=1, source_target_pairs={{0,8},{4,12},{8,0},{12,4},{1,9},{5,13},{9,1},{13,5},{2,10},{6,14},... | collective-permute-start | bytes 884744 | tf_op jit(solution)/shard_map/ppermute | solution.py:26
  68.1 26.3 %collective-permute-start.13 = (bf16[384,384]{1,0:T(8,128)(2,1)}, bf16[384,384]{1,0:T(8,128)(2,1)S(1)}, u32[]{:S(2)}, u32[]{:S(2)}) collective-permute-start(bf16[384,384]{1,0:T(8,128)(2,1)} %bitcast.12), channel_id=1, source_target_pairs={{0,12},{4,8},{8,4},{12,0},{1,13},{5,9},{9,5},{13,1},{2,14},{6,10},... | collective-permute-start | bytes 884744 | tf_op jit(solution)/shard_map/ppermute | solution.py:26
  70.3 28.6 %collective-permute-start.16 = (bf16[384,384]{1,0:T(8,128)(2,1)}, bf16[384,384]{1,0:T(8,128)(2,1)S(1)}, u32[]{:S(2)}, u32[]{:S(2)}) collective-permute-start(bf16[384,384]{1,0:T(8,128)(2,1)} %bitcast.14), channel_id=1, source_target_pairs={{0,12},{4,8},{8,4},{12,0},{1,13},{5,9},{9,5},{13,1},{2,14},{6,10},... | collective-permute-start | bytes 884744 | tf_op jit(solution)/shard_map/ppermute | solution.py:26
  85.5 20.7 %collective-permute-start.2 = (bf16[256,1536]{0,1:T(8,128)(2,1)S(1)}, bf16[256,1536]{0,1:T(8,128)(2,1)S(1)}, u32[]{:S(2)}, u32[]{:S(2)}) collective-permute-start(bf16[256,1536]{0,1:T(8,128)(2,1)S(1)} %bitcast.123), channel_id=1, source_target_pairs={{0,18},{2,16},{16,2},{18,0},{1,19},{3,17},{17,3},{19,1},{4,22},{6,... | collective-permute-start | bytes 2359304 | tf_op jit(solution)/shard_map/ppermute | solution.py:26
  94.4 12.0 %collective-permute-start.3 = (bf16[256,1536]{0,1:T(8,128)(2,1)S(1)}, bf16[256,1536]{0,1:T(8,128)(2,1)S(1)}, u32[]{:S(2)}, u32[]{:S(2)}) collective-permute-start(bf16[256,1536]{0,1:T(8,128)(2,1)S(1)} %bitcast.124), channel_id=1, source_target_pairs={{0,1},{1,0},{2,3},{3,2},{4,5},{5,4},{6,7},{7,6},{8,9},{9,8},{10,11... | collective-permute-start | bytes 2359304 | tf_op jit(solution)/shard_map/ppermute | solution.py:22
  98.9 18.8 %collective-permute-start.21 = (bf16[256,1536]{0,1:T(8,128)(2,1)S(1)}, bf16[256,1536]{0,1:T(8,128)(2,1)S(1)}, u32[]{:S(2)}, u32[]{:S(2)}) collective-permute-start(bf16[256,1536]{0,1:T(8,128)(2,1)S(1)} %bitcast.126), channel_id=1, source_target_pairs={{0,2},{2,0},{16,18},{18,16},{1,3},{3,1},{17,19},{19,17},{4,6},{6,4... | collective-permute-start | bytes 2359304 | tf_op jit(solution)/shard_map/ppermute | solution.py:26
  101.0 22.5 %collective-permute-start.22 = (bf16[256,1536]{0,1:T(8,128)(2,1)S(1)}, bf16[256,1536]{0,1:T(8,128)(2,1)S(1)}, u32[]{:S(2)}, u32[]{:S(2)}) collective-permute-start(bf16[256,1536]{0,1:T(8,128)(2,1)S(1)} %bitcast.127), channel_id=1, source_target_pairs={{0,16},{2,18},{16,0},{18,2},{1,17},{3,19},{17,1},{19,3},{4,20},{6,... | collective-permute-start | bytes 2359304 | tf_op jit(solution)/shard_map/ppermute | solution.py:26
  103.7 62.9 %collective-permute-start.23 = (bf16[256,1536]{0,1:T(8,128)(2,1)S(1)}, bf16[256,1536]{0,1:T(8,128)(2,1)S(1)}, u32[]{:S(2)}, u32[]{:S(2)}) collective-permute-start(bf16[256,1536]{0,1:T(8,128)(2,1)S(1)} %bitcast.128), channel_id=1, source_target_pairs={{0,18},{2,16},{16,2},{18,0},{1,19},{3,17},{17,3},{19,1},{4,22},{6,... | collective-permute-start | bytes 2359304 | tf_op jit(solution)/shard_map/ppermute | solution.py:26
  106.2 61.1 %collective-permute-start.24 = (bf16[256,1536]{0,1:T(8,128)(2,1)S(1)}, bf16[256,1536]{0,1:T(8,128)(2,1)S(1)}, u32[]{:S(2)}, u32[]{:S(2)}) collective-permute-start(bf16[256,1536]{0,1:T(8,128)(2,1)S(1)} %bitcast.129), channel_id=1, source_target_pairs={{0,1},{1,0},{2,3},{3,2},{4,5},{5,4},{6,7},{7,6},{8,9},{9,8},{10,11... | collective-permute-start | bytes 2359304 | tf_op jit(solution)/shard_map/ppermute | solution.py:22
  106.4 19.1 %collective-permute-start.7 = (bf16[384,640]{0,1:T(8,128)(2,1)S(1)}, bf16[384,640]{0,1:T(8,128)(2,1)S(1)}, u32[]{:S(2)}, u32[]{:S(2)}) collective-permute-start(bf16[384,640]{0,1:T(8,128)(2,1)S(1)} %copy.120), channel_id=1, source_target_pairs={{0,4},{4,0},{8,12},{12,8},{1,5},{5,1},{9,13},{13,9},{2,6},{6,2},{1... | collective-permute-start | bytes 1474568 | tf_op jit(solution)/shard_map/ppermute | solution.py:26
  117.8 37.6 %collective-permute-start.8 = (bf16[384,640]{0,1:T(8,128)(2,1)S(1)}, bf16[384,640]{0,1:T(8,128)(2,1)S(1)}, u32[]{:S(2)}, u32[]{:S(2)}) collective-permute-start(bf16[384,640]{0,1:T(8,128)(2,1)S(1)} %copy.120), channel_id=1, source_target_pairs={{0,8},{4,12},{8,0},{12,4},{1,9},{5,13},{9,1},{13,5},{2,10},{6,14},... | collective-permute-start | bytes 1474568 | tf_op jit(solution)/shard_map/ppermute | solution.py:26
  123.6 42.9 %collective-permute-start.9 = (bf16[384,640]{0,1:T(8,128)(2,1)S(1)}, bf16[384,640]{0,1:T(8,128)(2,1)S(1)}, u32[]{:S(2)}, u32[]{:S(2)}) collective-permute-start(bf16[384,640]{0,1:T(8,128)(2,1)S(1)} %copy.120), channel_id=1, source_target_pairs={{0,12},{4,8},{8,4},{12,0},{1,13},{5,9},{9,5},{13,1},{2,14},{6,10},... | collective-permute-start | bytes 1474568 | tf_op jit(solution)/shard_map/ppermute | solution.py:26
  125.5 44.0 %collective-permute-start.4 = (bf16[256,1536]{0,1:T(8,128)(2,1)}, bf16[256,1536]{0,1:T(8,128)(2,1)S(1)}, u32[]{:S(2)}, u32[]{:S(2)}) collective-permute-start(bf16[256,1536]{0,1:T(8,128)(2,1)} %collective-permute-done), channel_id=1, source_target_pairs={{0,1},{1,0},{2,3},{3,2},{4,5},{5,4},{6,7},{7,6},{8,9},{9,8},{10,11... | collective-permute-start | bytes 2359304 | tf_op jit(solution)/shard_map/ppermute | solution.py:22
  155.3 14.8 %collective-permute-start.5 = (bf16[256,1536]{0,1:T(8,128)(2,1)}, bf16[256,1536]{0,1:T(8,128)(2,1)S(1)}, u32[]{:S(2)}, u32[]{:S(2)}) collective-permute-start(bf16[256,1536]{0,1:T(8,128)(2,1)} %collective-permute-done.1), channel_id=1, source_target_pairs={{0,1},{1,0},{2,3},{3,2},{4,5},{5,4},{6,7},{7,6},{8,9},{9,8},{10,11... | collective-permute-start | bytes 2359304 | tf_op jit(solution)/shard_map/ppermute | solution.py:22
  166.4 3.8 collective-permute-start.6
  166.6 2.7 collective-permute-start.10
  167.3 3.2 collective-permute-start.25
  169.3 6.8 %collective-permute-start.26 = (bf16[256,1536]{0,1:T(8,128)(2,1)S(1)}, bf16[256,1536]{0,1:T(8,128)(2,1)S(1)}, u32[]{:S(2)}, u32[]{:S(2)}) collective-permute-start(bf16[256,1536]{0,1:T(8,128)(2,1)S(1)} %collective-permute-done.22), channel_id=1, source_target_pairs={{0,1},{1,0},{2,3},{3,2},{4,5},{5,4},{6,7},{7,6},{8,9},{9,8},{10,11... | collective-permute-start | bytes 2359304 | tf_op jit(solution)/shard_map/ppermute | solution.py:22
  169.6 21.9 %collective-permute-start.27 = (bf16[256,1536]{0,1:T(8,128)(2,1)S(1)}, bf16[256,1536]{0,1:T(8,128)(2,1)S(1)}, u32[]{:S(2)}, u32[]{:S(2)}) collective-permute-start(bf16[256,1536]{0,1:T(8,128)(2,1)S(1)} %collective-permute-done.23), channel_id=1, source_target_pairs={{0,1},{1,0},{2,3},{3,2},{4,5},{5,4},{6,7},{7,6},{8,9},{9,8},{10,11... | collective-permute-start | bytes 2359304 | tf_op jit(solution)/shard_map/ppermute | solution.py:22
  199.7 1.3 collective-permute-start.28
  201.4 13.5 %collective-permute-start.29 = (f32[2,2,2,2,256]{4,3,2,1,0:T(2,128)S(1)}, f32[2,2,2,2,256]{4,3,2,1,0:T(2,128)S(1)}, u32[]{:S(2)}, u32[]{:S(2)}) collective-permute-start(f32[2,2,2,2,256]{4,3,2,1,0:T(2,128)S(1)} %rev.16), channel_id=1, source_target_pairs={{0,18},{2,16},{16,2},{18,0},{1,19},{3,17},{17,3},{19,1},{4,22},{6,... | collective-permute-start | bytes 49160 | tf_op jit(solution)/shard_map/ppermute | solution.py:26
  204.3 10.5 %collective-permute-start.30 = (f32[2,2,2,2,256]{4,3,2,1,0:T(2,128)S(1)}, f32[2,2,2,2,256]{4,3,2,1,0:T(2,128)S(1)}, u32[]{:S(2)}, u32[]{:S(2)}) collective-permute-start(f32[2,2,2,2,256]{4,3,2,1,0:T(2,128)S(1)} %rev.17), channel_id=1, source_target_pairs={{0,2},{2,0},{16,18},{18,16},{1,3},{3,1},{17,19},{19,17},{4,6},{6,4... | collective-permute-start | bytes 49160 | tf_op jit(solution)/shard_map/ppermute | solution.py:26
  204.5 10.4 %collective-permute-start.31 = (f32[2,2,2,2,256]{4,3,2,1,0:T(2,128)S(1)}, f32[2,2,2,2,256]{4,3,2,1,0:T(2,128)S(1)}, u32[]{:S(2)}, u32[]{:S(2)}) collective-permute-start(f32[2,2,2,2,256]{4,3,2,1,0:T(2,128)S(1)} %rev.18), channel_id=1, source_target_pairs={{0,16},{2,18},{16,0},{18,2},{1,17},{3,19},{17,1},{19,3},{4,20},{6,... | collective-permute-start | bytes 49160 | tf_op jit(solution)/shard_map/ppermute | solution.py:26
  214.9 204.2 %collective-permute-start.17 = (bf16[1024,1536]{0,1:T(8,128)(2,1)}, bf16[1024,1536]{0,1:T(8,128)(2,1)}, u32[]{:S(2)}, u32[]{:S(2)}) collective-permute-start(bf16[1024,1536]{0,1:T(8,128)(2,1)} %slice.214), channel_id=1, source_target_pairs={{0,1},{1,0},{2,3},{3,2},{4,5},{5,4},{6,7},{7,6},{8,9},{9,8},{10,11... | collective-permute-start | bytes 9437192 | tf_op jit(solution)/shard_map/ppermute | solution.py:22
  215.0 40.8 %slice-start.7 = ((s8[6291456]{0:T(1024)(128)(4,1)}), s8[4194304]{0:T(1024)(128)(4,1)S(1)}, s32[]{:S(2)}) async-start(s8[6291456]{0:T(1024)(128)(4,1)} %bitcast.116), calls=%async_computation.13 | async-start | bytes 8388608
  226.6 44.6 %copy-start.10 = (bf16[2048,384]{1,0:T(8,128)(2,1)}, bf16[2048,384]{1,0:T(8,128)(2,1)S(1)}, u32[]{:S(2)}) copy-start(bf16[2048,384]{1,0:T(8,128)(2,1)S(1)} %get-tuple-element.64) | copy-start | bytes 4718596
  293.2 2.7 collective-permute-start.36
  295.9 6.0 %collective-permute-start.37 = (f32[169,128]{1,0:T(8,128)S(1)}, f32[169,128]{1,0:T(8,128)S(1)}, u32[]{:S(2)}, u32[]{:S(2)}) collective-permute-start(f32[169,128]{1,0:T(8,128)S(1)} %fusion.57), channel_id=1, source_target_pairs={{0,18},{2,16},{16,2},{18,0},{1,19},{3,17},{17,3},{19,1},{4,22},{6,... | collective-permute-start | bytes 259592 | tf_op jit(solution)/shard_map/ppermute | solution.py:26
  298.8 4.7 collective-permute-start.38
  299.0 4.6 collective-permute-start.39
  299.6 33.4 %collective-permute-start.50 = (bf16[384,384]{1,0:T(8,128)(2,1)S(1)}, bf16[384,384]{1,0:T(8,128)(2,1)S(1)}, u32[]{:S(2)}, u32[]{:S(2)}) collective-permute-start(bf16[384,384]{1,0:T(8,128)(2,1)S(1)} %get-tuple-element.82), channel_id=1, source_target_pairs={{0,8},{4,12},{8,0},{12,4},{1,9},{5,13},{9,1},{13,5},{2,10},{6,14},... | collective-permute-start | bytes 884744 | tf_op jit(solution)/shard_map/ppermute | solution.py:26
  299.7 33.1 %slice-start.4 = ((s8[4718592]{0:T(1024)(128)(4,1)}), s8[4194304]{0:T(1024)(128)(4,1)S(1)}, s32[]{:S(2)}) async-start(s8[4718592]{0:T(1024)(128)(4,1)} %bitcast.114), calls=%async_computation.10 | async-start | bytes 8388608
  299.7 33.1 %slice-start.5 = ((s8[4718592]{0:T(1024)(128)(4,1)}), s8[524288]{0:T(1024)(128)(4,1)S(1)}, s32[]{:S(2)}) async-start(s8[4718592]{0:T(1024)(128)(4,1)} %bitcast.114), calls=%async_computation.11 | async-start | bytes 1048576
  303.6 23.8 %collective-permute-start.40 = (f32[169,128]{1,0:T(8,128)S(1)}, f32[169,128]{1,0:T(8,128)S(1)}, u32[]{:S(2)}, u32[]{:S(2)}) collective-permute-start(f32[169,128]{1,0:T(8,128)S(1)} %add_add_fusion.1), channel_id=1, source_target_pairs={{0,12},{4,8},{8,4},{12,0},{1,13},{5,9},{9,5},{13,1},{2,14},{6,10},... | collective-permute-start | bytes 259592 | tf_op jit(solution)/shard_map/ppermute | solution.py:26
  305.4 22.3 %collective-permute-start.41 = (f32[169,128]{1,0:T(8,128)S(1)}, f32[169,128]{1,0:T(8,128)S(1)}, u32[]{:S(2)}, u32[]{:S(2)}) collective-permute-start(f32[169,128]{1,0:T(8,128)S(1)} %add_add_fusion.1), channel_id=1, source_target_pairs={{0,4},{4,0},{8,12},{12,8},{1,5},{5,1},{9,13},{13,9},{2,6},{6,2},{1... | collective-permute-start | bytes 259592 | tf_op jit(solution)/shard_map/ppermute | solution.py:26
  306.4 21.3 %collective-permute-start.42 = (f32[169,128]{1,0:T(8,128)S(1)}, f32[169,128]{1,0:T(8,128)S(1)}, u32[]{:S(2)}, u32[]{:S(2)}) collective-permute-start(f32[169,128]{1,0:T(8,128)S(1)} %add_add_fusion.1), channel_id=1, source_target_pairs={{0,8},{4,12},{8,0},{12,4},{1,9},{5,13},{9,1},{13,5},{2,10},{6,14},... | collective-permute-start | bytes 259592 | tf_op jit(solution)/shard_map/ppermute | solution.py:26
  327.4 9.9 %collective-permute-start.51 = (bf16[384,384]{1,0:T(8,128)(2,1)S(1)}, bf16[384,384]{1,0:T(8,128)(2,1)S(1)}, u32[]{:S(2)}, u32[]{:S(2)}) collective-permute-start(bf16[384,384]{1,0:T(8,128)(2,1)S(1)} %get-tuple-element.84), channel_id=1, source_target_pairs={{0,12},{4,8},{8,4},{12,0},{1,13},{5,9},{9,5},{13,1},{2,14},{6,10},... | collective-permute-start | bytes 884744 | tf_op jit(solution)/shard_map/ppermute | solution.py:26
  327.7 10.2 %collective-permute-start.52 = (bf16[384,384]{1,0:T(8,128)(2,1)S(1)}, bf16[384,384]{1,0:T(8,128)(2,1)S(1)}, u32[]{:S(2)}, u32[]{:S(2)}) collective-permute-start(bf16[384,384]{1,0:T(8,128)(2,1)S(1)} %get-tuple-element.83), channel_id=1, source_target_pairs={{0,4},{4,0},{8,12},{12,8},{1,5},{5,1},{9,13},{13,9},{2,6},{6,2},{1... | collective-permute-start | bytes 884744 | tf_op jit(solution)/shard_map/ppermute | solution.py:26
  327.7 1.9 collective-permute-start.46
  329.6 22.7 %collective-permute-start.43 = (bf16[384,384]{1,0:T(8,128)(2,1)S(1)}, bf16[384,384]{1,0:T(8,128)(2,1)S(1)}, u32[]{:S(2)}, u32[]{:S(2)}) collective-permute-start(bf16[384,384]{1,0:T(8,128)(2,1)S(1)} %get-tuple-element.85), channel_id=1, source_target_pairs={{0,8},{4,12},{8,0},{12,4},{1,9},{5,13},{9,1},{13,5},{2,10},{6,14},... | collective-permute-start | bytes 884744 | tf_op jit(solution)/shard_map/ppermute | solution.py:26
  333.0 48.3 %collective-permute-start.44 = (bf16[384,384]{1,0:T(8,128)(2,1)S(1)}, bf16[384,384]{1,0:T(8,128)(2,1)S(1)}, u32[]{:S(2)}, u32[]{:S(2)}) collective-permute-start(bf16[384,384]{1,0:T(8,128)(2,1)S(1)} %get-tuple-element.87), channel_id=1, source_target_pairs={{0,12},{4,8},{8,4},{12,0},{1,13},{5,9},{9,5},{13,1},{2,14},{6,10},... | collective-permute-start | bytes 884744 | tf_op jit(solution)/shard_map/ppermute | solution.py:26
  337.3 49.8 %collective-permute-start.45 = (bf16[384,384]{1,0:T(8,128)(2,1)}, bf16[384,384]{1,0:T(8,128)(2,1)}, u32[]{:S(2)}, u32[]{:S(2)}) collective-permute-start(bf16[384,384]{1,0:T(8,128)(2,1)} %get-tuple-element.86), channel_id=1, source_target_pairs={{0,4},{4,0},{8,12},{12,8},{1,5},{5,1},{9,13},{13,9},{2,6},{6,2},{1... | collective-permute-start | bytes 884744 | tf_op jit(solution)/shard_map/ppermute | solution.py:26
  337.9 57.9 %collective-permute-start.47 = (bf16[384,640]{0,1:T(8,128)(2,1)}, bf16[384,640]{0,1:T(8,128)(2,1)S(1)}, u32[]{:S(2)}, u32[]{:S(2)}) collective-permute-start(bf16[384,640]{0,1:T(8,128)(2,1)} %get-tuple-element.73), channel_id=1, source_target_pairs={{0,8},{4,12},{8,0},{12,4},{1,9},{5,13},{9,1},{13,5},{2,10},{6,14},... | collective-permute-start | bytes 1474568 | tf_op jit(solution)/shard_map/ppermute | solution.py:26
  352.3 50.0 %collective-permute-start.48 = (bf16[384,640]{0,1:T(8,128)(2,1)}, bf16[384,640]{0,1:T(8,128)(2,1)}, u32[]{:S(2)}, u32[]{:S(2)}) collective-permute-start(bf16[384,640]{0,1:T(8,128)(2,1)} %get-tuple-element.75), channel_id=1, source_target_pairs={{0,12},{4,8},{8,4},{12,0},{1,13},{5,9},{9,5},{13,1},{2,14},{6,10},... | collective-permute-start | bytes 1474568 | tf_op jit(solution)/shard_map/ppermute | solution.py:26
  381.3 21.0 %collective-permute-start.49 = (bf16[384,640]{0,1:T(8,128)(2,1)}, bf16[384,640]{0,1:T(8,128)(2,1)}, u32[]{:S(2)}, u32[]{:S(2)}) collective-permute-start(bf16[384,640]{0,1:T(8,128)(2,1)} %get-tuple-element.74), channel_id=1, source_target_pairs={{0,4},{4,0},{8,12},{12,8},{1,5},{5,1},{9,13},{13,9},{2,6},{6,2},{1... | collective-permute-start | bytes 1474568 | tf_op jit(solution)/shard_map/ppermute | solution.py:26
  382.2 10.2 %all-to-all-start.5 = ((bf16[8,48,384]{2,1,0:T(8,128)(2,1)}), bf16[8,48,384]{2,1,0:T(8,128)(2,1)S(1)}, u32[]{:S(2)}, u32[]{:S(2)}) async-start(bf16[8,48,384]{2,1,0:T(8,128)(2,1)} %bitcast.41), calls=%async_computation.5 | async-start | bytes 589824 | tf_op jit(solution)/shard_map/all_to_all | solution.py:309
  387.2 41.1 %collective-permute-start.32 = (bf16[1024,1536]{0,1:T(8,128)(2,1)}, bf16[1024,1536]{0,1:T(8,128)(2,1)}, u32[]{:S(2)}, u32[]{:S(2)}) collective-permute-start(bf16[1024,1536]{0,1:T(8,128)(2,1)} %slice.223), channel_id=1, source_target_pairs={{0,1},{1,0},{2,3},{3,2},{4,5},{5,4},{6,7},{7,6},{8,9},{9,8},{10,11... | collective-permute-start | bytes 9437192 | tf_op jit(solution)/shard_map/ppermute | solution.py:22
  392.4 12.8 %all-to-all-start.3 = ((bf16[8,48,384]{2,1,0:T(8,128)(2,1)}), bf16[8,48,384]{2,1,0:T(8,128)(2,1)S(1)}, u32[]{:S(2)}, u32[]{:S(2)}) async-start(bf16[8,48,384]{2,1,0:T(8,128)(2,1)} %bitcast.29), calls=%async_computation.3 | async-start | bytes 589824 | tf_op jit(solution)/shard_map/all_to_all | solution.py:309
  405.2 12.6 %all-to-all-start.4 = ((bf16[8,48,640]{2,1,0:T(8,128)(2,1)}), bf16[8,48,640]{2,1,0:T(8,128)(2,1)S(1)}, u32[]{:S(2)}, u32[]{:S(2)}) async-start(bf16[8,48,640]{2,1,0:T(8,128)(2,1)} %bitcast.31), calls=%async_computation.4 | async-start | bytes 983040 | tf_op jit(solution)/shard_map/all_to_all | solution.py:309
  424.8 36.3 %collective-permute-start.18 = (bf16[256,1536]{0,1:T(8,128)(2,1)}, bf16[256,1536]{0,1:T(8,128)(2,1)}, u32[]{:S(2)}, u32[]{:S(2)}) collective-permute-start(bf16[256,1536]{0,1:T(8,128)(2,1)} %get-tuple-element.79), channel_id=1, source_target_pairs={{0,2},{2,0},{16,18},{18,16},{1,3},{3,1},{17,19},{19,17},{4,6},{6,4... | collective-permute-start | bytes 2359304 | tf_op jit(solution)/shard_map/ppermute | solution.py:26
  426.3 37.4 %collective-permute-start.19 = (bf16[256,1536]{0,1:T(8,128)(2,1)S(1)}, bf16[256,1536]{0,1:T(8,128)(2,1)}, u32[]{:S(2)}, u32[]{:S(2)}) collective-permute-start(bf16[256,1536]{0,1:T(8,128)(2,1)S(1)} %get-tuple-element.81), channel_id=1, source_target_pairs={{0,16},{2,18},{16,0},{18,2},{1,17},{3,19},{17,1},{19,3},{4,20},{6,... | collective-permute-start | bytes 2359304 | tf_op jit(solution)/shard_map/ppermute | solution.py:26
  426.8 36.9 %collective-permute-start.20 = (bf16[256,1536]{0,1:T(8,128)(2,1)S(1)}, bf16[256,1536]{0,1:T(8,128)(2,1)}, u32[]{:S(2)}, u32[]{:S(2)}) collective-permute-start(bf16[256,1536]{0,1:T(8,128)(2,1)S(1)} %get-tuple-element.80), channel_id=1, source_target_pairs={{0,18},{2,16},{16,2},{18,0},{1,19},{3,17},{17,3},{19,1},{4,22},{6,... | collective-permute-start | bytes 2359304 | tf_op jit(solution)/shard_map/ppermute | solution.py:26
  432.1 46.4 %collective-permute-start.33 = (bf16[256,1536]{0,1:T(8,128)(2,1)S(1)}, bf16[256,1536]{0,1:T(8,128)(2,1)S(1)}, u32[]{:S(2)}, u32[]{:S(2)}) collective-permute-start(bf16[256,1536]{0,1:T(8,128)(2,1)S(1)} %get-tuple-element.76), channel_id=1, source_target_pairs={{0,2},{2,0},{16,18},{18,16},{1,3},{3,1},{17,19},{19,17},{4,6},{6,4... | collective-permute-start | bytes 2359304 | tf_op jit(solution)/shard_map/ppermute | solution.py:26
  433.6 46.9 %collective-permute-start.34 = (bf16[256,1536]{0,1:T(8,128)(2,1)S(1)}, bf16[256,1536]{0,1:T(8,128)(2,1)S(1)}, u32[]{:S(2)}, u32[]{:S(2)}) collective-permute-start(bf16[256,1536]{0,1:T(8,128)(2,1)S(1)} %get-tuple-element.78), channel_id=1, source_target_pairs={{0,16},{2,18},{16,0},{18,2},{1,17},{3,19},{17,1},{19,3},{4,20},{6,... | collective-permute-start | bytes 2359304 | tf_op jit(solution)/shard_map/ppermute | solution.py:26
  461.1 34.6 %collective-permute-start.35 = (bf16[256,1536]{0,1:T(8,128)(2,1)S(1)}, bf16[256,1536]{0,1:T(8,128)(2,1)S(1)}, u32[]{:S(2)}, u32[]{:S(2)}) collective-permute-start(bf16[256,1536]{0,1:T(8,128)(2,1)S(1)} %get-tuple-element.77), channel_id=1, source_target_pairs={{0,18},{2,16},{16,2},{18,0},{1,19},{3,17},{17,3},{19,1},{4,22},{6,... | collective-permute-start | bytes 2359304 | tf_op jit(solution)/shard_map/ppermute | solution.py:26
  (59 other events, 530.3 us)

commit v2 on v1

v2 whole, which is shorter than its diff:
```python
import functools

import jax
import jax.numpy as jnp
from jax import lax
from jax.experimental import pallas as pl
from jax.experimental.pallas import tpu as pltpu
from jax.sharding import Mesh
from jax.sharding import PartitionSpec as P

EPSILON = 1e-05
LANES = 128
LOW = jnp.bfloat16

PLANE = ("xi", "yi", "c")
LINE = ("xo", "zo")
EVERY = ("xo", "xi", "zo", "yi", "c")


def swap(value):
    return lax.ppermute(value, "c", [(0, 1), (1, 0)])


def cross(value, axes, distance, count):
    return lax.ppermute(value, axes, [(i, i ^ distance) for i in range(count)])


def shift_down(value, rows):
    if rows == 0:
        return value
    index = lax.broadcasted_iota(jnp.int32, value.shape, 0)
    return jnp.where(index >= rows, pltpu.roll(value, rows, 0), 0.0)


def shift_up(value, rows):
    if rows == 0:
        return value
    length = value.shape[0]
    index = lax.broadcasted_iota(jnp.int32, value.shape, 0)
    return jnp.where(index < length - rows, pltpu.roll(value, length - rows, 0), 0.0)


def softplus(value):
    return jnp.maximum(value, 0.0) + jnp.log1p(jnp.exp(-jnp.abs(value)))


def dot_low(left, right):
    return jnp.dot(left, right, preferred_element_type=jnp.float32)


def dot_nt(left, right):
    return lax.dot_general(left, right, (((1,), (1,)), ((), ())), preferred_element_type=jnp.float32)


def dot_tn(left, right):
    return lax.dot_general(left, right, (((0,), (0,)), ((), ())), preferred_element_type=jnp.float32)


def parts_of(value, count):
    terms = []
    for _ in range(count):
        terms.append(value.astype(LOW))
        value = value - terms[-1].astype(jnp.float32)
    return terms


def convolve(conv_input, taps, bias):
    kernel_taps = taps.shape[0]
    summed = bias
    for tap in range(kernel_taps):
        summed = summed + taps[tap : tap + 1] * shift_down(conv_input, kernel_taps - 1 - tap)
    return summed


def triangle(length, lower):
    row = lax.broadcasted_iota(jnp.int32, (length, length), 0)
    column = lax.broadcasted_iota(jnp.int32, (length, length), 1)
    return row >= column if lower else row <= column


def cumulate(mask, value, count):
    mask = mask.astype(LOW)
    return sum(dot_low(mask, term) for term in parts_of(value, count))


def pair_lanes(value, pair, first):
    return jnp.where(first, value[:, 2 * pair : 2 * pair + 1], value[:, 2 * pair + 1 : 2 * pair + 2])


def lanes_sum(value, head_count):
    inner = value.shape[1]
    lane = lax.broadcasted_iota(jnp.int32, (inner, LANES), 0)
    head = lax.broadcasted_iota(jnp.int32, (inner, LANES), 1)
    member = (lane // (inner // head_count) == head).astype(LOW)
    return sum(dot_low(term, member) for term in parts_of(value, 2))


def read(ref):
    if not isinstance(ref, tuple):
        return ref[...]
    near, far = ref
    return jnp.where(pl.program_id(0) < pl.num_programs(0) // 2, near[...], far[...])


def row_spread(row):
    return jnp.broadcast_to(row, (8, row.shape[1])).T[:, :1]


def scan_forward(heads, part, taps_ref, bias_ref, dt_ref, alog_ref, skip_ref, out_ref):
    inner = out_ref.shape[1]
    length = out_ref.shape[0]
    width = taps_ref.shape[1]
    states = (width - inner) // 2
    conv_low = jax.nn.silu(convolve(part[:, :width], taps_ref[...], bias_ref[...])).astype(LOW)
    step = softplus(part[:, width:] + dt_ref[...])
    lower = triangle(length, True)
    cumulative = cumulate(lower, step * -jnp.exp(alog_ref[...]), 3)
    across = cumulative.T
    scores = dot_nt(conv_low[:, inner + states :], conv_low[:, inner : inner + states])
    scores = jnp.where(lower, scores, 0.0)
    first = lax.broadcasted_iota(jnp.int32, (length, LANES), 1) < inner // heads
    for pair in range(heads // 2):
        lanes = slice(pair * LANES, (pair + 1) * LANES)
        values = conv_low[:, lanes].astype(jnp.float32)
        scaled = (values * pair_lanes(step, pair, first)).astype(LOW)
        sums = []
        for head in (2 * pair, 2 * pair + 1):
            spread = cumulative[:, head : head + 1] - across[head : head + 1, :]
            mixing = scores * jnp.exp(jnp.where(lower, spread, 0.0))
            sums.append(dot_low(mixing.astype(LOW), scaled))
        out_ref[:, lanes] = jnp.where(first, sums[0], sums[1]) + skip_ref[:, lanes] * values


def norm_kernel(hidden_ref, gain_ref, *refs):
    stream = hidden_ref[...].astype(jnp.float32)
    scale = lax.rsqrt(jnp.mean(stream * stream, axis=-1, keepdims=True) + EPSILON)
    refs[-1][...] = (stream * scale * gain_ref[...]).astype(LOW)


def mask_kernel(lengths_ref, cotangent_ref, *refs):
    row = lax.broadcasted_iota(jnp.int32, cotangent_ref.shape, 0)
    own = cotangent_ref[...].astype(jnp.float32)
    refs[-1][...] = jnp.where(row < lengths_ref[0], own, 0.0).astype(LOW)


def copy_kernel(value_ref, *refs):
    refs[-1][...] = value_ref[...]


def conv_kernel(
    heads,
    place_ref,
    normed_ref,
    piece_0,
    piece_1,
    piece_2,
    piece_3,
    other_ref,
    taps_ref,
    bias_ref,
    dt_ref,
    alog_ref,
    skip_ref,
    part_ref,
    scanned_ref,
    weight_ref,
):
    inner = scanned_ref.shape[1]
    states = other_ref.shape[1]
    chunk = piece_0.shape[0] // 2

    @pl.when(pl.program_id(0) == 0)
    def _():
        core = place_ref[8]
        for away, piece in enumerate((piece_0, piece_1, piece_2, piece_3)):
            for half in range(2):
                rows = pl.ds(pl.multiple_of(place_ref[2 * away + half], 16), chunk)
                local = slice(half * chunk, (half + 1) * chunk)
                own = piece[local, inner : inner + states]
                other = other_ref[(2 * away + half) * chunk : (2 * away + half + 1) * chunk, :]
                weight_ref[rows, :inner] = piece[local, :inner]
                weight_ref[rows, inner : inner + states] = jnp.where(core == 0, own, other)
                weight_ref[rows, inner + states : inner + 2 * states] = jnp.where(core == 0, other, own)
                weight_ref[rows, inner + 2 * states :] = piece[local, inner + states :]

    part = dot_low(read(normed_ref), weight_ref[...])
    part_ref[...] = part
    scan_forward(heads, part, taps_ref, bias_ref, dt_ref, alog_ref, skip_ref, scanned_ref)


def scan_backward(
    heads,
    part_ref,
    grad_ref,
    scanned_ref,
    taps_ref,
    bias_ref,
    dt_ref,
    alog_ref,
    skip_ref,
    out_ref,
    small_ref,
):
    inner = grad_ref.shape[1]
    length = grad_ref.shape[0]
    width = taps_ref.shape[1]
    states = (width - inner) // 2
    kernel_taps = taps_ref.shape[0]
    conv_input = part_ref[:, :width]
    summed = convolve(conv_input, taps_ref[...], bias_ref[...])
    gate = jax.nn.sigmoid(summed)
    conv_low = (summed * gate).astype(LOW)
    slope = gate * (1.0 + summed * (1.0 - gate))
    raw = part_ref[:, width:] + dt_ref[...]
    step = softplus(raw)
    decay = -jnp.exp(alog_ref[...])
    lower = triangle(length, True)
    cumulative = cumulate(lower, step * decay, 3)
    across = cumulative.T
    b_rows = conv_low[:, inner : inner + states]
    c_rows = conv_low[:, inner + states :]
    scores = jnp.where(lower, dot_nt(c_rows, b_rows), 0.0)
    values = conv_low[:, :inner].astype(jnp.float32)
    half = inner // heads
    first = lax.broadcasted_iota(jnp.int32, (length, LANES), 1) < half
    steps = jnp.concatenate([pair_lanes(step, pair, first) for pair in range(heads // 2)], axis=1)
    scaled = (values * steps).astype(LOW)
    grad = grad_ref[...]
    grad_low = grad.astype(LOW)
    grad_across = grad.T.astype(LOW)
    upper_rows = lax.broadcasted_iota(jnp.int32, (LANES, length), 0) < half
    grad_scores = jnp.zeros((length, length), jnp.float32)
    moved = []
    for pair in range(heads // 2):
        lanes = slice(pair * LANES, (pair + 1) * LANES)
        sums = []
        for head in (2 * pair, 2 * pair + 1):
            spread = cumulative[:, head : head + 1] - across[head : head + 1, :]
            decays = jnp.where(lower, jnp.exp(jnp.where(lower, spread, 0.0)), 0.0)
            mixing = (scores * decays).astype(LOW)
            own = first if head % 2 == 0 else jnp.logical_not(first)
            grad_own = jnp.where(own, grad[:, lanes], 0.0).astype(LOW)
            grad_scores = grad_scores + dot_nt(grad_own, scaled[:, lanes]) * decays
            sums.append(dot_low(grad_across[lanes], mixing))
        moved.append(jnp.where(upper_rows, sums[0], sums[1]).T)
    grad_scaled = jnp.concatenate(moved, axis=1)
    within = scanned_ref[...] - skip_ref[...] * values
    grad_cumulative = lanes_sum(
        grad_low.astype(jnp.float32) * within - scaled.astype(jnp.float32) * grad_scaled, heads
    )
    grad_rate = cumulate(triangle(length, False), grad_cumulative, 3)
    grad_step = grad_rate * decay + lanes_sum(values * grad_scaled, heads)
    grad_raw = grad_step * jax.nn.sigmoid(raw)
    grad_values = steps * grad_scaled + skip_ref[...] * grad
    scores_low = grad_scores.astype(LOW)
    grad_c = dot_low(scores_low, b_rows)
    grad_b = dot_low(c_rows.T, scores_low).T
    grad_summed = jnp.concatenate([grad_values, grad_b, grad_c], axis=1) * slope
    grad_input = jnp.zeros_like(grad_summed)
    rows = []
    for tap in range(kernel_taps):
        away = kernel_taps - 1 - tap
        grad_input = grad_input + taps_ref[tap : tap + 1, :] * shift_up(grad_summed, away)
        rows.append(jnp.sum(grad_summed * shift_down(conv_input, away), axis=0, keepdims=True))
    rows.append(jnp.sum(grad_summed, axis=0, keepdims=True))
    out_ref[:, :width] = grad_input.astype(LOW)
    out_ref[:, width:] = grad_raw.astype(LOW)

    for index, row in enumerate(rows):
        small_ref[index : index + 1, :width] += row
    small_ref[5:6, :inner] += jnp.sum(grad * values, axis=0, keepdims=True)
    small_ref[5:6, width:] += jnp.sum(grad_raw, axis=0, keepdims=True)
    small_ref[6:7, width:] += jnp.sum(grad_rate * step, axis=0, keepdims=True) * decay


def gate_kernel(
    place_ref,
    normed_ref,
    upstream_ref,
    scanned_ref,
    piece_0,
    piece_1,
    piece_2,
    piece_3,
    gain_ref,
    gate_ref,
    mixed_ref,
    gained_ref,
    stats_ref,
    gate_weight,
    out_weight,
):
    inner = gain_ref.shape[1]
    length = gate_ref.shape[0]
    chunk = piece_0.shape[0] // 2
    slot = pl.program_id(0)

    @pl.when(slot == 0)
    def _():
        for away, piece in enumerate((piece_0, piece_1, piece_2, piece_3)):
            for half in range(2):
                rows = pl.ds(pl.multiple_of(place_ref[2 * away + half], 16), chunk)
                local = slice(half * chunk, (half + 1) * chunk)
                gate_weight[rows, :] = piece[local, :inner]
                out_weight[rows, :] = piece[local, inner:]

    gate = dot_low(read(normed_ref), gate_weight[...])
    gated = scanned_ref[...] * jax.nn.silu(gate)
    gained = gated * gain_ref[...]
    grad_mixed = dot_low(read(upstream_ref), out_weight[...])
    gate_ref[...] = gate
    mixed_ref[...] = grad_mixed
    gained_ref[...] = gained.astype(LOW)
    squares = jnp.sum(gated * gated, axis=1, keepdims=True)
    products = jnp.sum(grad_mixed * gained, axis=1, keepdims=True)
    lane = lax.broadcasted_iota(jnp.int32, (length, LANES), 1)
    turned = jnp.where(lane == 0, squares, products).T
    stats_ref[pl.ds(slot, 1), :] = turned[0:1]
    stats_ref[pl.ds(pl.num_programs(0) + slot, 1), :] = turned[1:2]


def branch_kernel(place_ref, gained_ref, weight_ref, out_ref):
    out_ref[...] = dot_nt(gained_ref[...], weight_ref[...]).astype(LOW)


def early_kernel(
    inner_all,
    place_ref,
    normed_ref,
    upstream_ref,
    scanned_ref,
    gate_ref,
    mixed_ref,
    stats_ref,
    gain_ref,
    grad_gate_ref,
    grad_scanned_ref,
    gain_grad_ref,
    piece_0,
    piece_1,
    piece_2,
    piece_3,
    sums_ref,
):
    slot = pl.program_id(0)
    inner = gain_ref.shape[1]
    chunk = piece_0.shape[0] // 2
    count = pl.num_programs(0)
    scale = lax.rsqrt(stats_ref[pl.ds(slot, 1), :] / inner_all + EPSILON)
    slope = scale * scale * scale * stats_ref[pl.ds(count + slot, 1), :] / inner_all
    scale, slope = row_spread(scale), row_spread(slope)
    gate = gate_ref[...]
    scanned = scanned_ref[...]
    sigmoid = jax.nn.sigmoid(gate)
    silu = gate * sigmoid
    gated = scanned * silu
    scaled = gated * scale
    mixed_low = (scaled * gain_ref[...]).astype(LOW)
    grad_mixed = mixed_ref[...]
    grad_gated = grad_mixed * gain_ref[...] * scale - gated * slope
    grad_gate = (grad_gated * scanned * (sigmoid * (1.0 + gate * (1.0 - sigmoid)))).astype(LOW)
    grad_gate_ref[...] = grad_gate
    grad_scanned_ref[...] = grad_gated * silu

    @pl.when(slot == 0)
    def _():
        sums_ref[...] = jnp.zeros_like(sums_ref)
        gain_grad_ref[...] = jnp.zeros_like(gain_grad_ref)

    gain_grad_ref[0:1, :] += jnp.sum(grad_mixed * scaled, axis=0, keepdims=True)
    sums_ref[:, :inner] += dot_tn(read(normed_ref), grad_gate)
    sums_ref[:, inner:] += dot_tn(read(upstream_ref), mixed_low)

    @pl.when(slot == count - 1)
    def _():
        for away, piece in enumerate((piece_0, piece_1, piece_2, piece_3)):
            for half in range(2):
                rows = pl.ds(pl.multiple_of(place_ref[2 * away + half], 16), chunk)
                piece[half * chunk : (half + 1) * chunk, :] = sums_ref[rows, :].astype(LOW)


def back_kernel(
    heads,
    place_ref,
    part_ref,
    grad_ref,
    scanned_ref,
    grad_gate_ref,
    normed_ref,
    weight_ref,
    gate_weight,
    taps_ref,
    bias_ref,
    dt_ref,
    alog_ref,
    skip_ref,
    normed_grad_ref,
    small_ref,
    pre_ref,
    given_ref,
    piece_0,
    piece_1,
    piece_2,
    piece_3,
    sums_ref,
    conv_ref,
):
    slot = pl.program_id(0)
    inner = grad_ref.shape[1]
    width = taps_ref.shape[1]
    states = (width - inner) // 2
    chunk = piece_0.shape[0] // 2

    @pl.when(slot == 0)
    def _():
        small_ref[...] = jnp.zeros_like(small_ref)
        pre_ref[...] = jnp.zeros_like(pre_ref)
        sums_ref[...] = jnp.zeros_like(sums_ref)

    scan_backward(
        heads,
        part_ref,
        grad_ref,
        scanned_ref,
        taps_ref,
        bias_ref,
        dt_ref,
        alog_ref,
        skip_ref,
        conv_ref,
        small_ref,
    )
    normed = read(normed_ref)
    grad_conv = conv_ref[...]
    sums_ref[...] += dot_tn(normed, grad_conv)
    grad_normed = dot_nt(grad_gate_ref[...], gate_weight[...]) + dot_nt(grad_conv, weight_ref[...])
    pre_ref[0:1, :] += jnp.sum(grad_normed * normed.astype(jnp.float32), axis=0, keepdims=True)

    normed_grad_ref[...] = grad_normed.astype(LOW)

    @pl.when(slot == pl.num_programs(0) - 1)
    def _():
        core = place_ref[8]
        for away, piece in enumerate((piece_0, piece_1, piece_2, piece_3)):
            for half in range(2):
                rows = pl.ds(pl.multiple_of(place_ref[2 * away + half], 16), chunk)
                local = slice(half * chunk, (half + 1) * chunk)
                whole = slice((2 * away + half) * chunk, (2 * away + half + 1) * chunk)
                b_sums = sums_ref[rows, inner : inner + states].astype(LOW)
                c_sums = sums_ref[rows, inner + states : width].astype(LOW)
                given_ref[whole, :] = jnp.where(core == 0, c_sums, b_sums)
                piece[local, :inner] = sums_ref[rows, :inner].astype(LOW)
                piece[local, inner : inner + states] = jnp.where(core == 0, b_sums, c_sums)
                piece[local, inner + states :] = sums_ref[rows, width:].astype(LOW)


def row_block(length, width):
    return pl.BlockSpec((length, width), lambda slot, place: (slot, 0))


def core_block(length, width, half):
    def index(slot, place):
        return (2 * (slot % half) + (place[8] ^ (slot // half)), 0)

    return pl.BlockSpec((length, width), index)


def near_block(length, width, half):
    return pl.BlockSpec((length, width), lambda slot, place: (jnp.minimum(slot, half - 1), 0))


def far_block(length, width, half):
    return pl.BlockSpec((length, width), lambda slot, place: (jnp.maximum(slot - half, 0), 0))


def whole_block(shape):
    return pl.BlockSpec(shape, lambda slot, place: (0,) * len(shape))


def run_slots(kernel, slots, place, cut, whole, outs, scratch, micros, waits=(), block=row_block):
    in_specs, arrays, places = [], [], []
    for array in cut:
        places.append(len(arrays))
        if isinstance(array, tuple):
            length = 2 * array[0].shape[0] // slots
            in_specs.append(near_block(length, array[0].shape[1], slots // 2))
            in_specs.append(far_block(length, array[1].shape[1], slots // 2))
            arrays.extend(array)
        else:
            in_specs.append(block(array.shape[0] // slots, array.shape[1]))
            arrays.append(array)
    in_specs += [whole_block(array.shape) for array in whole]
    arrays += whole
    given = len(arrays)

    def run(place_ref, *refs):
        cut_refs = [
            (refs[at], refs[at + 1]) if isinstance(array, tuple) else refs[at]
            for at, array in zip(places, cut)
        ]
        kernel(place_ref, *cut_refs, *refs[given - len(whole) : given], *refs[given + len(waits) :])

    return pl.pallas_call(
        run,
        grid_spec=pltpu.PrefetchScalarGridSpec(
            num_scalar_prefetch=1,
            grid=(slots,),
            in_specs=in_specs + [pl.BlockSpec(memory_space=pl.ANY)] * len(waits),
            out_specs=[spec for _, _, spec in outs],
            scratch_shapes=scratch,
        ),
        out_shape=[jax.ShapeDtypeStruct(shape, dtype) for shape, dtype, _ in outs],
        compiler_params=pltpu.CompilerParams(vmem_limit_bytes=44 << 20),
        cost_estimate=pl.CostEstimate(flops=int(micros * 1e9), bytes_accessed=1 << 20, transcendentals=0),
    )(place, *arrays, *waits)


def copies(kernel, scalars, value, others, count, waits=()):
    shape = value.shape
    return pl.pallas_call(
        kernel,
        grid_spec=pltpu.PrefetchScalarGridSpec(
            num_scalar_prefetch=len(scalars),
            grid=(count,),
            in_specs=[pl.BlockSpec(array.shape, lambda *_: (0, 0)) for array in (value, *others)]
            + [pl.BlockSpec(memory_space=pl.ANY)] * len(waits),
            out_specs=pl.BlockSpec(shape, lambda index, *_: (index, 0)),
        ),
        out_shape=jax.ShapeDtypeStruct((count * shape[0], shape[1]), LOW),
        compiler_params=pltpu.CompilerParams(vmem_limit_bytes=16 << 20),
        cost_estimate=pl.CostEstimate(flops=int(2e9), bytes_accessed=1 << 20, transcendentals=0),
    )(*scalars, value, *others, *waits)


def combine(terms, dtype, waits=()):
    shape = terms[0].shape
    steps = max(1, shape[0] // 384)

    def run(*refs):
        values = [ref[...].astype(jnp.float32) for ref in refs[: len(terms)]]
        if len(values) == 4:
            values = [values[0] + values[1], values[2] + values[3]]
        refs[-1][...] = sum(values[1:], values[0]).astype(dtype)

    block = pl.BlockSpec((shape[0] // steps, shape[1]), lambda index: (index, 0))
    return pl.pallas_call(
        run,
        grid=(steps,),
        in_specs=[block] * len(terms) + [pl.BlockSpec(memory_space=pl.ANY)] * len(waits),
        out_specs=block,
        out_shape=jax.ShapeDtypeStruct(shape, dtype),
        cost_estimate=pl.CostEstimate(flops=int(1e9), bytes_accessed=1 << 20, transcendentals=0),
    )(*terms, *waits)


def hold(values, waits):
    anywhere = pl.BlockSpec(memory_space=pl.ANY)
    return pl.pallas_call(
        lambda *refs: None,
        in_specs=[anywhere] * (len(values) + len(waits)),
        out_specs=[anywhere] * len(values),
        out_shape=[jax.ShapeDtypeStruct(value.shape, value.dtype) for value in values],
        input_output_aliases={index: index for index in range(len(values))},
    )(*values, *waits)


def add_states(pieces, states, start):
    rows, width = states.shape[0] // len(pieces), states.shape[1]
    count = len(pieces)

    def run(*refs):
        for index in range(count):
            own = refs[index][...].astype(jnp.float32)
            other = refs[count][index * rows : (index + 1) * rows, :].astype(jnp.float32)
            refs[count + 1 + index][...] = (own + other).astype(LOW)

    block = pl.BlockSpec((rows, width), lambda _: (0, start // width))
    return pl.pallas_call(
        run,
        grid=(1,),
        in_specs=[block] * count + [pl.BlockSpec(states.shape, lambda _: (0, 0))],
        out_specs=[block] * count,
        out_shape=[jax.ShapeDtypeStruct(piece.shape, piece.dtype) for piece in pieces],
        input_output_aliases={index: index for index in range(count)},
        cost_estimate=pl.CostEstimate(flops=int(1e9), bytes_accessed=1 << 20, transcendentals=0),
    )(*pieces, states)


def columns_of(value, start, width, waits):
    return pl.pallas_call(
        copy_kernel,
        grid=(1,),
        in_specs=[
            pl.BlockSpec((value.shape[0], LANES * (width // LANES)), lambda _: (0, start // width))
        ]
        + [pl.BlockSpec(memory_space=pl.ANY)] * len(waits),
        out_specs=pl.BlockSpec((value.shape[0], width), lambda _: (0, 0)),
        out_shape=jax.ShapeDtypeStruct((value.shape[0], width), LOW),
        cost_estimate=pl.CostEstimate(flops=int(1e9), bytes_accessed=1 << 20, transcendentals=0),
    )(value, *waits)


def body(
    sizes,
    hidden_in,
    lengths,
    cotangent,
    pre_gain,
    in_weight,
    conv_weight,
    conv_bias,
    dt_bias,
    a_log,
    skip,
    inner_gain,
    out_weight,
):
    length, model = hidden_in.shape
    rows = in_weight.shape[0]
    inner_all = out_weight.shape[1]
    heads_all = dt_bias.shape[0]
    states = (conv_weight.shape[1] - inner_all) // 2
    ranks = sizes["xi"] * sizes["yi"] * sizes["c"]
    lines = sizes["xo"] * sizes["zo"]
    slots = ranks
    tokens = slots * length
    inner = inner_all // ranks
    heads = heads_all // ranks
    head_width = inner // heads
    core = lax.axis_index("c")
    rank = (lax.axis_index("xi") * sizes["yi"] + lax.axis_index("yi")) * sizes["c"] + core
    direct = sizes["xo"] == 1 and sizes["zo"] == 4
    piece_rows = model // 4
    chunk = piece_rows // 2
    spread = (sizes["xo"], sizes["zo"], sizes["xi"], sizes["yi"] * sizes["c"] * rows)
    natural = (sizes["xo"], sizes["xi"], sizes["zo"], sizes["yi"] * sizes["c"] * rows)
    if direct:
        planes = [lax.axis_index("zo") ^ away for away in range(4)]
        starts = [half * (model // 2) + plane * chunk for plane in planes for half in range(2)]
    else:
        starts = [chunk * index for index in range(8)]
    place = jnp.stack([jnp.asarray(value, jnp.int32) for value in (*starts, core)])

    def gather_rows(piece):
        if direct:
            return [piece] + [cross(piece, LINE, away, 4) for away in range(1, 4)]
        whole = lax.all_gather(piece, LINE, axis=0, tiled=True).reshape(*spread, -1)
        whole = whole.transpose(0, 2, 1, 3, 4).reshape(model, -1)
        return [whole[index * piece_rows : (index + 1) * piece_rows] for index in range(4)]

    def scatter_rows(pieces, waits=()):
        if direct:
            moved = [cross(pieces[away], LINE, away, 4) for away in (2, 3, 1)]
            return combine([pieces[0], *moved], LOW, waits)
        whole = jnp.concatenate(pieces, axis=0).reshape(*natural, -1)
        whole = whole.transpose(0, 2, 1, 3, 4).reshape(model, -1)
        moved = lax.all_to_all(whole, LINE, split_axis=0, concat_axis=0, tiled=True)
        return jnp.sum(moved.reshape(lines, model // lines, -1).astype(jnp.float32), axis=0).astype(LOW)

    def exchange(value):
        return lax.all_to_all(value, PLANE, split_axis=0, concat_axis=0, tiled=True)

    def gather_tokens(value):
        return lax.all_gather(value, PLANE, axis=0, tiled=True)

    def scatter_far(value):
        return lax.psum_scatter(value, PLANE, scatter_dimension=0, tiled=True)

    def by_rank(columns):
        return columns.reshape(rows, ranks, -1).transpose(1, 0, 2)

    first_state = 2 * inner_all
    first_step = first_state + 2 * states
    state_columns = in_weight[:, first_state:first_step].reshape(rows, 2, states).transpose(1, 0, 2)
    packed = jnp.concatenate(
        [
            by_rank(in_weight[:, :inner_all]),
            by_rank(out_weight),
            by_rank(in_weight[:, inner_all:first_state]),
            jnp.tile(state_columns, (ranks // 2, 1, 1)),
            jnp.pad(by_rank(in_weight[:, first_step:]), ((0, 0), (0, 0), (0, LANES - heads))),
        ],
        axis=2,
    )
    plane_weights = exchange(packed).reshape(ranks * rows, -1)
    conv_pieces = gather_rows(plane_weights[:, 2 * inner :])
    other_states = swap(jnp.concatenate([piece[:, inner : inner + states] for piece in conv_pieces], axis=0))
    late_pieces = gather_rows(columns_of(plane_weights, 0, 2 * inner, conv_pieces[1:]))

    stream = hidden_in.astype(jnp.float32)
    scale = lax.rsqrt(jnp.mean(stream * stream, axis=-1, keepdims=True) + EPSILON)
    valid = (jnp.arange(length) < lengths[0])[:, None]
    own_upstream = jnp.where(valid, cotangent, jnp.zeros_like(cotangent))
    own_normed = copies(norm_kernel, (), hidden_in, (pre_gain[None],), 1)
    normed = gather_tokens(own_normed)
    upstream = gather_tokens(copies(mask_kernel, (lengths,), cotangent, (), 1, (own_normed,)))

    def of_rank(value, count):
        return lax.dynamic_slice_in_dim(value, rank * count, count, axis=-1)

    taps = jnp.concatenate(
        [of_rank(conv_weight[:, :inner_all], inner), conv_weight[:, inner_all:]], axis=1
    )
    bias = jnp.concatenate([of_rank(conv_bias[:inner_all], inner), conv_bias[inner_all:]])[None]
    dt_row = jnp.pad(of_rank(dt_bias, heads), (0, LANES - heads))[None]
    alog_row = jnp.pad(of_rank(a_log, heads), (0, LANES - heads))[None]
    skip_row = jnp.repeat(of_rank(skip, heads), head_width)[None]
    gain_row = of_rank(inner_gain, inner)[None]
    params = (taps, bias, dt_row, alog_row, skip_row)
    part_width = inner + 2 * states + LANES

    part, scanned, conv_weights = run_slots(
        functools.partial(conv_kernel, heads),
        slots,
        place,
        (normed,),
        (*conv_pieces, other_states, *params),
        [
            ((tokens, part_width), jnp.float32, row_block(length, part_width)),
            ((tokens, inner), jnp.float32, row_block(length, inner)),
            ((model, part_width), LOW, whole_block((model, part_width))),
        ],
        [],
        12,
    )
    gate, grad_mixed, gained, stats, gate_weights, out_weights = run_slots(
        gate_kernel,
        slots,
        place,
        (normed, upstream, scanned),
        (*late_pieces, gain_row),
        [
            ((tokens, inner), jnp.float32, row_block(length, inner)),
            ((tokens, inner), jnp.float32, row_block(length, inner)),
            ((tokens, inner), LOW, row_block(length, inner)),
            ((2 * slots, length), jnp.float32, whole_block((2 * slots, length))),
            ((model, inner), LOW, whole_block((model, inner))),
            ((model, inner), LOW, whole_block((model, inner))),
        ],
        [],
        8,
    )
    stats = stats + swap(stats)
    far = [cross(stats, ("xi", "yi"), away, 4) for away in (3, 1, 2)]
    stats = (stats + far[0]) + (far[1] + far[2])
    (branch,) = run_slots(
        branch_kernel,
        slots,
        place,
        (gained,),
        (out_weights,),
        [((tokens, model), LOW, row_block(length, model))],
        [],
        5,
    )
    branch_own = scatter_far(branch)
    squares = lax.dynamic_index_in_dim(stats, rank, axis=0, keepdims=False)
    inner_scale = lax.rsqrt(squares / inner_all + EPSILON)[:, None]
    output = jnp.where(valid, stream + branch_own * inner_scale, 0.0).astype(LOW)

    piece_shape = (piece_rows, 2 * inner)
    grad_gate, grad_scanned, gain_grad, *early = run_slots(
        functools.partial(early_kernel, inner_all),
        slots,
        place,
        (normed, upstream, scanned, gate, grad_mixed),
        (stats, gain_row),
        [
            ((tokens, inner), LOW, row_block(length, inner)),
            ((tokens, inner), jnp.float32, row_block(length, inner)),
            ((8, inner), jnp.float32, whole_block((8, inner))),
        ]
        + [(piece_shape, LOW, whole_block(piece_shape))] * 4,
        [pltpu.VMEM((model, 2 * inner), jnp.float32)],
        16,
        (branch,),
    )
    piece_shape = (piece_rows, inner + states + LANES)
    held = run_slots(
        functools.partial(back_kernel, heads),
        slots,
        place,
        (part, grad_scanned, scanned, grad_gate, normed),
        (conv_weights, gate_weights, *params),
        [
            ((tokens, model), LOW, row_block(length, model)),
            ((8, part_width), jnp.float32, whole_block((8, part_width))),
            ((8, model), jnp.float32, whole_block((8, model))),
            ((model, states), LOW, whole_block((model, states))),
        ]
        + [(piece_shape, LOW, whole_block(piece_shape))] * 4,
        [pltpu.VMEM((model, part_width), jnp.float32), pltpu.VMEM((length, part_width), LOW)],
        40,
    )
    if direct:
        early_moved = [cross(early[away], LINE, away, 4) for away in (2, 3, 1)]
        held = hold(held, [*early_moved, branch_own])
    grad_normed, small, pre_grad, given, *pieces = held
    pieces = add_states(pieces, swap(given), inner)
    grad_own = scatter_far(grad_normed) * pre_gain
    along = jnp.mean(grad_own * stream, axis=-1, keepdims=True)
    grad_stream = grad_own * scale - stream * (scale**3 * along)
    grad_hidden = (own_upstream.astype(jnp.float32) + grad_stream).astype(LOW)

    def to_owners(value):
        return exchange(value.astype(LOW).reshape(ranks, rows, -1)).astype(jnp.float32)

    def all_columns(value):
        return value.transpose(1, 0, 2).reshape(rows, -1)

    early_sum = combine([early[0], *early_moved], LOW) if direct else scatter_rows(early)
    owned_early = to_owners(early_sum)
    conv_sum = scatter_rows(pieces)
    owned_conv = to_owners(conv_sum)
    owned_states = owned_conv[:, :, inner : inner + states].reshape(ranks // 2, 2, rows, states)
    owned_in = jnp.concatenate(
        [
            all_columns(owned_early[:, :, :inner]),
            all_columns(owned_conv[:, :, :inner]),
            all_columns(jnp.sum(owned_states, axis=0)),
            all_columns(owned_conv[:, :, inner + states : inner + states + heads]),
        ],
        axis=1,
    )
    owned_out = all_columns(owned_early[:, :, inner:])

    def place_rank(value, total):
        blank = jnp.zeros(value.shape[:-1] + (total,), jnp.float32)
        return lax.dynamic_update_slice_in_dim(blank, value, rank * value.shape[-1], axis=-1)

    taps_count = conv_weight.shape[0]
    width = taps.shape[1]
    conv_small = small[: taps_count + 1, :width]
    conv_small = jnp.concatenate(
        [place_rank(conv_small[:, :inner], inner_all), conv_small[:, inner:]], axis=1
    )
    head_small = jnp.stack(
        [
            small[5, width : width + heads],
            small[6, width : width + heads],
            jnp.sum(small[5, :inner].reshape(heads, head_width), axis=1),
        ]
    )
    head_small = jnp.pad(place_rank(head_small, heads_all), ((0, 0), (0, LANES - heads_all)))
    grads = (pre_grad[0] / pre_gain, conv_small, place_rank(gain_grad[0], inner_all), head_small)
    flat = jnp.concatenate([grad.reshape(-1, LANES) for grad in grads], axis=0)
    flat = combine([flat, swap(flat)], jnp.float32, (early_sum,))
    flat = combine([flat, *(cross(flat, ("xi", "yi"), away, 4) for away in (3, 1, 2))], jnp.float32, (conv_sum,))
    if direct:
        flat = combine([flat, *(cross(flat, LINE, away, 4) for away in (3, 1, 2))], jnp.float32)
    else:
        flat = lax.psum(flat, LINE)
    sums = []
    start = 0
    for grad in grads:
        count = grad.size // LANES
        sums.append(flat[start : start + count].reshape(grad.shape))
        start += count
    return (
        output,
        grad_hidden,
        sums[0],
        owned_in,
        sums[1][:taps_count],
        sums[1][taps_count],
        sums[3][0, :heads_all],
        sums[3][1, :heads_all],
        sums[3][2, :heads_all],
        sums[2],
        owned_out,
    )


def solution(mesh):
    dp, fsdp = mesh.shape["dp"], mesh.shape["fsdp"]
    shape = (dp // 2, 2, fsdp // 4, 2, 2)
    fine = Mesh(mesh.devices.reshape(shape), EVERY)
    split, kept = P(EVERY, None), P()
    in_specs = (split, P(EVERY), split, kept, split, kept, kept, kept, kept, kept, kept, split)
    out_specs = (split, split, kept, split, kept, kept, kept, kept, kept, kept, split)
    return jax.shard_map(
        functools.partial(body, dict(zip(EVERY, shape))),
        mesh=fine,
        in_specs=in_specs,
        out_specs=out_specs,
        check_vma=False,
    )
```

time: 507 us -> 348 us (0.69)
  waiting for transfers between devices: 238 us -> 104 us
  Pallas kernels: 40.2 us -> 110 us
  matrix products: 62.3 us -> 0 us
  starting transfers between devices: 77.7 us -> 35.4 us
  blocking collectives: 0 us -> 27.9 us
  other arithmetic: 29 us -> 6.88 us
  between operations: 3.15 us -> 15.1 us
  local copies, waits for them, and re-layouts: 50.6 us -> 44.1 us
    ppermute x39 -> x21, waiting for transfers between devices: 209 us -> 101 us  [cross(): return lax.ppermute(value, axes, [(i, i ^ distance) for i in range(count)])]
    pallas_call x2 -> x15, Pallas kernels: 40.2 us -> 110 us  [the longest x5 93.9 us: run_slots(): pl.pallas_call(run, grid_spec=pltpu.PrefetchScalarGridSpec(num_scalar_pre...]
    dot_general x9 -> x0, matrix products: 62.3 us -> none  [the longest x3 25.1 us: dot_nt(): lax.dot_general(left, right, (((1,), (1,)), ((), ())), preferred_element_...]
    all_to_all x0 -> x1, blocking collectives: none -> 27.9 us  [exchange(): return lax.all_to_all(value, PLANE, split_axis=0, concat_axis=0, tiled=True)]
    all_to_all x6 -> x2, waiting for transfers between devices: 27 us -> 0.01 us  [exchange(): return lax.all_to_all(value, PLANE, split_axis=0, concat_axis=0, tiled=True)]
    ppermute x39 -> x21, starting transfers between devices: 51.3 us -> 26.8 us  [cross(): return lax.ppermute(value, axes, [(i, i ^ distance) for i in range(count)])]
    all_to_all x6 -> x2, starting transfers between devices: 23.3 us -> 7.77 us  [exchange(): return lax.all_to_all(value, PLANE, split_axis=0, concat_axis=0, tiled=True)]
    unnamed x139 -> x112, local copies, waits for them, and re-layouts: 15.5 us -> 29.2 us
  transfers between devices with their start and end apart: 59 -> 31, of which waited for: 26 -> 14; matrix products, arithmetic and copies ran while one was open for 24% -> 5% of each run, Pallas kernels for 8% -> 26%
where the time goes in v2:
time: 348 us; the launch traced here: 344 us
  Pallas kernels  110 us (32%)
  waiting for transfers between devices  104 us (30%)
  local copies, waits for them, and re-layouts  44.1 us (13%)
  starting transfers between devices  35.4 us (10%)
  blocking collectives  27.9 us (8%)
  between operations  15.1 us (4%)
  other arithmetic  6.88 us (2%)
    ppermute x21, waiting for transfers between devices, cross(): return lax.ppermute(value, axes, [(i, i ^ distance) for i in range(count)])  101 us
    pallas_call x5, Pallas kernels, run_slots(): pl.pallas_call(run, grid_spec=pltpu.PrefetchScalarGridSpec(num_scalar_pre...  93.9 us
    unnamed x112, local copies, waits for them, and re-layouts  29.2 us
    all_to_all x1, blocking collectives, exchange(): return lax.all_to_all(value, PLANE, split_axis=0, concat_axis=0, tiled=True)  27.9 us
    ppermute x21, starting transfers between devices, cross(): return lax.ppermute(value, axes, [(i, i ^ distance) for i in range(count)])  26.8 us
    pallas_call x5, Pallas kernels, combine(): pl.pallas_call(run, grid=(steps,), in_specs=[block] * len(terms) + [pl.Bl...  10.2 us
    all_to_all x2, starting transfers between devices, exchange(): return lax.all_to_all(value, PLANE, split_axis=0, concat_axis=0, tiled=True)  7.77 us
  transfers between devices with their start and end apart: 31, of which 14 were waited for; matrix products, arithmetic and copies ran while one was open for 5% of the time, Pallas kernels for 26%

profile of v2, /device:TPU:16, one launch (start us, length us, event | category | flops | bytes accessed | tf_op | source)
XLA Modules:
  0.0 344.0 jit_solution(17368433655617863189)
XLA Ops:
  7.9 1.1 copy-done.1
  9.1 1.2 shard_map.203.refs_0_
  11.0 1.0 shard_map.204
  13.3 27.9 %all_to_all.15 = bf16[8,48,1408]{2,1,0:T(8,128)(2,1)} all-to-all(bf16[8,48,1408]{2,1,0:T(8,128)(2,1)S(1)} %pad_dynamic-update-slice_fusion), channel_id=1, replica_groups=mesh['xo'=1,'xi'=2,'zo'=4,'yi'=2,'c'=2] {'xi','yi','c'}, dimensions={0} | all-to-all | bytes 2162688 | tf_op jit(solution)/shard_map/all_to_all | solution.py:661
  41.2 1.1 slice.142.refs_1_
  42.2 1.6 collective-permute-start
  44.2 1.6 collective-permute-start.2
  47.2 0.9 slice.143
  48.1 15.4 %collective-permute-done.refs_2_.refs_0_ = bf16[384,640]{1,0:T(8,128)(2,1)S(1)} collective-permute-done((bf16[384,640]{1,0:T(8,128)(2,1)S(1)}, bf16[384,640]{1,0:T(8,128)(2,1)S(1)}, u32[]{:S(2)}, u32[]{:S(2)}) %collective-permute-start) | collective-permute-done | bytes 491552 | tf_op jit(solution)/shard_map/ppermute | solution.py:25
  63.5 13.5 %collective-permute-done.1.refs_3_.refs_1_ = bf16[384,640]{1,0:T(8,128)(2,1)S(1)} collective-permute-done((bf16[384,640]{1,0:T(8,128)(2,1)S(1)}, bf16[384,640]{1,0:T(8,128)(2,1)S(1)}, u32[]{:S(2)}, u32[]{:S(2)}) %collective-permute-start.1) | collective-permute-done | bytes 491552 | tf_op jit(solution)/shard_map/ppermute | solution.py:25
  77.0 11.1 %collective-permute-done.2.refs_4_.refs_2_ = bf16[384,640]{1,0:T(8,128)(2,1)S(1)} collective-permute-done((bf16[384,640]{1,0:T(8,128)(2,1)S(1)}, bf16[384,640]{1,0:T(8,128)(2,1)S(1)}, u32[]{:S(2)}, u32[]{:S(2)}) %collective-permute-start.2) | collective-permute-done | bytes 491552 | tf_op jit(solution)/shard_map/ppermute | solution.py:25
  88.0 0.9 pad_maximum_fusion.1
  89.0 1.9 shard_map.206.refs_3_
  90.9 1.9 collective-permute-start.5
  92.8 1.6 collective-permute-start.6
  95.2 1.0 copy-done.14
  96.2 1.0 copy-done.16
  97.2 1.0 copy-done.18
  98.3 1.0 copy-done.21
  99.3 18.2 %shard_map.205 = (f32[2048,768]{1,0:T(8,128)}, f32[2048,384]{1,0:T(8,128)S(1)}, bf16[1536,768]{1,0:T(8,128)(2,1)S(1)}) custom-call(s32[9]{0:T(128)S(1)} %stack.46.place_ref, bf16[2048,1536]{1,0:T(8,128)(2,1)} %all-gather.3.cloned.1.call-done.refs_0_.refs_4_, bf16[384,640]{1,0:T(8,128)(2,1)S(1)} %slice.142.refs_1_, bf16[384,640]{1,0:T(8,128)(2,1)S(1)} %copy-done.14, ...), custom_call_target="tpu_custom_call" | custom-call | flops 12000000000 | bytes 1048576 | tf_op jit(solution)/shard_map/pallas_call | solution.py:503
  117.5 1.7 copy-done.23
  119.1 1.4 copy-done.29
  120.6 11.6 %collective-permute-done.5.refs_5_ = bf16[384,768]{1,0:T(8,128)(2,1)} collective-permute-done((bf16[384,768]{1,0:T(8,128)(2,1)}, bf16[384,768]{1,0:T(8,128)(2,1)}, u32[]{:S(2)}, u32[]{:S(2)}) %collective-permute-start.5) | collective-permute-done | bytes 589856 | tf_op jit(solution)/shard_map/ppermute | solution.py:25
  132.1 13.9 %collective-permute-done.6.refs_6_ = bf16[384,768]{1,0:T(8,128)(2,1)} collective-permute-done((bf16[384,768]{1,0:T(8,128)(2,1)}, bf16[384,768]{1,0:T(8,128)(2,1)}, u32[]{:S(2)}, u32[]{:S(2)}) %collective-permute-start.6) | collective-permute-done | bytes 589856 | tf_op jit(solution)/shard_map/ppermute | solution.py:25
  146.1 14.0 %shard_map.207 = (f32[2048,384]{1,0:T(8,128)S(1)}, f32[2048,384]{1,0:T(8,128)}, bf16[2048,384]{1,0:T(8,128)(2,1)S(1)}, f32[16,256]{1,0:T(8,128)S(1)}, bf16[1536,...) custom-call(s32[9]{0:T(128)S(1)} %stack.46.place_ref, ...), custom_call_target="tpu_custom_call" | custom-call | flops 8000000000 | bytes 1048576 | tf_op jit(solution)/shard_map/pallas_call | solution.py:503
  160.1 1.6 copy-done.25
  161.7 5.4 %shard_map.208.refs_7_ = bf16[2048,1536]{1,0:T(8,128)(2,1)S(1)} custom-call(s32[9]{0:T(128)S(1)} %stack.46.place_ref, bf16[2048,384]{1,0:T(8,128)(2,1)S(1)} %get-tuple-element.48.refs_0_, bf16[1536,384]{1,0:T(8,128)(2,1)S(1)} %get-tuple-element.49.refs_1_), custom_call_target="tpu_custom_call" | custom-call | flops 5000000000 | bytes 1048576 | tf_op jit(solution)/shard_map/pallas_call | solution.py:503
  167.1 2.6 copy-done
  170.0 1.2 collective-permute-done.7
  171.8 1.8 collective-permute-start.8
  173.6 1.1 collective-permute-start.9
  175.0 1.5 collective-permute-done.8
  176.4 0.9 collective-permute-done.9
  177.3 2.3 copy-done.24
  179.6 16.5 %shard_map.209 = (bf16[2048,384]{1,0:T(8,128)(2,1)S(1)}, f32[2048,384]{1,0:T(8,128)S(1)}, f32[8,384]{1,0:T(8,128)S(1)}, bf16[384,768]{1,0:T(8,128)(2,1)S(1)}, bf...) custom-call(s32[9]{0:T(128)S(1)} %stack.46.place_ref, ...), custom_call_target="tpu_custom_call" | custom-call | flops 16000000000 | bytes 1048576 | tf_op jit(solution)/shard_map/pallas_call | solution.py:503
  197.0 1.6 copy-done.28
  199.2 3.8 %collective-permute-start.13 = (bf16[384,768]{1,0:T(8,128)(2,1)S(1)}, bf16[384,768]{1,0:T(8,128)(2,1)S(1)}, u32[]{:S(2)}, u32[]{:S(2)}) collective-permute-start(bf16[384,768]{1,0:T(8,128)(2,1)S(1)} %get-tuple-element.68), channel_id=1, source_target_pairs={{0,4},{4,0},{8,12},{12,8},{1,5},{5,1},{9,13},{13,9},{2,6},{6,2},{1... | collective-permute-start | bytes 1769480 | tf_op jit(solution)/shard_map/ppermute | solution.py:25
  203.0 39.8 %shard_map.210 = (bf16[2048,1536]{1,0:T(8,128)(2,1)}, f32[8,768]{1,0:T(8,128)S(1)}, f32[8,1536]{1,0:T(8,128)S(1)}, bf16[1536,128]{1,0:T(8,128)(2,1)S(1)}, bf16[3...) custom-call(s32[9]{0:T(128)S(1)} %stack.46.place_ref, ...), custom_call_target="tpu_custom_call" | custom-call | flops 40000000000 | bytes 1048576 | tf_op jit(solution)/shard_map/pallas_call | solution.py:503
  250.0 2.8 shard_map.212.refs_2_
  252.7 3.5 %all-to-all-start.1 = ((bf16[8,48,768]{2,1,0:T(8,128)(2,1)}), bf16[8,48,768]{2,1,0:T(8,128)(2,1)S(1)}, u32[]{:S(2)}, u32[]{:S(2)}) async-start(bf16[8,48,768]{2,1,0:T(8,128)(2,1)} %bitcast.93), calls=%async_computation.3 | async-start | bytes 1179648 | tf_op jit(solution)/shard_map/all_to_all | solution.py:661
  257.2 0.8 slice_reduce_fusion
  259.3 2.2 shard_map.214
  261.5 0.9 collective-permute-start.20
  262.5 3.5 %collective-permute-start.21 = (bf16[384,640]{1,0:T(8,128)(2,1)}, bf16[384,640]{1,0:T(8,128)(2,1)}, u32[]{:S(2)}, u32[]{:S(2)}) collective-permute-start(bf16[384,640]{1,0:T(8,128)(2,1)} %get-tuple-element.82), channel_id=1, source_target_pairs={{0,4},{4,0},{8,12},{12,8},{1,5},{5,1},{9,13},{13,9},{2,6},{6,2},{1... | collective-permute-start | bytes 1474568 | tf_op jit(solution)/shard_map/ppermute | solution.py:25
  266.2 1.1 collective-permute-done.14.refs_1_
  268.0 1.6 shard_map.213.refs_0_
  269.5 2.2 collective-permute-start.15
  272.3 22.3 %collective-permute-done.19.refs_1_ = bf16[384,640]{1,0:T(8,128)(2,1)S(1)} collective-permute-done((bf16[384,640]{1,0:T(8,128)(2,1)}, bf16[384,640]{1,0:T(8,128)(2,1)S(1)}, u32[]{:S(2)}, u32[]{:S(2)}) %collective-permute-start.19) | collective-permute-done | bytes 491552 | tf_op jit(solution)/shard_map/ppermute | solution.py:25
  294.6 1.2 collective-permute-start.17
  295.8 10.3 %collective-permute-done.20.refs_2_ = bf16[384,640]{1,0:T(8,128)(2,1)} collective-permute-done((bf16[384,640]{1,0:T(8,128)(2,1)}, bf16[384,640]{1,0:T(8,128)(2,1)}, u32[]{:S(2)}, u32[]{:S(2)}) %collective-permute-start.20) | collective-permute-done | bytes 491552 | tf_op jit(solution)/shard_map/ppermute | solution.py:25
  306.1 2.5 shard_map.215.refs_4_
  309.9 1.7 shard_map.216.refs_0_
  311.6 1.1 collective-permute-start.22
  312.7 2.4 collective-permute-start.24
  315.2 0.9 copy.87
  316.1 4.2 %all-to-all-start.2 = ((bf16[8,48,640]{2,1,0:T(8,128)(2,1)}), bf16[8,48,640]{2,1,0:T(8,128)(2,1)S(1)}, u32[]{:S(2)}, u32[]{:S(2)}) async-start(bf16[8,48,640]{2,1,0:T(8,128)(2,1)} %bitcast.26), calls=%async_computation.4 | async-start | bytes 983040 | tf_op jit(solution)/shard_map/all_to_all | solution.py:661
  321.6 1.7 shard_map.217
  324.7 1.3 slice_bitcast_fusion.6
  326.0 1.3 slice_bitcast_fusion.5
  327.3 1.3 slice_bitcast_fusion.7
  328.6 1.3 slice_bitcast_fusion.4
  331.8 2.0 pad_maximum_fusion
  333.9 1.6 fusion.2
  335.5 2.0 fusion.6
  (214 shorter events, 23.7 us)
Async XLA Ops:
  7.2 88.0 %all-gather.3.cloned.1.call-start = ((), (), s32[]{:S(2)}) async-start(), calls=%async_computation.5 | async-start | bytes 7077888 | tf_op jit(solution)/shard_map/all_gather | solution.py:664
  7.9 1.1 copy-start.1
  9.1 1.9 copy-start.3
  10.3 135.8 %all-gather.5.cloned.1.call-start = ((), (), s32[]{:S(2)}) async-start(), calls=%async_computation.6 | async-start | bytes 7077888 | tf_op jit(solution)/shard_map/all_gather | solution.py:664
  11.0 1.1 slice-start
  11.0 1.2 slice-start.1
  11.0 1.4 copy-start.33
  12.1 236.6 %reduce-scatter.3.cloned.1.call-start = ((), (), s32[]{:S(2)}) async-start(), calls=%async_computation.7 | async-start | bytes 7077888 | tf_op jit(solution)/shard_map/reduce_scatter | solution.py:667
  13.2 32.6 %copy-start.49 = (f32[48]{0:T(128)S(1)}, f32[48]{0:T(128)}, u32[]{:S(2)}) copy-start(f32[48]{0:T(128)} %param.19) | copy-start | bytes 580
  13.2 32.6 %copy-start.50 = (f32[48]{0:T(128)S(1)}, f32[48]{0:T(128)}, u32[]{:S(2)}) copy-start(f32[48]{0:T(128)} %param.20) | copy-start | bytes 580
  13.3 32.7 %slice-start.4 = ((f32[3328]{0:T(1024)}), f32[3072]{0:T(1024)S(1)}, s32[]{:S(2)}) async-start(f32[3328]{0:T(1024)} %param.18), calls=%async_computation.13 | async-start | bytes 24576 | tf_op jit(solution)/shard_map/slice | solution.py:704
  13.3 32.8 %slice-start.5 = ((f32[3328]{0:T(1024)}), f32[256]{0:T(256)S(1)}, s32[]{:S(2)}) async-start(f32[3328]{0:T(1024)} %param.18), calls=%async_computation.14 | async-start | bytes 2048 | tf_op jit(solution)/shard_map/slice | solution.py:704
  13.3 32.8 %copy-start.51 = (f32[48]{0:T(128)S(1)}, f32[48]{0:T(128)}, u32[]{:S(2)}) copy-start(f32[48]{0:T(128)} %param.21) | copy-start | bytes 580
  41.2 47.8 %slice-start.2 = ((f32[4,3328]{1,0:T(4,128)}), f32[4,3072]{1,0:T(4,128)S(1)}, s32[]{:S(2)}) async-start(f32[4,3328]{1,0:T(4,128)} %param.17), calls=%async_computation.11 | async-start | bytes 98304 | tf_op jit(solution)/shard_map/slice | solution.py:702
  41.2 47.8 %slice-start.3 = ((f32[4,3328]{1,0:T(4,128)}), f32[4,256]{1,0:T(4,128)S(1)}, s32[]{:S(2)}) async-start(f32[4,3328]{1,0:T(4,128)} %param.17), calls=%async_computation.12 | async-start | bytes 8192 | tf_op jit(solution)/shard_map/slice | solution.py:702
  42.2 21.2 %collective-permute-start = (bf16[384,640]{1,0:T(8,128)(2,1)S(1)}, bf16[384,640]{1,0:T(8,128)(2,1)S(1)}, u32[]{:S(2)}, u32[]{:S(2)}) collective-permute-start(bf16[384,640]{1,0:T(8,128)(2,1)S(1)} %slice.142.refs_1_), channel_id=1, source_target_pairs={{0,4},{4,0},{8,12},{12,8},{1,5},{5,1},{9,13},{13,9},{2,6},{6,2},{1... | collective-permute-start | bytes 1474568 | tf_op jit(solution)/shard_map/ppermute | solution.py:25
  43.9 33.1 %collective-permute-start.1 = (bf16[384,640]{1,0:T(8,128)(2,1)S(1)}, bf16[384,640]{1,0:T(8,128)(2,1)S(1)}, u32[]{:S(2)}, u32[]{:S(2)}) collective-permute-start(bf16[384,640]{1,0:T(8,128)(2,1)S(1)} %slice.142.refs_1_), channel_id=1, source_target_pairs={{0,8},{4,12},{8,0},{12,4},{1,9},{5,13},{9,1},{13,5},{2,10},{6,14},... | collective-permute-start | bytes 1474568 | tf_op jit(solution)/shard_map/ppermute | solution.py:25
  44.2 43.8 %collective-permute-start.2 = (bf16[384,640]{1,0:T(8,128)(2,1)S(1)}, bf16[384,640]{1,0:T(8,128)(2,1)S(1)}, u32[]{:S(2)}, u32[]{:S(2)}) collective-permute-start(bf16[384,640]{1,0:T(8,128)(2,1)S(1)} %slice.142.refs_1_), channel_id=1, source_target_pairs={{0,12},{4,8},{8,4},{12,0},{1,13},{5,9},{9,5},{13,1},{2,14},{6,10},... | collective-permute-start | bytes 1474568 | tf_op jit(solution)/shard_map/ppermute | solution.py:25
  63.5 25.5 %copy-start.13 = (bf16[384,640]{1,0:T(8,128)(2,1)}, bf16[384,640]{1,0:T(8,128)(2,1)S(1)}, u32[]{:S(2)}) copy-start(bf16[384,640]{1,0:T(8,128)(2,1)S(1)} %collective-permute-done.refs_2_.refs_0_) | copy-start | bytes 1474564
  77.0 12.0 %copy-start.15 = (bf16[384,640]{1,0:T(8,128)(2,1)}, bf16[384,640]{1,0:T(8,128)(2,1)S(1)}, u32[]{:S(2)}) copy-start(bf16[384,640]{1,0:T(8,128)(2,1)S(1)} %collective-permute-done.1.refs_3_.refs_1_) | copy-start | bytes 1474564
  88.9 5.5 %collective-permute-start.3 = (bf16[1536,128]{1,0:T(8,128)(2,1)}, bf16[1536,128]{1,0:T(8,128)(2,1)S(1)}, u32[]{:S(2)}, u32[]{:S(2)}) collective-permute-start(bf16[1536,128]{1,0:T(8,128)(2,1)} %pad_maximum_fusion.1), channel_id=1, source_target_pairs={{0,1},{1,0},{2,3},{3,2},{4,5},{5,4},{6,7},{7,6},{8,9},{9,8},{10,11... | collective-permute-start | bytes 1179656 | tf_op jit(solution)/shard_map/ppermute | solution.py:21
  90.9 29.7 %collective-permute-start.4 = (bf16[384,768]{1,0:T(8,128)(2,1)}, bf16[384,768]{1,0:T(8,128)(2,1)}, u32[]{:S(2)}, u32[]{:S(2)}) collective-permute-start(bf16[384,768]{1,0:T(8,128)(2,1)} %shard_map.206.refs_3_), channel_id=1, source_target_pairs={{0,4},{4,0},{8,12},{12,8},{1,5},{5,1},{9,13},{13,9},{2,6},{6,2},{1... | collective-permute-start | bytes 1769480 | tf_op jit(solution)/shard_map/ppermute | solution.py:25
  90.9 41.2 %collective-permute-start.5 = (bf16[384,768]{1,0:T(8,128)(2,1)}, bf16[384,768]{1,0:T(8,128)(2,1)}, u32[]{:S(2)}, u32[]{:S(2)}) collective-permute-start(bf16[384,768]{1,0:T(8,128)(2,1)} %shard_map.206.refs_3_), channel_id=1, source_target_pairs={{0,8},{4,12},{8,0},{12,4},{1,9},{5,13},{9,1},{13,5},{2,10},{6,14},... | collective-permute-start | bytes 1769480 | tf_op jit(solution)/shard_map/ppermute | solution.py:25
  92.8 53.3 %collective-permute-start.6 = (bf16[384,768]{1,0:T(8,128)(2,1)}, bf16[384,768]{1,0:T(8,128)(2,1)}, u32[]{:S(2)}, u32[]{:S(2)}) collective-permute-start(bf16[384,768]{1,0:T(8,128)(2,1)} %shard_map.206.refs_3_), channel_id=1, source_target_pairs={{0,12},{4,8},{8,4},{12,0},{1,13},{5,9},{9,5},{13,1},{2,14},{6,10},... | collective-permute-start | bytes 1769480 | tf_op jit(solution)/shard_map/ppermute | solution.py:25
  95.2 1.0 copy-start.14
  99.3 46.8 %copy-start.19 = (bf16[384,768]{1,0:T(8,128)(2,1)S(1)}, bf16[384,768]{1,0:T(8,128)(2,1)}, u32[]{:S(2)}) copy-start(bf16[384,768]{1,0:T(8,128)(2,1)} %shard_map.206.refs_3_) | copy-start | bytes 1769476
  117.5 1.7 copy-start.23
  119.1 1.5 copy-start.29
  160.1 1.6 copy-start.25
  161.7 5.4 %copy-start.26 = (bf16[1536,384]{1,0:T(8,128)(2,1)}, bf16[1536,384]{1,0:T(8,128)(2,1)S(1)}, u32[]{:S(2)}) copy-start(bf16[1536,384]{1,0:T(8,128)(2,1)S(1)} %get-tuple-element.57.refs_6_) | copy-start | bytes 3538948
  167.1 2.6 copy-start
  169.7 164.1 %reduce-scatter.5.cloned.1.call-start = ((), (), s32[]{:S(2)}) async-start(), calls=%async_computation.8 | async-start | bytes 7077888 | tf_op jit(solution)/shard_map/reduce_scatter | solution.py:667
  169.9 1.2 collective-permute-start.7
  171.2 3.8 %collective-permute-start.10 = (f32[16,256]{1,0:T(8,128)S(1)}, f32[16,256]{1,0:T(8,128)S(1)}, u32[]{:S(2)}, u32[]{:S(2)}) collective-permute-start(f32[16,256]{1,0:T(8,128)S(1)} %add.98), channel_id=1, source_target_pairs={{0,16},{2,18},{16,0},{18,2},{1,17},{3,19},{17,1},{19,3},{4,20},{6,... | collective-permute-start | bytes 49160 | tf_op jit(solution)/shard_map/ppermute | solution.py:25
  171.8 4.6 %collective-permute-start.8 = (f32[16,256]{1,0:T(8,128)S(1)}, f32[16,256]{1,0:T(8,128)S(1)}, u32[]{:S(2)}, u32[]{:S(2)}) collective-permute-start(f32[16,256]{1,0:T(8,128)S(1)} %add.98), channel_id=1, source_target_pairs={{0,18},{2,16},{16,2},{18,0},{1,19},{3,17},{17,3},{19,1},{4,22},{6,... | collective-permute-start | bytes 49160 | tf_op jit(solution)/shard_map/ppermute | solution.py:25
  173.6 3.7 %collective-permute-start.9 = (f32[16,256]{1,0:T(8,128)S(1)}, f32[16,256]{1,0:T(8,128)S(1)}, u32[]{:S(2)}, u32[]{:S(2)}) collective-permute-start(f32[16,256]{1,0:T(8,128)S(1)} %add.98), channel_id=1, source_target_pairs={{0,2},{2,0},{16,18},{18,16},{1,3},{3,1},{17,19},{19,17},{4,6},{6,4... | collective-permute-start | bytes 49160 | tf_op jit(solution)/shard_map/ppermute | solution.py:25
  177.3 2.3 copy-start.24
  179.6 23.4 %copy-start.27 = (bf16[1536,384]{1,0:T(8,128)(2,1)S(1)}, bf16[1536,384]{1,0:T(8,128)(2,1)}, u32[]{:S(2)}) copy-start(bf16[1536,384]{1,0:T(8,128)(2,1)} %copy-done.26) | copy-start | bytes 3538948
  179.6 23.4 %copy-start.30 = (bf16[1536,768]{1,0:T(8,128)(2,1)S(1)}, bf16[1536,768]{1,0:T(8,128)(2,1)}, u32[]{:S(2)}) copy-start(bf16[1536,768]{1,0:T(8,128)(2,1)} %copy-done.29) | copy-start | bytes 7077892
  197.0 1.6 copy-start.28
  198.6 49.3 %collective-permute-start.11 = (bf16[384,768]{1,0:T(8,128)(2,1)S(1)}, bf16[384,768]{1,0:T(8,128)(2,1)S(1)}, u32[]{:S(2)}, u32[]{:S(2)}) collective-permute-start(bf16[384,768]{1,0:T(8,128)(2,1)S(1)} %get-tuple-element.66), channel_id=1, source_target_pairs={{0,8},{4,12},{8,0},{12,4},{1,9},{5,13},{9,1},{13,5},{2,10},{6,14},... | collective-permute-start | bytes 1769480 | tf_op jit(solution)/shard_map/ppermute | solution.py:25
  198.6 50.0 %collective-permute-start.12 = (bf16[384,768]{1,0:T(8,128)(2,1)S(1)}, bf16[384,768]{1,0:T(8,128)(2,1)S(1)}, u32[]{:S(2)}, u32[]{:S(2)}) collective-permute-start(bf16[384,768]{1,0:T(8,128)(2,1)S(1)} %get-tuple-element.67), channel_id=1, source_target_pairs={{0,12},{4,8},{8,4},{12,0},{1,13},{5,9},{9,5},{13,1},{2,14},{6,10},... | collective-permute-start | bytes 1769480 | tf_op jit(solution)/shard_map/ppermute | solution.py:25
  199.2 49.4 %collective-permute-start.13 = (bf16[384,768]{1,0:T(8,128)(2,1)S(1)}, bf16[384,768]{1,0:T(8,128)(2,1)S(1)}, u32[]{:S(2)}, u32[]{:S(2)}) collective-permute-start(bf16[384,768]{1,0:T(8,128)(2,1)S(1)} %get-tuple-element.68), channel_id=1, source_target_pairs={{0,4},{4,0},{8,12},{12,8},{1,5},{5,1},{9,13},{13,9},{2,6},{6,2},{1... | collective-permute-start | bytes 1769480 | tf_op jit(solution)/shard_map/ppermute | solution.py:25
  250.0 6.3 %copy-start.9 = (bf16[1536,128]{1,0:T(8,128)(2,1)S(1)}, bf16[1536,128]{1,0:T(8,128)(2,1)}, u32[]{:S(2)}) copy-start(bf16[1536,128]{1,0:T(8,128)(2,1)} %get-tuple-element.78) | copy-start | bytes 1179652
  250.0 6.7 %copy-start.11 = (f32[8,768]{1,0:T(8,128)S(1)}, f32[8,768]{1,0:T(8,128)}, u32[]{:S(2)}) copy-start(f32[8,768]{1,0:T(8,128)} %get-tuple-element.71) | copy-start | bytes 73732
  252.7 13.3 %all-to-all-start.1 = ((bf16[8,48,768]{2,1,0:T(8,128)(2,1)}), bf16[8,48,768]{2,1,0:T(8,128)(2,1)S(1)}, u32[]{:S(2)}, u32[]{:S(2)}) async-start(bf16[8,48,768]{2,1,0:T(8,128)(2,1)} %bitcast.93), calls=%async_computation.3 | async-start | bytes 1179648 | tf_op jit(solution)/shard_map/all_to_all | solution.py:661
  256.3 2.3 collective-permute-start.18
  259.3 6.6 %copy-start.38 = (f32[1536]{0:T(1024)S(1)}, f32[1536]{0:T(1024)}, u32[]{:S(2)}) copy-start(f32[1536]{0:T(1024)} %param.15) | copy-start | bytes 18436
  261.5 33.0 %collective-permute-start.19 = (bf16[384,640]{1,0:T(8,128)(2,1)}, bf16[384,640]{1,0:T(8,128)(2,1)S(1)}, u32[]{:S(2)}, u32[]{:S(2)}) collective-permute-start(bf16[384,640]{1,0:T(8,128)(2,1)} %get-tuple-element.80), channel_id=1, source_target_pairs={{0,8},{4,12},{8,0},{12,4},{1,9},{5,13},{9,1},{13,5},{2,10},{6,14},... | collective-permute-start | bytes 1474568 | tf_op jit(solution)/shard_map/ppermute | solution.py:25
  261.5 44.6 %collective-permute-start.20 = (bf16[384,640]{1,0:T(8,128)(2,1)}, bf16[384,640]{1,0:T(8,128)(2,1)}, u32[]{:S(2)}, u32[]{:S(2)}) collective-permute-start(bf16[384,640]{1,0:T(8,128)(2,1)} %get-tuple-element.81), channel_id=1, source_target_pairs={{0,12},{4,8},{8,4},{12,0},{1,13},{5,9},{9,5},{13,1},{2,14},{6,10},... | collective-permute-start | bytes 1474568 | tf_op jit(solution)/shard_map/ppermute | solution.py:25
  262.5 43.6 %collective-permute-start.21 = (bf16[384,640]{1,0:T(8,128)(2,1)}, bf16[384,640]{1,0:T(8,128)(2,1)}, u32[]{:S(2)}, u32[]{:S(2)}) collective-permute-start(bf16[384,640]{1,0:T(8,128)(2,1)} %get-tuple-element.82), channel_id=1, source_target_pairs={{0,4},{4,0},{8,12},{12,8},{1,5},{5,1},{9,13},{13,9},{2,6},{6,2},{1... | collective-permute-start | bytes 1474568 | tf_op jit(solution)/shard_map/ppermute | solution.py:25
  265.9 1.4 copy-start.39
  266.0 1.4 collective-permute-start.14
  269.5 39.1 %collective-permute-start.15 = (f32[169,128]{1,0:T(8,128)}, f32[169,128]{1,0:T(8,128)S(1)}, u32[]{:S(2)}, u32[]{:S(2)}) collective-permute-start(f32[169,128]{1,0:T(8,128)} %shard_map.213.refs_0_), channel_id=1, source_target_pairs={{0,18},{2,16},{16,2},{18,0},{1,19},{3,17},{17,3},{19,1},{4,22},{6,... | collective-permute-start | bytes 259592 | tf_op jit(solution)/shard_map/ppermute | solution.py:25
  271.7 36.9 %collective-permute-start.16 = (f32[169,128]{1,0:T(8,128)}, f32[169,128]{1,0:T(8,128)S(1)}, u32[]{:S(2)}, u32[]{:S(2)}) collective-permute-start(f32[169,128]{1,0:T(8,128)} %shard_map.213.refs_0_), channel_id=1, source_target_pairs={{0,2},{2,0},{16,18},{18,16},{1,3},{3,1},{17,19},{19,17},{4,6},{6,4... | collective-permute-start | bytes 259592 | tf_op jit(solution)/shard_map/ppermute | solution.py:25
  294.6 11.6 %copy-start.40 = (bf16[384,640]{1,0:T(8,128)(2,1)}, bf16[384,640]{1,0:T(8,128)(2,1)S(1)}, u32[]{:S(2)}) copy-start(bf16[384,640]{1,0:T(8,128)(2,1)S(1)} %collective-permute-done.19.refs_1_) | copy-start | bytes 1474564
  294.6 14.1 %collective-permute-start.17 = (f32[169,128]{1,0:T(8,128)}, f32[169,128]{1,0:T(8,128)S(1)}, u32[]{:S(2)}, u32[]{:S(2)}) collective-permute-start(f32[169,128]{1,0:T(8,128)} %shard_map.213.refs_0_), channel_id=1, source_target_pairs={{0,16},{2,18},{16,0},{18,2},{1,17},{3,19},{17,1},{19,3},{4,20},{6,... | collective-permute-start | bytes 259592 | tf_op jit(solution)/shard_map/ppermute | solution.py:25
  311.6 8.7 %collective-permute-start.22 = (f32[169,128]{1,0:T(8,128)}, f32[169,128]{1,0:T(8,128)S(1)}, u32[]{:S(2)}, u32[]{:S(2)}) collective-permute-start(f32[169,128]{1,0:T(8,128)} %shard_map.216.refs_0_), channel_id=1, source_target_pairs={{0,12},{4,8},{8,4},{12,0},{1,13},{5,9},{9,5},{13,1},{2,14},{6,10},... | collective-permute-start | bytes 259592 | tf_op jit(solution)/shard_map/ppermute | solution.py:25
  312.7 7.6 %collective-permute-start.23 = (f32[169,128]{1,0:T(8,128)}, f32[169,128]{1,0:T(8,128)S(1)}, u32[]{:S(2)}, u32[]{:S(2)}) collective-permute-start(f32[169,128]{1,0:T(8,128)} %shard_map.216.refs_0_), channel_id=1, source_target_pairs={{0,4},{4,0},{8,12},{12,8},{1,5},{5,1},{9,13},{13,9},{2,6},{6,2},{1... | collective-permute-start | bytes 259592 | tf_op jit(solution)/shard_map/ppermute | solution.py:25
  312.7 7.6 %collective-permute-start.24 = (f32[169,128]{1,0:T(8,128)}, f32[169,128]{1,0:T(8,128)S(1)}, u32[]{:S(2)}, u32[]{:S(2)}) collective-permute-start(f32[169,128]{1,0:T(8,128)} %shard_map.216.refs_0_), channel_id=1, source_target_pairs={{0,8},{4,12},{8,0},{12,4},{1,9},{5,13},{9,1},{13,5},{2,10},{6,14},... | collective-permute-start | bytes 259592 | tf_op jit(solution)/shard_map/ppermute | solution.py:25
  316.1 13.9 %all-to-all-start.2 = ((bf16[8,48,640]{2,1,0:T(8,128)(2,1)}), bf16[8,48,640]{2,1,0:T(8,128)(2,1)S(1)}, u32[]{:S(2)}, u32[]{:S(2)}) async-start(bf16[8,48,640]{2,1,0:T(8,128)(2,1)} %bitcast.26), calls=%async_computation.4 | async-start | bytes 983040 | tf_op jit(solution)/shard_map/all_to_all | solution.py:661
  331.0 2.9 copy-start.2
  331.8 3.7 %copy-start.31 = (bf16[256,1536]{1,0:T(8,128)(2,1)S(1)}, bf16[256,1536]{1,0:T(8,128)(2,1)}, u32[]{:S(2)}) copy-start(bf16[256,1536]{1,0:T(8,128)(2,1)} %reduce-scatter.3.cloned.1.call-done.refs_11_) | copy-start | bytes 2359300
  333.8 1.7 copy-start.32
  (25 other events, 19.5 us)
Sparse Core Ops, SparseCore 0:
  10.5 56.1 all-gather.2
  69.1 45.5 all-gather.4
  169.8 60.2 reduce-scatter.2
  249.8 62.5 reduce-scatter.4

commit v3 on v2

--- a/solution.py
+++ b/solution.py
@@ -285,7 +285,7 @@
     gain_ref,
     gate_ref,
     mixed_ref,
-    gained_ref,
+    branch_ref,
     stats_ref,
     gate_weight,
     out_weight,
@@ -310,17 +310,13 @@
     grad_mixed = dot_low(read(upstream_ref), out_weight[...])
     gate_ref[...] = gate
     mixed_ref[...] = grad_mixed
-    gained_ref[...] = gained.astype(LOW)
+    branch_ref[...] = dot_nt(gained.astype(LOW), out_weight[...]).astype(LOW)
     squares = jnp.sum(gated * gated, axis=1, keepdims=True)
     products = jnp.sum(grad_mixed * gained, axis=1, keepdims=True)
     lane = lax.broadcasted_iota(jnp.int32, (length, LANES), 1)
     turned = jnp.where(lane == 0, squares, products).T
     stats_ref[pl.ds(slot, 1), :] = turned[0:1]
     stats_ref[pl.ds(pl.num_programs(0) + slot, 1), :] = turned[1:2]
-
-
-def branch_kernel(place_ref, gained_ref, weight_ref, out_ref):
-    out_ref[...] = dot_nt(gained_ref[...], weight_ref[...]).astype(LOW)
 
 
 def early_kernel(
@@ -394,9 +390,8 @@
     dt_ref,
     alog_ref,
     skip_ref,
+    gain_grad_ref,
     normed_grad_ref,
-    small_ref,
-    pre_ref,
     given_ref,
     piece_0,
     piece_1,
@@ -404,12 +399,15 @@
     piece_3,
     sums_ref,
     conv_ref,
+    small_ref,
+    pre_ref,
+    extra_ref,
 ):
     slot = pl.program_id(0)
     inner = grad_ref.shape[1]
     width = taps_ref.shape[1]
     states = (width - inner) // 2
-    chunk = piece_0.shape[0] // 2
+    chunk = sums_ref.shape[0] // 8
 
     @pl.when(slot == 0)
     def _():
@@ -441,6 +439,20 @@
     @pl.when(slot == pl.num_programs(0) - 1)
     def _():
         core = place_ref[8]
+        taps_count = taps_ref.shape[0]
+        extra_ref[...] = jnp.zeros_like(extra_ref)
+        extra_ref[: taps_count + 1, :] = small_ref[: taps_count + 1, :width]
+        extra_ref[5:6, :inner] = small_ref[5:6, :inner]
+        extra_ref[5:6, inner:] = pre_ref[0:1, 2 * width :]
+        extra_ref[6:7, :inner] = gain_grad_ref[0:1, :]
+        extra_ref[6:7, inner : inner + LANES] = small_ref[5:6, width:]
+        extra_ref[6:7, inner + LANES :] = small_ref[6:7, width:]
+        extra_ref[7:8, :] = pre_ref[0:1, :width]
+        extra_ref[8:9, :] = pre_ref[0:1, width : 2 * width]
+        high, rest = parts_of(extra_ref[...], 2)
+        for piece in (piece_0, piece_1, piece_2, piece_3):
+            piece[8 * chunk // 4 : 8 * chunk // 4 + 16, :] = high
+            piece[8 * chunk // 4 + 16 :, :] = rest
         for away, piece in enumerate((piece_0, piece_1, piece_2, piece_3)):
             for half in range(2):
                 rows = pl.ds(pl.multiple_of(place_ref[2 * away + half], 16), chunk)
@@ -564,9 +576,100 @@
     )(*values, *waits)
 
 
+def small_rows(below):
+    return below[:16].astype(jnp.float32) + below[16:].astype(jnp.float32)
+
+
+def side_sums(left, right, ranks):
+    rows, width = left[0].shape
+    own = rows // ranks
+    terms = (*left, *right)
+    small_width = right[0].shape[1]
+
+    def run(*refs):
+        def total(these, read):
+            values = [read(ref) for ref in these]
+            return (values[0] + values[1]) + (values[2] + values[3])
+
+        out_ref = refs[-1]
+        high, rest = parts_of(total(refs[4:8], lambda ref: small_rows(ref[rows:, :])), 2)
+        for rank in range(ranks):
+            local = slice(rank * own, (rank + 1) * own)
+            out_ref[rank, :own, :width] = total(refs[:4], lambda ref: ref[local, :].astype(jnp.float32)).astype(LOW)
+            out_ref[rank, :own, width:] = total(refs[4:8], lambda ref: ref[local, :].astype(jnp.float32)).astype(LOW)
+            out_ref[rank, own:, :small_width] = high
+            out_ref[rank, own:, small_width : 2 * small_width] = rest
+            out_ref[rank, own:, 2 * small_width :] = jnp.zeros_like(out_ref[rank, own:, 2 * small_width :])
+
+    shape = (ranks, own + 16, width + small_width)
+    return pl.pallas_call(
+        run,
+        out_shape=jax.ShapeDtypeStruct(shape, LOW),
+        compiler_params=pltpu.CompilerParams(vmem_limit_bytes=24 << 20),
+        cost_estimate=pl.CostEstimate(flops=int(3e9), bytes_accessed=1 << 20, transcendentals=0),
+    )(*terms)
+
+
+def owner_outputs(owned, rows, heads, states, sizes, waits):
+    proj, inner_all, taps_shape, model = sizes
+    ranks = owned.shape[0]
+    inner = inner_all // ranks
+    width = inner + 2 * states
+
+    def blocks(ref, store):
+        def lanes_of(value, rank):
+            lane = lax.broadcasted_iota(jnp.int32, value.shape, 1)
+            value = jnp.where(lane < heads, value, 0.0)
+            return pltpu.roll(value, rank * heads, 1)
+
+        in_ref, out_ref, taps_ref, bias_ref, gain_ref, pre_ref, head_ref = store
+        taps_count = taps_shape[0]
+        shared, b_sum, c_sum, step_sum, dt_sum, alog_sum, skip_sum = [0.0] * 7
+        for rank in range(ranks):
+            lanes = slice(rank * inner, (rank + 1) * inner)
+            main = ref[rank, :rows, :].astype(jnp.float32)
+            extra = ref[rank, rows:, :width].astype(jnp.float32) + ref[rank, rows:, width : 2 * width].astype(jnp.float32)
+            in_ref[:, lanes] = main[:, :inner]
+            out_ref[:, lanes] = main[:, inner : 2 * inner]
+            in_ref[:, inner_all + rank * inner : inner_all + (rank + 1) * inner] = main[:, 2 * inner : 3 * inner]
+            if rank % 2 == 0:
+                b_sum = b_sum + main[:, 3 * inner : 3 * inner + states]
+            else:
+                c_sum = c_sum + main[:, 3 * inner : 3 * inner + states]
+            step_sum = step_sum + lanes_of(main[:, 3 * inner + states :], rank)
+            shared = shared + extra
+            taps_ref[:, lanes] = extra[:taps_count, :inner]
+            bias_ref[:, lanes] = extra[taps_count : taps_count + 1, :inner]
+            gain_ref[:, lanes] = extra[6:7, :inner]
+            dt_sum = dt_sum + lanes_of(extra[6:7, inner : inner + LANES], rank)
+            alog_sum = alog_sum + lanes_of(extra[6:7, inner + LANES :], rank)
+            skip_sum = skip_sum + lanes_of(lanes_sum(extra[:, :inner], heads)[5:6], rank)
+        first_state = 2 * inner_all
+        in_ref[:, first_state : first_state + states] = b_sum
+        in_ref[:, first_state + states : first_state + 2 * states] = c_sum
+        in_ref[:, first_state + 2 * states :] = step_sum[:, : proj - first_state - 2 * states]
+        taps_ref[:, inner_all:] = shared[:taps_count, inner:]
+        bias_ref[:, inner_all:] = shared[taps_count : taps_count + 1, inner:]
+        pre_ref[:, :width] = shared[7:8]
+        pre_ref[:, width : 2 * width] = shared[8:9]
+        pre_ref[:, 2 * width :] = shared[5:6, inner : inner + model - 2 * width]
+        head_ref[0:1, :] = dt_sum
+        head_ref[1:2, :] = alog_sum
+        head_ref[2:3, :] = skip_sum
+
+    shapes = [(rows, proj), (rows, inner_all), taps_shape, (1, taps_shape[1]), (1, inner_all), (1, model), (8, LANES)]
+    return pl.pallas_call(
+        lambda ref, *refs: blocks(ref, refs[len(waits) :]),
+        in_specs=[pl.BlockSpec(owned.shape, lambda: (0, 0, 0))] + [pl.BlockSpec(memory_space=pl.ANY)] * len(waits),
+        out_shape=[jax.ShapeDtypeStruct(shape, jnp.float32) for shape in shapes],
+        compiler_params=pltpu.CompilerParams(vmem_limit_bytes=24 << 20),
+        cost_estimate=pl.CostEstimate(flops=int(3e9), bytes_accessed=1 << 20, transcendentals=0),
+    )(owned, *waits)
+
+
 def add_states(pieces, states, start):
-    rows, width = states.shape[0] // len(pieces), states.shape[1]
     count = len(pieces)
+    rows, width = states.shape[0] // count, states.shape[1]
 
     def run(*refs):
         for index in range(count):
@@ -648,10 +751,7 @@
         whole = whole.transpose(0, 2, 1, 3, 4).reshape(model, -1)
         return [whole[index * piece_rows : (index + 1) * piece_rows] for index in range(4)]
 
-    def scatter_rows(pieces, waits=()):
-        if direct:
-            moved = [cross(pieces[away], LINE, away, 4) for away in (2, 3, 1)]
-            return combine([pieces[0], *moved], LOW, waits)
+    def scatter_rows(pieces):
         whole = jnp.concatenate(pieces, axis=0).reshape(*natural, -1)
         whole = whole.transpose(0, 2, 1, 3, 4).reshape(model, -1)
         moved = lax.all_to_all(whole, LINE, split_axis=0, concat_axis=0, tiled=True)
@@ -691,7 +791,7 @@
     scale = lax.rsqrt(jnp.mean(stream * stream, axis=-1, keepdims=True) + EPSILON)
     valid = (jnp.arange(length) < lengths[0])[:, None]
     own_upstream = jnp.where(valid, cotangent, jnp.zeros_like(cotangent))
-    own_normed = copies(norm_kernel, (), hidden_in, (pre_gain[None],), 1)
+    own_normed = copies(norm_kernel, (), hidden_in, (pre_gain[None],), 1, (plane_weights,))
     normed = gather_tokens(own_normed)
     upstream = gather_tokens(copies(mask_kernel, (lengths,), cotangent, (), 1, (own_normed,)))
 
@@ -723,7 +823,7 @@
         [],
         12,
     )
-    gate, grad_mixed, gained, stats, gate_weights, out_weights = run_slots(
+    gate, grad_mixed, branch, stats, gate_weights = run_slots(
         gate_kernel,
         slots,
         place,
@@ -732,27 +832,16 @@
         [
             ((tokens, inner), jnp.float32, row_block(length, inner)),
             ((tokens, inner), jnp.float32, row_block(length, inner)),
-            ((tokens, inner), LOW, row_block(length, inner)),
+            ((tokens, model), LOW, row_block(length, model)),
             ((2 * slots, length), jnp.float32, whole_block((2 * slots, length))),
             ((model, inner), LOW, whole_block((model, inner))),
-            ((model, inner), LOW, whole_block((model, inner))),
         ],
-        [],
-        8,
+        [pltpu.VMEM((model, inner), LOW)],
+        14,
     )
     stats = stats + swap(stats)
     far = [cross(stats, ("xi", "yi"), away, 4) for away in (3, 1, 2)]
     stats = (stats + far[0]) + (far[1] + far[2])
-    (branch,) = run_slots(
-        branch_kernel,
-        slots,
-        place,
-        (gained,),
-        (out_weights,),
-        [((tokens, model), LOW, row_block(length, model))],
-        [],
-        5,
-    )
     branch_own = scatter_far(branch)
     squares = lax.dynamic_index_in_dim(stats, rank, axis=0, keepdims=False)
     inner_scale = lax.rsqrt(squares / inner_all + EPSILON)[:, None]
@@ -773,101 +862,71 @@
         + [(piece_shape, LOW, whole_block(piece_shape))] * 4,
         [pltpu.VMEM((model, 2 * inner), jnp.float32)],
         16,
-        (branch,),
-    )
-    piece_shape = (piece_rows, inner + states + LANES)
+    )
+    width = taps.shape[1]
+    piece_shape = (piece_rows + 32, inner + states + LANES)
     held = run_slots(
         functools.partial(back_kernel, heads),
         slots,
         place,
         (part, grad_scanned, scanned, grad_gate, normed),
-        (conv_weights, gate_weights, *params),
+        (conv_weights, gate_weights, *params, gain_grad),
         [
             ((tokens, model), LOW, row_block(length, model)),
-            ((8, part_width), jnp.float32, whole_block((8, part_width))),
-            ((8, model), jnp.float32, whole_block((8, model))),
             ((model, states), LOW, whole_block((model, states))),
         ]
         + [(piece_shape, LOW, whole_block(piece_shape))] * 4,
-        [pltpu.VMEM((model, part_width), jnp.float32), pltpu.VMEM((length, part_width), LOW)],
+        [
+            pltpu.VMEM((model, part_width), jnp.float32),
+            pltpu.VMEM((length, part_width), LOW),
+            pltpu.VMEM((8, part_width), jnp.float32),
+            pltpu.VMEM((8, model), jnp.float32),
+            pltpu.VMEM((16, width), jnp.float32),
+        ],
         40,
     )
     if direct:
         early_moved = [cross(early[away], LINE, away, 4) for away in (2, 3, 1)]
         held = hold(held, [*early_moved, branch_own])
-    grad_normed, small, pre_grad, given, *pieces = held
+    grad_normed, given, *pieces = held
     pieces = add_states(pieces, swap(given), inner)
+    if direct:
+        conv_moved = [cross(pieces[away], LINE, away, 4) for away in (1, 2, 3)]
+    else:
+        conv_moved = []
     grad_own = scatter_far(grad_normed) * pre_gain
     along = jnp.mean(grad_own * stream, axis=-1, keepdims=True)
     grad_stream = grad_own * scale - stream * (scale**3 * along)
     grad_hidden = (own_upstream.astype(jnp.float32) + grad_stream).astype(LOW)
 
-    def to_owners(value):
-        return exchange(value.astype(LOW).reshape(ranks, rows, -1)).astype(jnp.float32)
-
-    def all_columns(value):
-        return value.transpose(1, 0, 2).reshape(rows, -1)
-
-    early_sum = combine([early[0], *early_moved], LOW) if direct else scatter_rows(early)
-    owned_early = to_owners(early_sum)
-    conv_sum = scatter_rows(pieces)
-    owned_conv = to_owners(conv_sum)
-    owned_states = owned_conv[:, :, inner : inner + states].reshape(ranks // 2, 2, rows, states)
-    owned_in = jnp.concatenate(
-        [
-            all_columns(owned_early[:, :, :inner]),
-            all_columns(owned_conv[:, :, :inner]),
-            all_columns(jnp.sum(owned_states, axis=0)),
-            all_columns(owned_conv[:, :, inner + states : inner + states + heads]),
-        ],
-        axis=1,
-    )
-    owned_out = all_columns(owned_early[:, :, inner:])
-
-    def place_rank(value, total):
-        blank = jnp.zeros(value.shape[:-1] + (total,), jnp.float32)
-        return lax.dynamic_update_slice_in_dim(blank, value, rank * value.shape[-1], axis=-1)
-
-    taps_count = conv_weight.shape[0]
-    width = taps.shape[1]
-    conv_small = small[: taps_count + 1, :width]
-    conv_small = jnp.concatenate(
-        [place_rank(conv_small[:, :inner], inner_all), conv_small[:, inner:]], axis=1
-    )
-    head_small = jnp.stack(
-        [
-            small[5, width : width + heads],
-            small[6, width : width + heads],
-            jnp.sum(small[5, :inner].reshape(heads, head_width), axis=1),
-        ]
-    )
-    head_small = jnp.pad(place_rank(head_small, heads_all), ((0, 0), (0, LANES - heads_all)))
-    grads = (pre_grad[0] / pre_gain, conv_small, place_rank(gain_grad[0], inner_all), head_small)
-    flat = jnp.concatenate([grad.reshape(-1, LANES) for grad in grads], axis=0)
-    flat = combine([flat, swap(flat)], jnp.float32, (early_sum,))
-    flat = combine([flat, *(cross(flat, ("xi", "yi"), away, 4) for away in (3, 1, 2))], jnp.float32, (conv_sum,))
     if direct:
-        flat = combine([flat, *(cross(flat, LINE, away, 4) for away in (3, 1, 2))], jnp.float32)
+        early_terms, conv_terms = [early[0], *early_moved], [pieces[0], *conv_moved]
+        side = side_sums(early_terms, conv_terms, ranks)
     else:
-        flat = lax.psum(flat, LINE)
-    sums = []
-    start = 0
-    for grad in grads:
-        count = grad.size // LANES
-        sums.append(flat[start : start + count].reshape(grad.shape))
-        start += count
+        extra = small_rows(pieces[0][piece_rows:])
+        high, rest = parts_of(lax.psum(extra, LINE), 2)
+        side = jnp.concatenate([scatter_rows(early), scatter_rows([p[:piece_rows] for p in pieces])], axis=1)
+        below = jnp.pad(jnp.concatenate([high, rest], axis=1), ((0, 0), (0, side.shape[1] - 2 * width)))
+        below = jnp.broadcast_to(below[None], (ranks, *below.shape))
+        side = jnp.pad(side.reshape(ranks, rows, -1), ((0, 0), (0, -rows % 16), (0, 0)))
+        side = jnp.concatenate([side, below], axis=1)
+    owned = exchange(side)
+    sizes_out = (in_weight.shape[1], inner_all, conv_weight.shape, model)
+    owned_in, owned_out, taps_grad, bias_grad, gain_grads, pre_grad, head_grads = owner_outputs(
+        owned, rows + -rows % 16, heads, states, sizes_out, (grad_hidden, output)
+    )
     return (
         output,
         grad_hidden,
-        sums[0],
-        owned_in,
-        sums[1][:taps_count],
-        sums[1][taps_count],
-        sums[3][0, :heads_all],
-        sums[3][1, :heads_all],
-        sums[3][2, :heads_all],
-        sums[2],
-        owned_out,
+        pre_grad[0] / pre_gain,
+        owned_in[:rows],
+        taps_grad,
+        bias_grad[0],
+        head_grads[0, :heads_all],
+        head_grads[1, :heads_all],
+        head_grads[2, :heads_all],
+        gain_grads[0],
+        owned_out[:rows],
     )
 
 

time: 348 us -> 334 us (0.960)
  waiting for transfers between devices: 104 us -> 148 us
  blocking collectives: 27.9 us -> 0 us
  local copies, waits for them, and re-layouts: 44.1 us -> 34.8 us
  Pallas kernels: 110 us -> 101 us
  starting transfers between devices: 35.4 us -> 29.9 us
    all_to_all x2, waiting for transfers between devices: 0.01 us -> 29.5 us  [exchange(): return lax.all_to_all(value, PLANE, split_axis=0, concat_axis=0, tiled=True)]
    all_to_all x1 -> x0, blocking collectives: 27.9 us -> none  [exchange(): return lax.all_to_all(value, PLANE, split_axis=0, concat_axis=0, tiled=True)]
    ppermute x21 -> x15, waiting for transfers between devices: 101 us -> 115 us  [cross(): return lax.ppermute(value, axes, [(i, i ^ distance) for i in range(count)])]
    pallas_call x5 -> x2, Pallas kernels: 10.2 us -> 3.65 us  [the longest x1 1.94 us: side_sums(): pl.pallas_call(run, out_shape=jax.ShapeDtypeStruct(shape, LOW), compiler_...]
    reshape x9 -> x0, local copies, waits for them, and re-layouts: 4.98 us -> none  [the longest x2 2.61 us: body(): sums.append(flat[start:start + count].reshape(grad.shape))]
    ppermute x21 -> x15, starting transfers between devices: 26.8 us -> 22.1 us  [cross(): return lax.ppermute(value, axes, [(i, i ^ distance) for i in range(count)])]
    pallas_call x5 -> x4, Pallas kernels: 93.9 us -> 91.3 us  [run_slots(): pl.pallas_call(run, grid_spec=pltpu.PrefetchScalarGridSpec(num_scalar_pre...]
    unnamed x112 -> x83, local copies, waits for them, and re-layouts: 29.2 us -> 26.7 us
  transfers between devices with their start and end apart: 31 -> 24, of which waited for: 14 -> 15; matrix products, arithmetic and copies ran while one was open for 5% -> 2% of each run, Pallas kernels for 26% -> 25%
where the time goes in v3:
time: 334 us; the launch traced here: 333 us
  waiting for transfers between devices  148 us (44%)
  Pallas kernels  101 us (30%)
  local copies, waits for them, and re-layouts  34.8 us (10%)
  starting transfers between devices  29.9 us (9%)
  between operations  14.8 us (4%)
  other arithmetic  5.02 us (2%)
    ppermute x15, waiting for transfers between devices, cross(): return lax.ppermute(value, axes, [(i, i ^ distance) for i in range(count)])  115 us
    pallas_call x4, Pallas kernels, run_slots(): pl.pallas_call(run, grid_spec=pltpu.PrefetchScalarGridSpec(num_scalar_pre...  91.3 us
    all_to_all x2, waiting for transfers between devices, exchange(): return lax.all_to_all(value, PLANE, split_axis=0, concat_axis=0, tiled=True)  29.5 us
    unnamed x83, local copies, waits for them, and re-layouts  26.7 us
    ppermute x15, starting transfers between devices, cross(): return lax.ppermute(value, axes, [(i, i ^ distance) for i in range(count)])  22.1 us
    all_to_all x2, starting transfers between devices, exchange(): return lax.all_to_all(value, PLANE, split_axis=0, concat_axis=0, tiled=True)  7.3 us
  transfers between devices with their start and end apart: 24, of which 15 were waited for; matrix products, arithmetic and copies ran while one was open for 2% of the time, Pallas kernels for 25%

profile of v3, /device:TPU:16, one launch (start us, length us, event | category | flops | bytes accessed | tf_op | source)
XLA Modules:
  0.0 333.1 jit_solution(12686978250894416867)
XLA Ops:
  7.2 0.8 slice.52
  7.9 0.7 slice.51
  8.7 1.1 fusion.11
  10.1 0.7 fusion.9
  10.8 0.7 fusion.8
  11.6 0.7 fusion.7
  13.6 3.7 %all-to-all-start = ((bf16[8,48,1408]{2,1,0:T(8,128)(2,1)}), bf16[8,48,1408]{2,1,0:T(8,128)(2,1)S(1)}, u32[]{:S(2)}, u32[]{:S(2)}) async-start(bf16[8,48,1408]{2,1,0:T(8,128)(2,1)} %pad_dynamic-update-slice_fusion), calls=%async_computation | async-start | bytes 2162688 | tf_op jit(solution)/shard_map/all_to_all | solution.py:761
  17.4 14.7 %all-to-all-done = bf16[8,48,1408]{2,1,0:T(8,128)(2,1)S(1)} async-done(((bf16[8,48,1408]{2,1,0:T(8,128)(2,1)}), bf16[8,48,1408]{2,1,0:T(8,128)(2,1)S(1)}, u32[]{:S(2)}, u32[]{:S(2)}) %all-to-all-start) | async-done | bytes 1081376 | tf_op jit(solution)/shard_map/all_to_all | solution.py:761
  32.2 1.2 shard_map.203.refs_0_
  34.1 1.0 shard_map.204
  35.8 3.5 %collective-permute-start.1 = (bf16[384,640]{1,0:T(8,128)(2,1)S(1)}, bf16[384,640]{1,0:T(8,128)(2,1)}, u32[]{:S(2)}, u32[]{:S(2)}) collective-permute-start(bf16[384,640]{1,0:T(8,128)(2,1)S(1)} %slice.65.refs_1_), channel_id=1, source_target_pairs={{0,8},{4,12},{8,0},{12,4},{1,9},{5,13},{9,1},{13,5},{2,10},{6,14},... | collective-permute-start | bytes 1474568 | tf_op jit(solution)/shard_map/ppermute | solution.py:25
  39.5 0.8 dynamic_slice.27
  40.7 30.0 %collective-permute-done.2.refs_4_.refs_2_ = bf16[384,640]{1,0:T(8,128)(2,1)} collective-permute-done((bf16[384,640]{1,0:T(8,128)(2,1)S(1)}, bf16[384,640]{1,0:T(8,128)(2,1)}, u32[]{:S(2)}, u32[]{:S(2)}) %collective-permute-start.2) | collective-permute-done | bytes 491552 | tf_op jit(solution)/shard_map/ppermute | solution.py:25
  70.7 0.9 slice.69
  71.6 6.1 %collective-permute-done.1.refs_3_.refs_1_ = bf16[384,640]{1,0:T(8,128)(2,1)} collective-permute-done((bf16[384,640]{1,0:T(8,128)(2,1)S(1)}, bf16[384,640]{1,0:T(8,128)(2,1)}, u32[]{:S(2)}, u32[]{:S(2)}) %collective-permute-start.1) | collective-permute-done | bytes 491552 | tf_op jit(solution)/shard_map/ppermute | solution.py:25
  77.7 0.9 slice.68
  78.6 0.9 slice.67
  79.7 1.9 shard_map.206.refs_3_
  81.6 1.5 collective-permute-start.6
  83.2 4.4 %collective-permute-start.5 = (bf16[384,768]{1,0:T(8,128)(2,1)}, bf16[384,768]{1,0:T(8,128)(2,1)}, u32[]{:S(2)}, u32[]{:S(2)}) collective-permute-start(bf16[384,768]{1,0:T(8,128)(2,1)} %shard_map.206.refs_3_), channel_id=1, source_target_pairs={{0,8},{4,12},{8,0},{12,4},{1,9},{5,13},{9,1},{13,5},{2,10},{6,14},... | collective-permute-start | bytes 1769480 | tf_op jit(solution)/shard_map/ppermute | solution.py:25
  87.6 18.9 %shard_map.205 = (f32[2048,768]{1,0:T(8,128)}, f32[2048,384]{1,0:T(8,128)S(1)}, bf16[1536,768]{1,0:T(8,128)(2,1)S(1)}) custom-call(s32[9]{0:T(128)S(1)} %stack.39.place_ref, bf16[2048,1536]{1,0:T(8,128)(2,1)} %all-gather.3.cloned.1.call-done.refs_0_.refs_4_, bf16[384,640]{1,0:T(8,128)(2,1)S(1)} %slice.65.refs_1_, ...), custom_call_target="tpu_custom_call" | custom-call | flops 12000000000 | bytes 1048576 | tf_op jit(solution)/shard_map/pallas_call | solution.py:515
  106.5 1.6 copy-done.22
  108.1 1.5 copy-done.27
  109.6 13.7 %collective-permute-done.6.refs_6_ = bf16[384,768]{1,0:T(8,128)(2,1)} collective-permute-done((bf16[384,768]{1,0:T(8,128)(2,1)}, bf16[384,768]{1,0:T(8,128)(2,1)}, u32[]{:S(2)}, u32[]{:S(2)}) %collective-permute-start.6) | collective-permute-done | bytes 589856 | tf_op jit(solution)/shard_map/ppermute | solution.py:25
  123.3 11.3 %collective-permute-done.5.refs_5_ = bf16[384,768]{1,0:T(8,128)(2,1)} collective-permute-done((bf16[384,768]{1,0:T(8,128)(2,1)}, bf16[384,768]{1,0:T(8,128)(2,1)}, u32[]{:S(2)}, u32[]{:S(2)}) %collective-permute-start.5) | collective-permute-done | bytes 589856 | tf_op jit(solution)/shard_map/ppermute | solution.py:25
  134.6 16.4 %shard_map.207 = (f32[2048,384]{1,0:T(8,128)S(1)}, f32[2048,384]{1,0:T(8,128)S(1)}, bf16[2048,1536]{1,0:T(8,128)(2,1)}, f32[16,256]{1,0:T(8,128)S(1)}, bf16[1536,384]{1,0:T(8,128)(2,1)S(1)}) custom-call(s32[9]{0:T(128)S(1)} %stack.39.place_ref, bf16[2048,1536]{1,0:T(8,128)(2,1)} %all-gather.3.cloned.1.call-done.refs_0_.refs_4_, ...), custom_call_target="tpu_custom_call" | custom-call | flops 14000000000 | bytes 1048576 | tf_op jit(solution)/shard_map/pallas_call | solution.py:515
  151.1 1.6 copy-done.24
  152.7 1.6 copy-done.25
  154.4 1.0 copy-done.29
  155.7 1.2 collective-permute-done.7
  157.6 1.3 collective-permute-start.9
  158.9 1.5 collective-permute-start.8
  161.3 2.2 collective-permute-done.8
  163.5 2.5 copy-done.23
  166.0 15.9 %shard_map.208 = (bf16[2048,384]{1,0:T(8,128)(2,1)S(1)}, f32[2048,384]{1,0:T(8,128)S(1)}, f32[8,384]{1,0:T(8,128)S(1)}, bf16[384,768]{1,0:T(8,128)(2,1)S(1)}, bf...) custom-call(s32[9]{0:T(128)S(1)} %stack.39.place_ref, ...), custom_call_target="tpu_custom_call" | custom-call | flops 16000000000 | bytes 1048576 | tf_op jit(solution)/shard_map/pallas_call | solution.py:515
  182.0 1.6 copy-done.26
  183.6 3.7 %collective-permute-start.11 = (bf16[384,768]{1,0:T(8,128)(2,1)S(1)}, bf16[384,768]{1,0:T(8,128)(2,1)S(1)}, u32[]{:S(2)}, u32[]{:S(2)}) collective-permute-start(bf16[384,768]{1,0:T(8,128)(2,1)S(1)} %get-tuple-element.66), channel_id=1, source_target_pairs={{0,8},{4,12},{8,0},{12,4},{1,9},{5,13},{9,1},{13,5},{2,10},{6,14},... | collective-permute-start | bytes 1769480 | tf_op jit(solution)/shard_map/ppermute | solution.py:25
  187.8 1.0 collective-permute-start.13
  188.8 40.0 %shard_map.209 = (bf16[2048,1536]{1,0:T(8,128)(2,1)}, bf16[1536,128]{1,0:T(8,128)(2,1)S(1)}, bf16[416,640]{1,0:T(8,128)(2,1)S(1)}, bf16[416,640]{1,0:T(8,128)(2,...) custom-call(s32[9]{0:T(128)S(1)} %stack.39.place_ref, f32[2048,768]{1,0:T(8,128)} %get-tuple-element.52.refs_0_, ...), custom_call_target="tpu_custom_call" | custom-call | flops 40000000000 | bytes 1048576 | tf_op jit(solution)/shard_map/pallas_call | solution.py:515
  228.8 0.8 copy-done.12
  229.6 0.8 copy-done.14
  230.4 0.8 copy-done.15
  231.2 0.8 copy-done.16
  232.7 4.2 %collective-permute-done.12.refs_7_.refs_2_ = bf16[384,768]{1,0:T(8,128)(2,1)S(1)} collective-permute-done((bf16[384,768]{1,0:T(8,128)(2,1)S(1)}, bf16[384,768]{1,0:T(8,128)(2,1)S(1)}, u32[]{:S(2)}, u32[]{:S(2)}) %collective-permute-start.12) | collective-permute-done | bytes 589856 | tf_op jit(solution)/shard_map/ppermute | solution.py:25
  237.0 0.8 copy-done.8
  238.0 1.0 copy-done.18
  239.0 1.7 collective-permute-done.14.refs_4_
  241.4 2.1 shard_map.211
  243.5 1.7 collective-permute-start.16
  245.3 1.7 collective-permute-start.17
  247.0 18.8 %collective-permute-done.15.refs_5_ = bf16[416,640]{1,0:T(8,128)(2,1)} collective-permute-done((bf16[416,640]{1,0:T(8,128)(2,1)}, bf16[416,640]{1,0:T(8,128)(2,1)}, u32[]{:S(2)}, u32[]{:S(2)}) %collective-permute-start.15) | collective-permute-done | bytes 532512 | tf_op jit(solution)/shard_map/ppermute | solution.py:25
  265.8 15.1 %collective-permute-done.16.refs_6_ = bf16[416,640]{1,0:T(8,128)(2,1)} collective-permute-done((bf16[416,640]{1,0:T(8,128)(2,1)}, bf16[416,640]{1,0:T(8,128)(2,1)}, u32[]{:S(2)}, u32[]{:S(2)}) %collective-permute-start.16) | collective-permute-done | bytes 532512 | tf_op jit(solution)/shard_map/ppermute | solution.py:25
  280.9 12.5 %collective-permute-done.17.refs_7_ = bf16[416,640]{1,0:T(8,128)(2,1)} collective-permute-done((bf16[416,640]{1,0:T(8,128)(2,1)}, bf16[416,640]{1,0:T(8,128)(2,1)}, u32[]{:S(2)}, u32[]{:S(2)}) %collective-permute-start.17) | collective-permute-done | bytes 532512 | tf_op jit(solution)/shard_map/ppermute | solution.py:25
  293.5 1.0 copy-done.13
  294.5 1.1 copy-done.21
  295.6 1.9 shard_map.212
  297.5 1.1 copy-done.2
  298.7 3.6 %all-to-all-start.1 = ((bf16[8,64,1408]{2,1,0:T(8,128)(2,1)}), bf16[8,64,1408]{2,1,0:T(8,128)(2,1)S(1)}, u32[]{:S(2)}, u32[]{:S(2)}) async-start(bf16[8,64,1408]{2,1,0:T(8,128)(2,1)} %copy-done.2), calls=%async_computation.3 | async-start | bytes 2883584 | tf_op jit(solution)/shard_map/all_to_all | solution.py:761
  302.3 1.7 fusion.2
  304.0 2.0 fusion.6
  306.0 14.8 %all-to-all-done.1.ref = bf16[8,64,1408]{2,1,0:T(8,128)(2,1)S(1)} async-done(((bf16[8,64,1408]{2,1,0:T(8,128)(2,1)}), bf16[8,64,1408]{2,1,0:T(8,128)(2,1)S(1)}, u32[]{:S(2)}, u32[]{:S(2)}) %all-to-all-start.1) | async-done | bytes 1441824 | tf_op jit(solution)/shard_map/all_to_all | solution.py:761
  320.8 1.1 copy-done.4
  322.0 1.1 copy-done.5
  323.1 1.7 shard_map.213
  (131 shorter events, 9.1 us)
Async XLA Ops:
  7.2 3.6 %copy-start.33 = (bf16[48,3072]{1,0:T(8,128)(2,1)S(1)}, bf16[48,3072]{1,0:T(8,128)(2,1)}, u32[]{:S(2)}) copy-start(bf16[48,3072]{1,0:T(8,128)(2,1)} %param.23) | copy-start | bytes 884740
  11.6 5.8 %copy-start.34 = (f32[1536]{0:T(1024)S(1)}, f32[1536]{0:T(1024)}, u32[]{:S(2)}) copy-start(f32[1536]{0:T(1024)} %param.15) | copy-start | bytes 18436
  11.6 20.6 %copy-start = (bf16[256,1536]{1,0:T(8,128)(2,1)S(1)}, bf16[256,1536]{1,0:T(8,128)(2,1)}, u32[]{:S(2)}) copy-start(bf16[256,1536]{1,0:T(8,128)(2,1)} %hidden_ref.1) | copy-start | bytes 2359300
  13.6 18.5 %all-to-all-start = ((bf16[8,48,1408]{2,1,0:T(8,128)(2,1)}), bf16[8,48,1408]{2,1,0:T(8,128)(2,1)S(1)}, u32[]{:S(2)}, u32[]{:S(2)}) async-start(bf16[8,48,1408]{2,1,0:T(8,128)(2,1)} %pad_dynamic-update-slice_fusion), calls=%async_computation | async-start | bytes 2162688 | tf_op jit(solution)/shard_map/all_to_all | solution.py:761
  17.4 70.2 %all-gather.3.cloned.1.call-start = ((), (), s32[]{:S(2)}) async-start(), calls=%async_computation.4 | async-start | bytes 7077888 | tf_op jit(solution)/shard_map/all_gather | solution.py:764
  32.2 8.5 %copy-start.1 = (bf16[8,48,1408]{2,1,0:T(8,128)(2,1)}, bf16[8,48,1408]{2,1,0:T(8,128)(2,1)S(1)}, u32[]{:S(2)}) copy-start(bf16[8,48,1408]{2,1,0:T(8,128)(2,1)S(1)} %all-to-all-done) | copy-start | bytes 3244036
  32.2 1.9 copy-start.3
  33.4 101.2 %all-gather.5.cloned.1.call-start = ((), (), s32[]{:S(2)}) async-start(), calls=%async_computation.5 | async-start | bytes 7077888 | tf_op jit(solution)/shard_map/all_gather | solution.py:764
  35.1 4.2 %copy-start.36 = (f32[48]{0:T(128)S(1)}, f32[48]{0:T(128)}, u32[]{:S(2)}) copy-start(f32[48]{0:T(128)} %param.19) | copy-start | bytes 580
  35.1 4.3 %copy-start.37 = (f32[48]{0:T(128)S(1)}, f32[48]{0:T(128)}, u32[]{:S(2)}) copy-start(f32[48]{0:T(128)} %param.20) | copy-start | bytes 580
  35.1 4.3 %copy-start.38 = (f32[48]{0:T(128)S(1)}, f32[48]{0:T(128)}, u32[]{:S(2)}) copy-start(f32[48]{0:T(128)} %param.21) | copy-start | bytes 580
  35.1 5.3 %slice-start.3 = ((f32[3328]{0:T(1024)}), f32[3072]{0:T(1024)S(1)}, s32[]{:S(2)}) async-start(f32[3328]{0:T(1024)} %param.18), calls=%async_computation.11 | async-start | bytes 24576 | tf_op jit(solution)/shard_map/slice | solution.py:804
  35.1 5.4 %slice-start.2 = ((f32[3328]{0:T(1024)}), f32[256]{0:T(256)S(1)}, s32[]{:S(2)}) async-start(f32[3328]{0:T(1024)} %param.18), calls=%async_computation.10 | async-start | bytes 2048 | tf_op jit(solution)/shard_map/slice | solution.py:804
  35.2 44.5 %slice-start.1 = ((f32[4,3328]{1,0:T(4,128)}), f32[4,3072]{1,0:T(4,128)S(1)}, s32[]{:S(2)}) async-start(f32[4,3328]{1,0:T(4,128)} %param.17), calls=%async_computation.9 | async-start | bytes 98304 | tf_op jit(solution)/shard_map/slice | solution.py:802
  35.2 44.5 %slice-start = ((f32[4,3328]{1,0:T(4,128)}), f32[4,256]{1,0:T(4,128)S(1)}, s32[]{:S(2)}) async-start(f32[4,3328]{1,0:T(4,128)} %param.17), calls=%async_computation.8 | async-start | bytes 8192 | tf_op jit(solution)/shard_map/slice | solution.py:802
  35.2 201.8 %reduce-scatter.3.cloned.1.call-start = ((), (), s32[]{:S(2)}) async-start(), calls=%async_computation.6 | async-start | bytes 7077888 | tf_op jit(solution)/shard_map/reduce_scatter | solution.py:767
  35.3 35.4 %collective-permute-start.2 = (bf16[384,640]{1,0:T(8,128)(2,1)S(1)}, bf16[384,640]{1,0:T(8,128)(2,1)}, u32[]{:S(2)}, u32[]{:S(2)}) collective-permute-start(bf16[384,640]{1,0:T(8,128)(2,1)S(1)} %slice.65.refs_1_), channel_id=1, source_target_pairs={{0,12},{4,8},{8,4},{12,0},{1,13},{5,9},{9,5},{13,1},{2,14},{6,10},... | collective-permute-start | bytes 1474568 | tf_op jit(solution)/shard_map/ppermute | solution.py:25
  35.8 41.9 %collective-permute-start.1 = (bf16[384,640]{1,0:T(8,128)(2,1)S(1)}, bf16[384,640]{1,0:T(8,128)(2,1)}, u32[]{:S(2)}, u32[]{:S(2)}) collective-permute-start(bf16[384,640]{1,0:T(8,128)(2,1)S(1)} %slice.65.refs_1_), channel_id=1, source_target_pairs={{0,8},{4,12},{8,0},{12,4},{1,9},{5,13},{9,1},{13,5},{2,10},{6,14},... | collective-permute-start | bytes 1474568 | tf_op jit(solution)/shard_map/ppermute | solution.py:25
  39.3 39.3 %collective-permute-start = (bf16[384,640]{1,0:T(8,128)(2,1)S(1)}, bf16[384,640]{1,0:T(8,128)(2,1)}, u32[]{:S(2)}, u32[]{:S(2)}) collective-permute-start(bf16[384,640]{1,0:T(8,128)(2,1)S(1)} %slice.65.refs_1_), channel_id=1, source_target_pairs={{0,4},{4,0},{8,12},{12,8},{1,5},{5,1},{9,13},{13,9},{2,6},{6,2},{1... | collective-permute-start | bytes 1474568 | tf_op jit(solution)/shard_map/ppermute | solution.py:25
  79.6 8.0 %collective-permute-start.3 = (bf16[1536,128]{1,0:T(8,128)(2,1)S(1)}, bf16[1536,128]{1,0:T(8,128)(2,1)S(1)}, u32[]{:S(2)}, u32[]{:S(2)}) collective-permute-start(bf16[1536,128]{1,0:T(8,128)(2,1)S(1)} %pad_maximum_fusion), channel_id=1, source_target_pairs={{0,1},{1,0},{2,3},{3,2},{4,5},{5,4},{6,7},{7,6},{8,9},{9,8},{10,11... | collective-permute-start | bytes 1179656 | tf_op jit(solution)/shard_map/ppermute | solution.py:21
  81.6 41.7 %collective-permute-start.6 = (bf16[384,768]{1,0:T(8,128)(2,1)}, bf16[384,768]{1,0:T(8,128)(2,1)}, u32[]{:S(2)}, u32[]{:S(2)}) collective-permute-start(bf16[384,768]{1,0:T(8,128)(2,1)} %shard_map.206.refs_3_), channel_id=1, source_target_pairs={{0,12},{4,8},{8,4},{12,0},{1,13},{5,9},{9,5},{13,1},{2,14},{6,10},... | collective-permute-start | bytes 1769480 | tf_op jit(solution)/shard_map/ppermute | solution.py:25
  83.2 51.5 %collective-permute-start.5 = (bf16[384,768]{1,0:T(8,128)(2,1)}, bf16[384,768]{1,0:T(8,128)(2,1)}, u32[]{:S(2)}, u32[]{:S(2)}) collective-permute-start(bf16[384,768]{1,0:T(8,128)(2,1)} %shard_map.206.refs_3_), channel_id=1, source_target_pairs={{0,8},{4,12},{8,0},{12,4},{1,9},{5,13},{9,1},{13,5},{2,10},{6,14},... | collective-permute-start | bytes 1769480 | tf_op jit(solution)/shard_map/ppermute | solution.py:25
  87.6 47.1 %collective-permute-start.4 = (bf16[384,768]{1,0:T(8,128)(2,1)}, bf16[384,768]{1,0:T(8,128)(2,1)}, u32[]{:S(2)}, u32[]{:S(2)}) collective-permute-start(bf16[384,768]{1,0:T(8,128)(2,1)} %shard_map.206.refs_3_), channel_id=1, source_target_pairs={{0,4},{4,0},{8,12},{12,8},{1,5},{5,1},{9,13},{13,9},{2,6},{6,2},{1... | collective-permute-start | bytes 1769480 | tf_op jit(solution)/shard_map/ppermute | solution.py:25
  87.6 47.1 %copy-start.19 = (bf16[384,768]{1,0:T(8,128)(2,1)S(1)}, bf16[384,768]{1,0:T(8,128)(2,1)}, u32[]{:S(2)}) copy-start(bf16[384,768]{1,0:T(8,128)(2,1)} %shard_map.206.refs_3_) | copy-start | bytes 1769476
  106.5 1.6 copy-start.22
  108.1 1.5 copy-start.27
  151.1 1.6 copy-start.24
  152.7 1.6 copy-start.25
  154.4 1.0 copy-start.29
  155.4 146.9 %reduce-scatter.5.cloned.1.call-start = ((), (), s32[]{:S(2)}) async-start(), calls=%async_computation.7 | async-start | bytes 7077888 | tf_op jit(solution)/shard_map/reduce_scatter | solution.py:767
  155.6 1.2 collective-permute-start.7
  156.9 3.7 %collective-permute-start.10 = (f32[16,256]{1,0:T(8,128)S(1)}, f32[16,256]{1,0:T(8,128)S(1)}, u32[]{:S(2)}, u32[]{:S(2)}) collective-permute-start(f32[16,256]{1,0:T(8,128)S(1)} %add.93), channel_id=1, source_target_pairs={{0,16},{2,18},{16,0},{18,2},{1,17},{3,19},{17,1},{19,3},{4,20},{6,... | collective-permute-start | bytes 49160 | tf_op jit(solution)/shard_map/ppermute | solution.py:25
  157.6 3.7 %collective-permute-start.9 = (f32[16,256]{1,0:T(8,128)S(1)}, f32[16,256]{1,0:T(8,128)S(1)}, u32[]{:S(2)}, u32[]{:S(2)}) collective-permute-start(f32[16,256]{1,0:T(8,128)S(1)} %add.93), channel_id=1, source_target_pairs={{0,2},{2,0},{16,18},{18,16},{1,3},{3,1},{17,19},{19,17},{4,6},{6,4... | collective-permute-start | bytes 49160 | tf_op jit(solution)/shard_map/ppermute | solution.py:25
  158.9 4.6 %collective-permute-start.8 = (f32[16,256]{1,0:T(8,128)S(1)}, f32[16,256]{1,0:T(8,128)S(1)}, u32[]{:S(2)}, u32[]{:S(2)}) collective-permute-start(f32[16,256]{1,0:T(8,128)S(1)} %add.93), channel_id=1, source_target_pairs={{0,18},{2,16},{16,2},{18,0},{1,19},{3,17},{17,3},{19,1},{4,22},{6,... | collective-permute-start | bytes 49160 | tf_op jit(solution)/shard_map/ppermute | solution.py:25
  163.5 2.5 copy-start.23
  166.0 22.8 %copy-start.28 = (bf16[1536,768]{1,0:T(8,128)(2,1)S(1)}, bf16[1536,768]{1,0:T(8,128)(2,1)}, u32[]{:S(2)}) copy-start(bf16[1536,768]{1,0:T(8,128)(2,1)} %copy-done.27) | copy-start | bytes 7077892
  166.0 22.8 %copy-start.30 = (bf16[1536,384]{1,0:T(8,128)(2,1)S(1)}, bf16[1536,384]{1,0:T(8,128)(2,1)}, u32[]{:S(2)}) copy-start(bf16[1536,384]{1,0:T(8,128)(2,1)} %copy-done.29) | copy-start | bytes 3538948
  181.9 1.6 copy-start.26
  183.6 45.2 %copy-start.20 = (bf16[384,768]{1,0:T(8,128)(2,1)}, bf16[384,768]{1,0:T(8,128)(2,1)S(1)}, u32[]{:S(2)}) copy-start(bf16[384,768]{1,0:T(8,128)(2,1)S(1)} %get-tuple-element.70.refs_0_) | copy-start | bytes 1769476
  183.6 49.1 %collective-permute-start.11 = (bf16[384,768]{1,0:T(8,128)(2,1)S(1)}, bf16[384,768]{1,0:T(8,128)(2,1)S(1)}, u32[]{:S(2)}, u32[]{:S(2)}) collective-permute-start(bf16[384,768]{1,0:T(8,128)(2,1)S(1)} %get-tuple-element.66), channel_id=1, source_target_pairs={{0,8},{4,12},{8,0},{12,4},{1,9},{5,13},{9,1},{13,5},{2,10},{6,14},... | collective-permute-start | bytes 1769480 | tf_op jit(solution)/shard_map/ppermute | solution.py:25
  187.3 49.7 %collective-permute-start.12 = (bf16[384,768]{1,0:T(8,128)(2,1)S(1)}, bf16[384,768]{1,0:T(8,128)(2,1)S(1)}, u32[]{:S(2)}, u32[]{:S(2)}) collective-permute-start(bf16[384,768]{1,0:T(8,128)(2,1)S(1)} %get-tuple-element.67), channel_id=1, source_target_pairs={{0,12},{4,8},{8,4},{12,0},{1,13},{5,9},{9,5},{13,1},{2,14},{6,10},... | collective-permute-start | bytes 1769480 | tf_op jit(solution)/shard_map/ppermute | solution.py:25
  187.8 49.2 %collective-permute-start.13 = (bf16[384,768]{1,0:T(8,128)(2,1)S(1)}, bf16[384,768]{1,0:T(8,128)(2,1)S(1)}, u32[]{:S(2)}, u32[]{:S(2)}) collective-permute-start(bf16[384,768]{1,0:T(8,128)(2,1)S(1)} %get-tuple-element.68), channel_id=1, source_target_pairs={{0,4},{4,0},{8,12},{12,8},{1,5},{5,1},{9,13},{13,9},{2,6},{6,2},{1... | collective-permute-start | bytes 1769480 | tf_op jit(solution)/shard_map/ppermute | solution.py:25
  228.8 0.8 copy-start.12
  229.6 0.8 copy-start.14
  230.4 0.8 copy-start.15
  232.7 4.2 %copy-start.6 = (bf16[384,768]{1,0:T(8,128)(2,1)}, bf16[384,768]{1,0:T(8,128)(2,1)S(1)}, u32[]{:S(2)}) copy-start(bf16[384,768]{1,0:T(8,128)(2,1)S(1)} %collective-permute-done.11.refs_6_.refs_1_) | copy-start | bytes 1769476
  237.0 0.8 copy-start.8
  237.0 1.0 copy-start.10
  238.0 1.0 copy-start.18
  239.0 1.7 collective-permute-start.14
  241.4 52.0 %copy-start.7 = (bf16[384,768]{1,0:T(8,128)(2,1)S(1)}, bf16[384,768]{1,0:T(8,128)(2,1)}, u32[]{:S(2)}) copy-start(bf16[384,768]{1,0:T(8,128)(2,1)} %copy-done.6) | copy-start | bytes 1769476
  241.4 52.0 %copy-start.9 = (bf16[384,768]{1,0:T(8,128)(2,1)S(1)}, bf16[384,768]{1,0:T(8,128)(2,1)}, u32[]{:S(2)}) copy-start(bf16[384,768]{1,0:T(8,128)(2,1)} %copy-done.8) | copy-start | bytes 1769476
  241.4 52.0 %copy-start.11 = (bf16[384,768]{1,0:T(8,128)(2,1)S(1)}, bf16[384,768]{1,0:T(8,128)(2,1)}, u32[]{:S(2)}) copy-start(bf16[384,768]{1,0:T(8,128)(2,1)} %copy-done.10) | copy-start | bytes 1769476
  243.5 22.3 %collective-permute-start.15 = (bf16[416,640]{1,0:T(8,128)(2,1)}, bf16[416,640]{1,0:T(8,128)(2,1)}, u32[]{:S(2)}, u32[]{:S(2)}) collective-permute-start(bf16[416,640]{1,0:T(8,128)(2,1)} %get-tuple-element.77), channel_id=1, source_target_pairs={{0,4},{4,0},{8,12},{12,8},{1,5},{5,1},{9,13},{13,9},{2,6},{6,2},{1... | collective-permute-start | bytes 1597448 | tf_op jit(solution)/shard_map/ppermute | solution.py:25
  243.5 37.4 %collective-permute-start.16 = (bf16[416,640]{1,0:T(8,128)(2,1)}, bf16[416,640]{1,0:T(8,128)(2,1)}, u32[]{:S(2)}, u32[]{:S(2)}) collective-permute-start(bf16[416,640]{1,0:T(8,128)(2,1)} %get-tuple-element.78), channel_id=1, source_target_pairs={{0,8},{4,12},{8,0},{12,4},{1,9},{5,13},{9,1},{13,5},{2,10},{6,14},... | collective-permute-start | bytes 1597448 | tf_op jit(solution)/shard_map/ppermute | solution.py:25
  245.3 48.2 %collective-permute-start.17 = (bf16[416,640]{1,0:T(8,128)(2,1)}, bf16[416,640]{1,0:T(8,128)(2,1)}, u32[]{:S(2)}, u32[]{:S(2)}) collective-permute-start(bf16[416,640]{1,0:T(8,128)(2,1)} %get-tuple-element.79), channel_id=1, source_target_pairs={{0,12},{4,8},{8,4},{12,0},{1,13},{5,9},{9,5},{13,1},{2,14},{6,10},... | collective-permute-start | bytes 1597448 | tf_op jit(solution)/shard_map/ppermute | solution.py:25
  293.5 1.0 copy-start.13
  294.5 1.1 copy-start.21
  297.5 1.1 copy-start.2
  298.7 22.2 %all-to-all-start.1 = ((bf16[8,64,1408]{2,1,0:T(8,128)(2,1)}), bf16[8,64,1408]{2,1,0:T(8,128)(2,1)S(1)}, u32[]{:S(2)}, u32[]{:S(2)}) async-start(bf16[8,64,1408]{2,1,0:T(8,128)(2,1)} %copy-done.2), calls=%async_computation.3 | async-start | bytes 2883584 | tf_op jit(solution)/shard_map/all_to_all | solution.py:761
  302.3 1.7 copy-start.31
  302.3 1.7 copy-start.32
  320.8 1.1 copy-start.4
  322.0 1.1 copy-start.5
  (3 other events, 2.3 us)
Sparse Core Ops, SparseCore 0:
  33.5 45.6 all-gather.2
  81.6 45.5 all-gather.4
  155.5 62.6 reduce-scatter.2
  238.1 60.8 reduce-scatter.4

commit v4 on v3

--- a/solution.py
+++ b/solution.py
@@ -11,6 +11,7 @@
 EPSILON = 1e-05
 LANES = 128
 LOW = jnp.bfloat16
+LOG2E = 1.4426950408889634
 
 PLANE = ("xi", "yi", "c")
 LINE = ("xo", "zo")
@@ -91,8 +92,14 @@
     inner = value.shape[1]
     lane = lax.broadcasted_iota(jnp.int32, (inner, LANES), 0)
     head = lax.broadcasted_iota(jnp.int32, (inner, LANES), 1)
-    member = (lane // (inner // head_count) == head).astype(LOW)
+    start = head * (inner // head_count)
+    member = jnp.logical_and(lane >= start, lane < start + inner // head_count).astype(LOW)
     return sum(dot_low(term, member) for term in parts_of(value, 2))
+
+
+def turned_columns(rows):
+    blank = jnp.zeros((LANES - rows.shape[0], rows.shape[1]), rows.dtype)
+    return jnp.concatenate([rows, blank], axis=0).T
 
 
 def read(ref):
@@ -114,7 +121,7 @@
     conv_low = jax.nn.silu(convolve(part[:, :width], taps_ref[...], bias_ref[...])).astype(LOW)
     step = softplus(part[:, width:] + dt_ref[...])
     lower = triangle(length, True)
-    cumulative = cumulate(lower, step * -jnp.exp(alog_ref[...]), 3)
+    cumulative = cumulate(lower, step * (-jnp.exp(alog_ref[...]) * LOG2E), 3)
     across = cumulative.T
     scores = dot_nt(conv_low[:, inner + states :], conv_low[:, inner : inner + states])
     scores = jnp.where(lower, scores, 0.0)
@@ -126,7 +133,7 @@
         sums = []
         for head in (2 * pair, 2 * pair + 1):
             spread = cumulative[:, head : head + 1] - across[head : head + 1, :]
-            mixing = scores * jnp.exp(jnp.where(lower, spread, 0.0))
+            mixing = scores * jnp.exp2(jnp.minimum(spread, 0.0))
             sums.append(dot_low(mixing.astype(LOW), scaled))
         out_ref[:, lanes] = jnp.where(first, sums[0], sums[1]) + skip_ref[:, lanes] * values
 
@@ -167,12 +174,13 @@
 ):
     inner = scanned_ref.shape[1]
     states = other_ref.shape[1]
-    chunk = piece_0.shape[0] // 2
+    chunk = weight_ref.shape[0] // 8
 
     @pl.when(pl.program_id(0) == 0)
     def _():
         core = place_ref[8]
         for away, piece in enumerate((piece_0, piece_1, piece_2, piece_3)):
+            steps = turned_columns(piece[2 * chunk :, : 2 * chunk].astype(jnp.float32)).astype(LOW)
             for half in range(2):
                 rows = pl.ds(pl.multiple_of(place_ref[2 * away + half], 16), chunk)
                 local = slice(half * chunk, (half + 1) * chunk)
@@ -181,7 +189,7 @@
                 weight_ref[rows, :inner] = piece[local, :inner]
                 weight_ref[rows, inner : inner + states] = jnp.where(core == 0, own, other)
                 weight_ref[rows, inner + states : inner + 2 * states] = jnp.where(core == 0, other, own)
-                weight_ref[rows, inner + 2 * states :] = piece[local, inner + states :]
+                weight_ref[rows, inner + 2 * states :] = steps[local]
 
     part = dot_low(read(normed_ref), weight_ref[...])
     part_ref[...] = part
@@ -189,6 +197,8 @@
 
 
 def scan_backward(
+    counts,
+    beside,
     heads,
     part_ref,
     grad_ref,
@@ -215,7 +225,7 @@
     step = softplus(raw)
     decay = -jnp.exp(alog_ref[...])
     lower = triangle(length, True)
-    cumulative = cumulate(lower, step * decay, 3)
+    cumulative = cumulate(lower, step * (decay * LOG2E), 3)
     across = cumulative.T
     b_rows = conv_low[:, inner : inner + states]
     c_rows = conv_low[:, inner + states :]
@@ -236,10 +246,11 @@
         sums = []
         for head in (2 * pair, 2 * pair + 1):
             spread = cumulative[:, head : head + 1] - across[head : head + 1, :]
-            decays = jnp.where(lower, jnp.exp(jnp.where(lower, spread, 0.0)), 0.0)
+            decays = jnp.exp2(jnp.minimum(spread, 0.0))
             mixing = (scores * decays).astype(LOW)
             own = first if head % 2 == 0 else jnp.logical_not(first)
             grad_own = jnp.where(own, grad[:, lanes], 0.0).astype(LOW)
+            beside(head)
             grad_scores = grad_scores + dot_nt(grad_own, scaled[:, lanes]) * decays
             sums.append(dot_low(grad_across[lanes], mixing))
         moved.append(jnp.where(upper_rows, sums[0], sums[1]).T)
@@ -252,7 +263,7 @@
     grad_step = grad_rate * decay + lanes_sum(values * grad_scaled, heads)
     grad_raw = grad_step * jax.nn.sigmoid(raw)
     grad_values = steps * grad_scaled + skip_ref[...] * grad
-    scores_low = grad_scores.astype(LOW)
+    scores_low = jnp.where(lower, grad_scores, 0.0).astype(LOW)
     grad_c = dot_low(scores_low, b_rows)
     grad_b = dot_low(c_rows.T, scores_low).T
     grad_summed = jnp.concatenate([grad_values, grad_b, grad_c], axis=1) * slope
@@ -260,17 +271,21 @@
     rows = []
     for tap in range(kernel_taps):
         away = kernel_taps - 1 - tap
-        grad_input = grad_input + taps_ref[tap : tap + 1, :] * shift_up(grad_summed, away)
-        rows.append(jnp.sum(grad_summed * shift_down(conv_input, away), axis=0, keepdims=True))
+        shifted = shift_up(grad_summed, away)
+        grad_input = grad_input + taps_ref[tap : tap + 1, :] * shifted
+        rows.append(jnp.sum(shifted * conv_input, axis=0, keepdims=True))
     rows.append(jnp.sum(grad_summed, axis=0, keepdims=True))
     out_ref[:, :width] = grad_input.astype(LOW)
     out_ref[:, width:] = grad_raw.astype(LOW)
 
+    def counted(row):
+        return jnp.where(counts, row, 0.0)
+
     for index, row in enumerate(rows):
-        small_ref[index : index + 1, :width] += row
-    small_ref[5:6, :inner] += jnp.sum(grad * values, axis=0, keepdims=True)
-    small_ref[5:6, width:] += jnp.sum(grad_raw, axis=0, keepdims=True)
-    small_ref[6:7, width:] += jnp.sum(grad_rate * step, axis=0, keepdims=True) * decay
+        small_ref[index : index + 1, :width] += counted(row)
+    small_ref[5:6, :inner] += counted(jnp.sum(grad * values, axis=0, keepdims=True))
+    small_ref[5:6, width:] += counted(jnp.sum(grad_raw, axis=0, keepdims=True))
+    small_ref[6:7, width:] += counted(jnp.sum(grad_rate * step, axis=0, keepdims=True) * decay)
 
 
 def gate_kernel(
@@ -315,8 +330,12 @@
     products = jnp.sum(grad_mixed * gained, axis=1, keepdims=True)
     lane = lax.broadcasted_iota(jnp.int32, (length, LANES), 1)
     turned = jnp.where(lane == 0, squares, products).T
-    stats_ref[pl.ds(slot, 1), :] = turned[0:1]
-    stats_ref[pl.ds(pl.num_programs(0) + slot, 1), :] = turned[1:2]
+    span = stats_ref.shape[1]
+    for part in range(length // span):
+        row = slot * (length // span) + part
+        lanes = slice(part * span, (part + 1) * span)
+        stats_ref[pl.ds(row, 1), :] = turned[0:1, lanes]
+        stats_ref[pl.ds(stats_ref.shape[0] // 2 + row, 1), :] = turned[1:2, lanes]
 
 
 def early_kernel(
@@ -342,9 +361,15 @@
     inner = gain_ref.shape[1]
     chunk = piece_0.shape[0] // 2
     count = pl.num_programs(0)
-    scale = lax.rsqrt(stats_ref[pl.ds(slot, 1), :] / inner_all + EPSILON)
-    slope = scale * scale * scale * stats_ref[pl.ds(count + slot, 1), :] / inner_all
-    scale, slope = row_spread(scale), row_spread(slope)
+    scales, slopes = [], []
+    span = gate_ref.shape[0] // stats_ref.shape[1]
+    for part in range(span):
+        row = slot * span + part
+        scale = lax.rsqrt(stats_ref[pl.ds(row, 1), :] / inner_all + EPSILON)
+        slope = scale * scale * scale * stats_ref[pl.ds(stats_ref.shape[0] // 2 + row, 1), :] / inner_all
+        scales.append(row_spread(scale))
+        slopes.append(row_spread(slope))
+    scale, slope = jnp.concatenate(scales, axis=0), jnp.concatenate(slopes, axis=0)
     gate = gate_ref[...]
     scanned = scanned_ref[...]
     sigmoid = jax.nn.sigmoid(gate)
@@ -399,6 +424,7 @@
     piece_3,
     sums_ref,
     conv_ref,
+    last_ref,
     small_ref,
     pre_ref,
     extra_ref,
@@ -414,8 +440,24 @@
         small_ref[...] = jnp.zeros_like(small_ref)
         pre_ref[...] = jnp.zeros_like(pre_ref)
         sums_ref[...] = jnp.zeros_like(sums_ref)
+        conv_ref[...] = jnp.zeros_like(conv_ref)
+
+    last_ref[...] = conv_ref[...]
+    block = normed_ref.shape[1] // heads
+
+    def beside(index):
+        columns = slice(index * block, (index + 1) * block)
+        normed = normed_ref[:, columns]
+        sums_ref[columns, :] += dot_tn(normed, last_ref[...])
+        grad_normed = dot_nt(grad_gate_ref[...], gate_weight[columns, :])
+        grad_normed = grad_normed + dot_nt(last_ref[...], weight_ref[columns, :])
+        pre_sum = jnp.sum(grad_normed * normed.astype(jnp.float32), axis=0, keepdims=True)
+        pre_ref[0:1, columns] += jnp.where(slot > 0, pre_sum, 0.0)
+        normed_grad_ref[:, columns] = grad_normed.astype(LOW)
 
     scan_backward(
+        slot < pl.num_programs(0) - 1,
+        beside,
         heads,
         part_ref,
         grad_ref,
@@ -428,42 +470,42 @@
         conv_ref,
         small_ref,
     )
-    normed = read(normed_ref)
-    grad_conv = conv_ref[...]
-    sums_ref[...] += dot_tn(normed, grad_conv)
-    grad_normed = dot_nt(grad_gate_ref[...], gate_weight[...]) + dot_nt(grad_conv, weight_ref[...])
-    pre_ref[0:1, :] += jnp.sum(grad_normed * normed.astype(jnp.float32), axis=0, keepdims=True)
-
-    normed_grad_ref[...] = grad_normed.astype(LOW)
-
     @pl.when(slot == pl.num_programs(0) - 1)
     def _():
         core = place_ref[8]
-        taps_count = taps_ref.shape[0]
+        count = taps_ref.shape[0] + 1
+        wide = inner + states
         extra_ref[...] = jnp.zeros_like(extra_ref)
-        extra_ref[: taps_count + 1, :] = small_ref[: taps_count + 1, :width]
+        extra_ref[:count, :] = small_ref[:count, :wide]
         extra_ref[5:6, :inner] = small_ref[5:6, :inner]
-        extra_ref[5:6, inner:] = pre_ref[0:1, 2 * width :]
+        extra_ref[5:6, inner:] = small_ref[6:7, width:]
         extra_ref[6:7, :inner] = gain_grad_ref[0:1, :]
-        extra_ref[6:7, inner : inner + LANES] = small_ref[5:6, width:]
-        extra_ref[6:7, inner + LANES :] = small_ref[6:7, width:]
-        extra_ref[7:8, :] = pre_ref[0:1, :width]
-        extra_ref[8:9, :] = pre_ref[0:1, width : 2 * width]
+        extra_ref[6:7, inner:] = small_ref[5:6, width:]
+        for part in range(3):
+            extra_ref[7 + part : 8 + part, :] = pre_ref[0:1, part * wide : (part + 1) * wide]
+        for part in range(count - 1):
+            extra_ref[10:11, part * states : (part + 1) * states] = small_ref[part : part + 1, wide:width]
+        extra_ref[11:12, :states] = small_ref[count - 1 : count, wide:width]
         high, rest = parts_of(extra_ref[...], 2)
         for piece in (piece_0, piece_1, piece_2, piece_3):
-            piece[8 * chunk // 4 : 8 * chunk // 4 + 16, :] = high
-            piece[8 * chunk // 4 + 16 :, :] = rest
+            piece[2 * chunk + 16 : 2 * chunk + 32, :] = high
+            piece[2 * chunk + 32 :, :] = rest
+            piece[2 * chunk : 2 * chunk + 16, 2 * chunk :] = jnp.zeros((16, wide - 2 * chunk), LOW)
         for away, piece in enumerate((piece_0, piece_1, piece_2, piece_3)):
             for half in range(2):
                 rows = pl.ds(pl.multiple_of(place_ref[2 * away + half], 16), chunk)
                 local = slice(half * chunk, (half + 1) * chunk)
                 whole = slice((2 * away + half) * chunk, (2 * away + half + 1) * chunk)
+                step_rows = [] if half == 0 else step_rows
                 b_sums = sums_ref[rows, inner : inner + states].astype(LOW)
                 c_sums = sums_ref[rows, inner + states : width].astype(LOW)
+                steps = sums_ref[rows, width:]
                 given_ref[whole, :] = jnp.where(core == 0, c_sums, b_sums)
                 piece[local, :inner] = sums_ref[rows, :inner].astype(LOW)
                 piece[local, inner : inner + states] = jnp.where(core == 0, b_sums, c_sums)
-                piece[local, inner + states :] = sums_ref[rows, width:].astype(LOW)
+                step_rows.append(steps)
+            turned = jnp.concatenate(step_rows, axis=0).T[:16]
+            piece[2 * chunk : 2 * chunk + 16, : 2 * chunk] = turned.astype(LOW)
 
 
 def row_block(length, width):
@@ -477,6 +519,16 @@
     return pl.BlockSpec((length, width), index)
 
 
+def early_block(slots):
+    return lambda length, width: pl.BlockSpec(
+        (length, width), lambda step, place: (jnp.minimum(step, slots - 1), 0)
+    )
+
+
+def late_block(length, width):
+    return pl.BlockSpec((length, width), lambda step, place: (jnp.maximum(step - 1, 0), 0))
+
+
 def near_block(length, width, half):
     return pl.BlockSpec((length, width), lambda slot, place: (jnp.minimum(slot, half - 1), 0))
 
@@ -489,7 +541,7 @@
     return pl.BlockSpec(shape, lambda slot, place: (0,) * len(shape))
 
 
-def run_slots(kernel, slots, place, cut, whole, outs, scratch, micros, waits=(), block=row_block):
+def run_slots(kernel, slots, place, cut, whole, outs, scratch, micros, waits=(), specs=None):
     in_specs, arrays, places = [], [], []
     for array in cut:
         places.append(len(arrays))
@@ -499,8 +551,10 @@
             in_specs.append(far_block(length, array[1].shape[1], slots // 2))
             arrays.extend(array)
         else:
-            in_specs.append(block(array.shape[0] // slots, array.shape[1]))
+            spec = row_block if specs is None else specs[len(places) - 1]
+            in_specs.append(spec(array.shape[0] // slots, array.shape[1]))
             arrays.append(array)
+    arrays = [pltpu.with_memory_space_constraint(array, pltpu.HBM) for array in arrays]
     in_specs += [whole_block(array.shape) for array in whole]
     arrays += whole
     given = len(arrays)
@@ -516,12 +570,12 @@
         run,
         grid_spec=pltpu.PrefetchScalarGridSpec(
             num_scalar_prefetch=1,
-            grid=(slots,),
+            grid=(slots if specs is None else slots + 1,),
             in_specs=in_specs + [pl.BlockSpec(memory_space=pl.ANY)] * len(waits),
             out_specs=[spec for _, _, spec in outs],
             scratch_shapes=scratch,
         ),
-        out_shape=[jax.ShapeDtypeStruct(shape, dtype) for shape, dtype, _ in outs],
+        out_shape=[pltpu.HBM(shape, dtype) for shape, dtype, _ in outs],
         compiler_params=pltpu.CompilerParams(vmem_limit_bytes=44 << 20),
         cost_estimate=pl.CostEstimate(flops=int(micros * 1e9), bytes_accessed=1 << 20, transcendentals=0),
     )(place, *arrays, *waits)
@@ -580,43 +634,46 @@
     return below[:16].astype(jnp.float32) + below[16:].astype(jnp.float32)
 
 
-def side_sums(left, right, ranks):
-    rows, width = left[0].shape
+def side_sums(terms, ranks, small, waits):
+    width = terms[0].shape[1]
+    rows = terms[0].shape[0] - 48 if small else terms[0].shape[0]
     own = rows // ranks
-    terms = (*left, *right)
-    small_width = right[0].shape[1]
 
     def run(*refs):
-        def total(these, read):
-            values = [read(ref) for ref in these]
+        def total(read):
+            values = [read(ref) for ref in refs[:4]]
             return (values[0] + values[1]) + (values[2] + values[3])
 
         out_ref = refs[-1]
-        high, rest = parts_of(total(refs[4:8], lambda ref: small_rows(ref[rows:, :])), 2)
+        if small:
+            steps = turned_columns(total(lambda ref: ref[rows : rows + 16, :rows].astype(jnp.float32))).astype(LOW)
+            high, rest = parts_of(total(lambda ref: small_rows(ref[rows + 16 :, :])), 2)
         for rank in range(ranks):
             local = slice(rank * own, (rank + 1) * own)
-            out_ref[rank, :own, :width] = total(refs[:4], lambda ref: ref[local, :].astype(jnp.float32)).astype(LOW)
-            out_ref[rank, :own, width:] = total(refs[4:8], lambda ref: ref[local, :].astype(jnp.float32)).astype(LOW)
-            out_ref[rank, own:, :small_width] = high
-            out_ref[rank, own:, small_width : 2 * small_width] = rest
-            out_ref[rank, own:, 2 * small_width :] = jnp.zeros_like(out_ref[rank, own:, 2 * small_width :])
-
-    shape = (ranks, own + 16, width + small_width)
+            out_ref[rank, :own, :width] = total(lambda ref: ref[local, :].astype(jnp.float32)).astype(LOW)
+            if small:
+                out_ref[rank, :own, width:] = steps[local]
+                out_ref[rank, own : own + 16, :width] = high
+                out_ref[rank, own + 16 :, :width] = rest
+                out_ref[rank, own:, width:] = jnp.zeros((32, LANES), LOW)
+
+    whole = pl.BlockSpec(terms[0].shape, lambda: (0, 0))
+    shape = (ranks, own + 32, width + LANES) if small else (ranks, own, width)
     return pl.pallas_call(
         run,
+        in_specs=[whole] * 4 + [pl.BlockSpec(memory_space=pl.ANY)] * len(waits),
         out_shape=jax.ShapeDtypeStruct(shape, LOW),
         compiler_params=pltpu.CompilerParams(vmem_limit_bytes=24 << 20),
-        cost_estimate=pl.CostEstimate(flops=int(3e9), bytes_accessed=1 << 20, transcendentals=0),
-    )(*terms)
-
-
-def owner_outputs(owned, rows, heads, states, sizes, waits):
+        cost_estimate=pl.CostEstimate(flops=int(2e9), bytes_accessed=1 << 20, transcendentals=0),
+    )(*terms, *waits)
+
+
+def owner_outputs(early, owned, rows, heads, states, sizes, waits):
     proj, inner_all, taps_shape, model = sizes
     ranks = owned.shape[0]
     inner = inner_all // ranks
-    width = inner + 2 * states
-
-    def blocks(ref, store):
+
+    def blocks(early_ref, ref, store):
         def lanes_of(value, rank):
             lane = lax.broadcasted_iota(jnp.int32, value.shape, 1)
             value = jnp.where(lane < heads, value, 0.0)
@@ -628,43 +685,63 @@
         for rank in range(ranks):
             lanes = slice(rank * inner, (rank + 1) * inner)
             main = ref[rank, :rows, :].astype(jnp.float32)
-            extra = ref[rank, rows:, :width].astype(jnp.float32) + ref[rank, rows:, width : 2 * width].astype(jnp.float32)
-            in_ref[:, lanes] = main[:, :inner]
-            out_ref[:, lanes] = main[:, inner : 2 * inner]
-            in_ref[:, inner_all + rank * inner : inner_all + (rank + 1) * inner] = main[:, 2 * inner : 3 * inner]
+            extra = small_rows(ref[rank, rows:, : inner + states])
+            in_ref[:, lanes] = early_ref[rank, :, :inner].astype(jnp.float32)
+            out_ref[:, lanes] = early_ref[rank, :, inner:].astype(jnp.float32)
+            in_ref[:, inner_all + rank * inner : inner_all + (rank + 1) * inner] = main[:, :inner]
             if rank % 2 == 0:
-                b_sum = b_sum + main[:, 3 * inner : 3 * inner + states]
+                b_sum = b_sum + main[:, inner : inner + states]
             else:
-                c_sum = c_sum + main[:, 3 * inner : 3 * inner + states]
-            step_sum = step_sum + lanes_of(main[:, 3 * inner + states :], rank)
+                c_sum = c_sum + main[:, inner : inner + states]
+            step_sum = step_sum + lanes_of(main[:, inner + states :], rank)
             shared = shared + extra
             taps_ref[:, lanes] = extra[:taps_count, :inner]
             bias_ref[:, lanes] = extra[taps_count : taps_count + 1, :inner]
             gain_ref[:, lanes] = extra[6:7, :inner]
-            dt_sum = dt_sum + lanes_of(extra[6:7, inner : inner + LANES], rank)
-            alog_sum = alog_sum + lanes_of(extra[6:7, inner + LANES :], rank)
+            dt_sum = dt_sum + lanes_of(extra[6:7, inner:], rank)
+            alog_sum = alog_sum + lanes_of(extra[5:6, inner:], rank)
             skip_sum = skip_sum + lanes_of(lanes_sum(extra[:, :inner], heads)[5:6], rank)
         first_state = 2 * inner_all
         in_ref[:, first_state : first_state + states] = b_sum
         in_ref[:, first_state + states : first_state + 2 * states] = c_sum
         in_ref[:, first_state + 2 * states :] = step_sum[:, : proj - first_state - 2 * states]
-        taps_ref[:, inner_all:] = shared[:taps_count, inner:]
-        bias_ref[:, inner_all:] = shared[taps_count : taps_count + 1, inner:]
-        pre_ref[:, :width] = shared[7:8]
-        pre_ref[:, width : 2 * width] = shared[8:9]
-        pre_ref[:, 2 * width :] = shared[5:6, inner : inner + model - 2 * width]
+        taps_ref[:, inner_all : inner_all + states] = shared[:taps_count, inner:]
+        bias_ref[:, inner_all : inner_all + states] = shared[taps_count : taps_count + 1, inner:]
+        for tap in range(taps_count):
+            taps_ref[tap : tap + 1, inner_all + states :] = shared[10:11, tap * states : (tap + 1) * states]
+        bias_ref[:, inner_all + states :] = shared[11:12, :states]
+        wide = inner + states
+        for part in range(3):
+            pre_ref[:, part * wide : (part + 1) * wide] = shared[7 + part : 8 + part]
         head_ref[0:1, :] = dt_sum
         head_ref[1:2, :] = alog_sum
         head_ref[2:3, :] = skip_sum
 
     shapes = [(rows, proj), (rows, inner_all), taps_shape, (1, taps_shape[1]), (1, inner_all), (1, model), (8, LANES)]
     return pl.pallas_call(
-        lambda ref, *refs: blocks(ref, refs[len(waits) :]),
-        in_specs=[pl.BlockSpec(owned.shape, lambda: (0, 0, 0))] + [pl.BlockSpec(memory_space=pl.ANY)] * len(waits),
+        lambda early_ref, ref, *refs: blocks(early_ref, ref, refs[len(waits) :]),
+        in_specs=[pl.BlockSpec(array.shape, lambda: (0, 0, 0)) for array in (early, owned)]
+        + [pl.BlockSpec(memory_space=pl.ANY)] * len(waits),
         out_shape=[jax.ShapeDtypeStruct(shape, jnp.float32) for shape in shapes],
         compiler_params=pltpu.CompilerParams(vmem_limit_bytes=24 << 20),
         cost_estimate=pl.CostEstimate(flops=int(3e9), bytes_accessed=1 << 20, transcendentals=0),
-    )(owned, *waits)
+    )(early, owned, *waits)
+
+
+def pack_steps(value, start, width):
+    rows = value.shape[0]
+
+    def run(value_ref, out_ref):
+        out_ref[:rows, :] = value_ref[:, start : start + width]
+        steps = value_ref[:, start + width : start + width + LANES].astype(jnp.float32)
+        out_ref[rows:, :rows] = steps.T[:16].astype(LOW)
+        out_ref[rows:, rows:] = jnp.zeros((16, width - rows), LOW)
+
+    return pl.pallas_call(
+        run,
+        out_shape=jax.ShapeDtypeStruct((rows + 16, width), LOW),
+        cost_estimate=pl.CostEstimate(flops=int(1e9), bytes_accessed=1 << 20, transcendentals=0),
+    )(value)
 
 
 def add_states(pieces, states, start):
@@ -783,8 +860,13 @@
         axis=2,
     )
     plane_weights = exchange(packed).reshape(ranks * rows, -1)
-    conv_pieces = gather_rows(plane_weights[:, 2 * inner :])
-    other_states = swap(jnp.concatenate([piece[:, inner : inner + states] for piece in conv_pieces], axis=0))
+    if direct:
+        conv_pieces = gather_rows(pack_steps(plane_weights, 2 * inner, inner + states))
+    else:
+        conv_pieces = [pack_steps(piece, 0, inner + states) for piece in gather_rows(plane_weights[:, 2 * inner :])]
+    other_states = swap(
+        jnp.concatenate([piece[:piece_rows, inner : inner + states] for piece in conv_pieces], axis=0)
+    )
     late_pieces = gather_rows(columns_of(plane_weights, 0, 2 * inner, conv_pieces[1:]))
 
     stream = hidden_in.astype(jnp.float32)
@@ -825,14 +907,14 @@
     )
     gate, grad_mixed, branch, stats, gate_weights = run_slots(
         gate_kernel,
-        slots,
+        slots // 2,
         place,
         (normed, upstream, scanned),
         (*late_pieces, gain_row),
         [
-            ((tokens, inner), jnp.float32, row_block(length, inner)),
-            ((tokens, inner), jnp.float32, row_block(length, inner)),
-            ((tokens, model), LOW, row_block(length, model)),
+            ((tokens, inner), jnp.float32, row_block(2 * length, inner)),
+            ((tokens, inner), jnp.float32, row_block(2 * length, inner)),
+            ((tokens, model), LOW, row_block(2 * length, model)),
             ((2 * slots, length), jnp.float32, whole_block((2 * slots, length))),
             ((model, inner), LOW, whole_block((model, inner))),
         ],
@@ -850,13 +932,13 @@
     piece_shape = (piece_rows, 2 * inner)
     grad_gate, grad_scanned, gain_grad, *early = run_slots(
         functools.partial(early_kernel, inner_all),
-        slots,
+        slots // 2,
         place,
         (normed, upstream, scanned, gate, grad_mixed),
         (stats, gain_row),
         [
-            ((tokens, inner), LOW, row_block(length, inner)),
-            ((tokens, inner), jnp.float32, row_block(length, inner)),
+            ((tokens, inner), LOW, row_block(2 * length, inner)),
+            ((tokens, inner), jnp.float32, row_block(2 * length, inner)),
             ((8, inner), jnp.float32, whole_block((8, inner))),
         ]
         + [(piece_shape, LOW, whole_block(piece_shape))] * 4,
@@ -864,7 +946,7 @@
         16,
     )
     width = taps.shape[1]
-    piece_shape = (piece_rows + 32, inner + states + LANES)
+    piece_shape = (piece_rows + 48, inner + states)
     held = run_slots(
         functools.partial(back_kernel, heads),
         slots,
@@ -872,18 +954,20 @@
         (part, grad_scanned, scanned, grad_gate, normed),
         (conv_weights, gate_weights, *params, gain_grad),
         [
-            ((tokens, model), LOW, row_block(length, model)),
+            ((tokens, model), LOW, late_block(length, model)),
             ((model, states), LOW, whole_block((model, states))),
         ]
         + [(piece_shape, LOW, whole_block(piece_shape))] * 4,
         [
             pltpu.VMEM((model, part_width), jnp.float32),
             pltpu.VMEM((length, part_width), LOW),
+            pltpu.VMEM((length, part_width), LOW),
             pltpu.VMEM((8, part_width), jnp.float32),
             pltpu.VMEM((8, model), jnp.float32),
-            pltpu.VMEM((16, width), jnp.float32),
+            pltpu.VMEM((16, inner + states), jnp.float32),
         ],
-        40,
+        30,
+        specs=[early_block(slots)] * 3 + [late_block] * 2,
     )
     if direct:
         early_moved = [cross(early[away], LINE, away, 4) for away in (2, 3, 1)]
@@ -900,20 +984,25 @@
     grad_hidden = (own_upstream.astype(jnp.float32) + grad_stream).astype(LOW)
 
     if direct:
-        early_terms, conv_terms = [early[0], *early_moved], [pieces[0], *conv_moved]
-        side = side_sums(early_terms, conv_terms, ranks)
+        early_owned = exchange(side_sums([early[0], *early_moved], ranks, False, pieces[:1]))
+        owned = exchange(side_sums([pieces[0], *conv_moved], ranks, True, (early_owned,)))
     else:
-        extra = small_rows(pieces[0][piece_rows:])
-        high, rest = parts_of(lax.psum(extra, LINE), 2)
-        side = jnp.concatenate([scatter_rows(early), scatter_rows([p[:piece_rows] for p in pieces])], axis=1)
-        below = jnp.pad(jnp.concatenate([high, rest], axis=1), ((0, 0), (0, side.shape[1] - 2 * width)))
-        below = jnp.broadcast_to(below[None], (ranks, *below.shape))
-        side = jnp.pad(side.reshape(ranks, rows, -1), ((0, 0), (0, -rows % 16), (0, 0)))
-        side = jnp.concatenate([side, below], axis=1)
-    owned = exchange(side)
+        below = jnp.concatenate(parts_of(lax.psum(small_rows(pieces[0][piece_rows + 16 :]), LINE), 2), axis=0)
+        below = jnp.pad(jnp.broadcast_to(below[None], (ranks, *below.shape)), ((0, 0), (0, 0), (0, LANES)))
+
+        def padded(value):
+            return jnp.pad(value.reshape(ranks, rows, -1), ((0, 0), (0, -rows % 16), (0, 0)))
+
+        def with_steps(piece):
+            steps = piece[piece_rows : piece_rows + 16, :piece_rows].T
+            return jnp.concatenate([piece[:piece_rows], jnp.pad(steps, ((0, 0), (0, LANES - 16)))], axis=1)
+
+        early_owned = exchange(padded(scatter_rows(early)))
+        conv = padded(scatter_rows([with_steps(piece) for piece in pieces]))
+        owned = exchange(jnp.concatenate([conv, below], axis=1))
     sizes_out = (in_weight.shape[1], inner_all, conv_weight.shape, model)
     owned_in, owned_out, taps_grad, bias_grad, gain_grads, pre_grad, head_grads = owner_outputs(
-        owned, rows + -rows % 16, heads, states, sizes_out, (grad_hidden, output)
+        early_owned, owned, rows + -rows % 16, heads, states, sizes_out, (output,)
     )
     return (
         output,

time: 334 us -> 314 us (0.940)
  waiting for transfers between devices: 148 us -> 131 us
  local copies, waits for them, and re-layouts: 34.8 us -> 20.5 us
  Pallas kernels: 101 us -> 107 us
    unnamed x83 -> x69, local copies, waits for them, and re-layouts: 26.7 us -> 14.2 us
    ppermute x15, waiting for transfers between devices: 115 us -> 105 us  [cross(): return lax.ppermute(value, axes, [(i, i ^ distance) for i in range(count)])]
    all_to_all x2 -> x3, waiting for transfers between devices: 29.5 us -> 22.2 us  [exchange(): return lax.all_to_all(value, PLANE, split_axis=0, concat_axis=0, tiled=True)]
    pallas_call x2 -> x4, Pallas kernels: 3.65 us -> 8.43 us  [the longest x2 4.67 us: side_sums(): pl.pallas_call(run, in_specs=[whole] * 4 + [pl.BlockSpec(memory_space=pl....]
    all_to_all x2 -> x3, starting transfers between devices: 7.3 us -> 11.1 us  [exchange(): return lax.all_to_all(value, PLANE, split_axis=0, concat_axis=0, tiled=True)]
  transfers between devices with their start and end apart: 24 -> 25, of which waited for: 15 -> 15; matrix products, arithmetic and copies ran while one was open for 2% -> 2% of each run, Pallas kernels for 25% -> 28%
where the time goes in v4:
time: 314 us; the launch traced here: 312 us
  waiting for transfers between devices  131 us (42%)
  Pallas kernels  107 us (34%)
  starting transfers between devices  33 us (11%)
  local copies, waits for them, and re-layouts  20.5 us (7%)
  between operations  14.8 us (5%)
  other arithmetic  6.7 us (2%)
    ppermute x15, waiting for transfers between devices, cross(): return lax.ppermute(value, axes, [(i, i ^ distance) for i in range(count)])  105 us
    pallas_call x4, Pallas kernels, run_slots(): pl.pallas_call(run, grid_spec=pltpu.PrefetchScalarGridSpec(num_scalar_pre...  92.2 us
    all_to_all x3, waiting for transfers between devices, exchange(): return lax.all_to_all(value, PLANE, split_axis=0, concat_axis=0, tiled=True)  22.2 us
    ppermute x15, starting transfers between devices, cross(): return lax.ppermute(value, axes, [(i, i ^ distance) for i in range(count)])  21.5 us
    unnamed x69, local copies, waits for them, and re-layouts  14.2 us
    all_to_all x3, starting transfers between devices, exchange(): return lax.all_to_all(value, PLANE, split_axis=0, concat_axis=0, tiled=True)  11.1 us
  transfers between devices with their start and end apart: 25, of which 15 were waited for; matrix products, arithmetic and copies ran while one was open for 2% of the time, Pallas kernels for 28%

profile of v4, /device:TPU:16, one launch (start us, length us, event | category | flops | bytes accessed | tf_op | source)
XLA Modules:
  0.0 312.5 jit_solution(1518508640876078836)
XLA Ops:
  7.2 0.8 slice.48
  7.9 0.7 slice.47
  8.7 1.1 fusion.11
  10.1 0.7 fusion.9
  10.8 0.7 fusion.8
  11.6 0.7 fusion.7
  12.3 0.7 constant_dynamic-update-slice_fusion
  13.0 0.7 pad_dynamic-update-slice_fusion
  13.6 3.7 %all-to-all-start = ((bf16[8,48,1408]{2,1,0:T(8,128)(2,1)}), bf16[8,48,1408]{2,1,0:T(8,128)(2,1)S(1)}, u32[]{:S(2)}, u32[]{:S(2)}) async-start(bf16[8,48,1408]{2,1,0:T(8,128)(2,1)} %pad_dynamic-update-slice_fusion), calls=%async_computation | async-start | bytes 2162688 | tf_op jit(solution)/shard_map/all_to_all | solution.py:838
  17.4 14.7 %all-to-all-done = bf16[8,48,1408]{2,1,0:T(8,128)(2,1)S(1)} async-done(((bf16[8,48,1408]{2,1,0:T(8,128)(2,1)}), bf16[8,48,1408]{2,1,0:T(8,128)(2,1)S(1)}, u32[]{:S(2)}, u32[]{:S(2)}) %all-to-all-start) | async-done | bytes 1081376 | tf_op jit(solution)/shard_map/all_to_all | solution.py:838
  32.2 1.2 shard_map.203.refs_0_
  34.2 1.0 shard_map.204
  35.3 2.1 shard_map.205.refs_1_
  37.8 3.5 %collective-permute-start.1 = (bf16[400,512]{1,0:T(8,128)(2,1)}, bf16[400,512]{1,0:T(8,128)(2,1)S(1)}, u32[]{:S(2)}, u32[]{:S(2)}) collective-permute-start(bf16[400,512]{1,0:T(8,128)(2,1)} %shard_map.205.refs_1_), channel_id=1, source_target_pairs={{0,8},{4,12},{8,0},{12,4},{1,9},{5,13},{9,1},{13,5},{2,10},{6,14},... | collective-permute-start | bytes 1228808 | tf_op jit(solution)/shard_map/ppermute | solution.py:26
  41.5 0.8 dynamic_slice.27
  42.7 0.9 slice.60
  43.6 23.9 %collective-permute-done.2.refs_4_.refs_2_ = bf16[400,512]{1,0:T(8,128)(2,1)S(1)} collective-permute-done((bf16[400,512]{1,0:T(8,128)(2,1)}, bf16[400,512]{1,0:T(8,128)(2,1)S(1)}, u32[]{:S(2)}, u32[]{:S(2)}) %collective-permute-start.2) | collective-permute-done | bytes 409632 | tf_op jit(solution)/shard_map/ppermute | solution.py:26
  67.5 5.5 %collective-permute-done.1.refs_3_.refs_1_ = bf16[400,512]{1,0:T(8,128)(2,1)S(1)} collective-permute-done((bf16[400,512]{1,0:T(8,128)(2,1)}, bf16[400,512]{1,0:T(8,128)(2,1)S(1)}, u32[]{:S(2)}, u32[]{:S(2)}) %collective-permute-start.1) | collective-permute-done | bytes 409632 | tf_op jit(solution)/shard_map/ppermute | solution.py:26
  73.1 0.9 pad_maximum_fusion
  74.0 2.0 shard_map.207.refs_3_
  76.0 1.6 collective-permute-start.6
  77.6 4.2 %collective-permute-start.5 = (bf16[384,768]{1,0:T(8,128)(2,1)}, bf16[384,768]{1,0:T(8,128)(2,1)}, u32[]{:S(2)}, u32[]{:S(2)}) collective-permute-start(bf16[384,768]{1,0:T(8,128)(2,1)} %shard_map.207.refs_3_), channel_id=1, source_target_pairs={{0,8},{4,12},{8,0},{12,4},{1,9},{5,13},{9,1},{13,5},{2,10},{6,14},... | collective-permute-start | bytes 1769480 | tf_op jit(solution)/shard_map/ppermute | solution.py:26
  81.8 1.0 copy-done.13
  82.8 1.0 copy-done.15
  83.8 1.0 copy-done.17
  84.8 19.0 %shard_map.206 = (f32[2048,768]{1,0:T(8,128)}, f32[2048,384]{1,0:T(8,128)}, bf16[1536,768]{1,0:T(8,128)(2,1)}) custom-call(s32[9]{0:T(128)S(1)} %stack.39.place_ref, bf16[2048,1536]{1,0:T(8,128)(2,1)} %all-gather.3.cloned.1.call-done.refs_0_.refs_4_, bf16[400,512]{1,0:T(8,128)(2,1)S(1)} %copy-done.11, bf16[400,512]{1,0:T(8,128)(2,1)S(1)} %copy-done.17, ...), custom_call_target="tpu_custom_call" | custom-call | flops 12000000000 | bytes 1048576 | tf_op jit(solution)/shard_map/pallas_call | solution.py:569
  103.8 14.0 %collective-permute-done.6.refs_6_ = bf16[384,768]{1,0:T(8,128)(2,1)} collective-permute-done((bf16[384,768]{1,0:T(8,128)(2,1)}, bf16[384,768]{1,0:T(8,128)(2,1)}, u32[]{:S(2)}, u32[]{:S(2)}) %collective-permute-start.6) | collective-permute-done | bytes 589856 | tf_op jit(solution)/shard_map/ppermute | solution.py:26
  117.7 11.3 %collective-permute-done.5.refs_5_ = bf16[384,768]{1,0:T(8,128)(2,1)} collective-permute-done((bf16[384,768]{1,0:T(8,128)(2,1)}, bf16[384,768]{1,0:T(8,128)(2,1)}, u32[]{:S(2)}, u32[]{:S(2)}) %collective-permute-start.5) | collective-permute-done | bytes 589856 | tf_op jit(solution)/shard_map/ppermute | solution.py:26
  129.1 1.1 copy-done.18
  130.1 16.0 %shard_map.208 = (f32[2048,384]{1,0:T(8,128)}, f32[2048,384]{1,0:T(8,128)}, bf16[2048,1536]{1,0:T(8,128)(2,1)}, f32[16,256]{1,0:T(8,128)}, bf16[1536,384]{1,0:T(8,128)(2,1)}) custom-call(s32[9]{0:T(128)S(1)} %stack.39.place_ref, bf16[2048,1536]{1,0:T(8,128)(2,1)} %all-gather.3.cloned.1.call-done.refs_0_.refs_4_, ...), custom_call_target="tpu_custom_call" | custom-call | flops 14000000000 | bytes 1048576 | tf_op jit(solution)/shard_map/pallas_call | solution.py:569
  146.8 1.2 collective-permute-done.7
  148.0 0.7 collective-permute-start.10
  148.7 1.3 collective-permute-start.9
  150.0 1.5 collective-permute-start.8
  151.8 0.7 collective-permute-done.9
  152.4 2.2 collective-permute-done.8
  154.7 18.1 %shard_map.209 = (bf16[2048,384]{1,0:T(8,128)(2,1)}, f32[2048,384]{1,0:T(8,128)}, f32[8,384]{1,0:T(8,128)}, bf16[384,768]{1,0:T(8,128)(2,1)}, bf16[384,768]{1,0:...) custom-call(s32[9]{0:T(128)S(1)} %stack.39.place_ref, ...), custom_call_target="tpu_custom_call" | custom-call | flops 16000000000 | bytes 1048576 | tf_op jit(solution)/shard_map/pallas_call | solution.py:569
  172.8 3.3 %collective-permute-start.11 = (bf16[384,768]{1,0:T(8,128)(2,1)}, bf16[384,768]{1,0:T(8,128)(2,1)S(1)}, u32[]{:S(2)}, u32[]{:S(2)}) collective-permute-start(bf16[384,768]{1,0:T(8,128)(2,1)} %get-tuple-element.66), channel_id=1, source_target_pairs={{0,8},{4,12},{8,0},{12,4},{1,9},{5,13},{9,1},{13,5},{2,10},{6,14},... | collective-permute-start | bytes 1769480 | tf_op jit(solution)/shard_map/ppermute | solution.py:26
  176.6 1.0 collective-permute-start.13
  177.6 0.7 copy-done.22
  178.3 39.1 %shard_map.210 = (bf16[2048,1536]{1,0:T(8,128)(2,1)}, bf16[1536,128]{1,0:T(8,128)(2,1)}, bf16[432,512]{1,0:T(8,128)(2,1)}, bf16[432,512]{1,0:T(8,128)(2,1)}, bf1...) custom-call(s32[9]{0:T(128)S(1)} %stack.39.place_ref, f32[2048,768]{1,0:T(8,128)} %get-tuple-element.52.refs_0_, ...), custom_call_target="tpu_custom_call" | custom-call | flops 30000001024 | bytes 1048576 | tf_op jit(solution)/shard_map/pallas_call | solution.py:569
  217.5 8.7 %collective-permute-done.12.refs_7_.refs_2_ = bf16[384,768]{1,0:T(8,128)(2,1)S(1)} collective-permute-done((bf16[384,768]{1,0:T(8,128)(2,1)}, bf16[384,768]{1,0:T(8,128)(2,1)S(1)}, u32[]{:S(2)}, u32[]{:S(2)}) %collective-permute-start.12) | collective-permute-done | bytes 589856 | tf_op jit(solution)/shard_map/ppermute | solution.py:26
  226.2 0.8 copy-done.8
  227.0 1.0 copy-done.24
  228.0 1.7 collective-permute-done.14.refs_4_
  229.7 0.7 copy-done.28
  230.5 2.1 shard_map.212
  232.6 1.0 copy-done.10
  233.6 1.2 copy-done.19
  234.8 2.3 shard_map.213
  237.1 3.5 %all-to-all-start.1 = ((bf16[8,48,768]{2,1,0:T(8,128)(2,1)}), bf16[8,48,768]{2,1,0:T(8,128)(2,1)S(1)}, u32[]{:S(2)}, u32[]{:S(2)}) async-start(bf16[8,48,768]{2,1,0:T(8,128)(2,1)} %shard_map.213), calls=%async_computation.3 | async-start | bytes 1179648 | tf_op jit(solution)/shard_map/all_to_all | solution.py:838
  240.7 2.2 collective-permute-start.16
  242.9 1.2 collective-permute-start.17
  244.2 15.6 %collective-permute-done.15.refs_1_ = bf16[432,512]{1,0:T(8,128)(2,1)S(1)} collective-permute-done((bf16[432,512]{1,0:T(8,128)(2,1)}, bf16[432,512]{1,0:T(8,128)(2,1)S(1)}, u32[]{:S(2)}, u32[]{:S(2)}) %collective-permute-start.15) | collective-permute-done | bytes 442400 | tf_op jit(solution)/shard_map/ppermute | solution.py:26
  259.8 13.0 %collective-permute-done.16.refs_2_ = bf16[432,512]{1,0:T(8,128)(2,1)S(1)} collective-permute-done((bf16[432,512]{1,0:T(8,128)(2,1)}, bf16[432,512]{1,0:T(8,128)(2,1)S(1)}, u32[]{:S(2)}, u32[]{:S(2)}) %collective-permute-start.16) | collective-permute-done | bytes 442400 | tf_op jit(solution)/shard_map/ppermute | solution.py:26
  272.8 10.3 %collective-permute-done.17.refs_3_ = bf16[432,512]{1,0:T(8,128)(2,1)} collective-permute-done((bf16[432,512]{1,0:T(8,128)(2,1)}, bf16[432,512]{1,0:T(8,128)(2,1)}, u32[]{:S(2)}, u32[]{:S(2)}) %collective-permute-start.17) | collective-permute-done | bytes 442400 | tf_op jit(solution)/shard_map/ppermute | solution.py:26
  283.1 2.4 shard_map.214
  285.5 3.9 %all-to-all-start.2 = ((bf16[8,80,640]{2,1,0:T(8,128)(2,1)}), bf16[8,80,640]{2,1,0:T(8,128)(2,1)S(1)}, u32[]{:S(2)}, u32[]{:S(2)}) async-start(bf16[8,80,640]{2,1,0:T(8,128)(2,1)} %shard_map.214), calls=%async_computation.4 | async-start | bytes 1638400 | tf_op jit(solution)/shard_map/all_to_all | solution.py:838
  289.4 1.6 fusion.2
  291.1 2.8 fusion.6
  293.9 7.5 %all-to-all-done.2.ref = bf16[8,80,640]{2,1,0:T(8,128)(2,1)S(1)} async-done(((bf16[8,80,640]{2,1,0:T(8,128)(2,1)}), bf16[8,80,640]{2,1,0:T(8,128)(2,1)S(1)}, u32[]{:S(2)}, u32[]{:S(2)}) %all-to-all-start.2) | async-done | bytes 819232 | tf_op jit(solution)/shard_map/all_to_all | solution.py:838
  301.4 1.1 copy-done.5
  302.5 1.7 shard_map.215
  305.3 0.6 reduce.1
  (120 shorter events, 4.5 us)
Async XLA Ops:
  7.2 3.6 %copy-start.25 = (bf16[48,3072]{1,0:T(8,128)(2,1)S(1)}, bf16[48,3072]{1,0:T(8,128)(2,1)}, u32[]{:S(2)}) copy-start(bf16[48,3072]{1,0:T(8,128)(2,1)} %param.23) | copy-start | bytes 884740
  11.6 5.8 %copy-start.26 = (f32[1536]{0:T(1024)S(1)}, f32[1536]{0:T(1024)}, u32[]{:S(2)}) copy-start(f32[1536]{0:T(1024)} %param.15) | copy-start | bytes 18436
  11.6 20.6 %copy-start = (bf16[256,1536]{1,0:T(8,128)(2,1)S(1)}, bf16[256,1536]{1,0:T(8,128)(2,1)}, u32[]{:S(2)}) copy-start(bf16[256,1536]{1,0:T(8,128)(2,1)} %hidden_ref.1) | copy-start | bytes 2359300
  13.6 18.5 %all-to-all-start = ((bf16[8,48,1408]{2,1,0:T(8,128)(2,1)}), bf16[8,48,1408]{2,1,0:T(8,128)(2,1)S(1)}, u32[]{:S(2)}, u32[]{:S(2)}) async-start(bf16[8,48,1408]{2,1,0:T(8,128)(2,1)} %pad_dynamic-update-slice_fusion), calls=%async_computation | async-start | bytes 2162688 | tf_op jit(solution)/shard_map/all_to_all | solution.py:838
  17.4 64.4 %all-gather.3.cloned.1.call-start = ((), (), s32[]{:S(2)}) async-start(), calls=%async_computation.5 | async-start | bytes 7077888 | tf_op jit(solution)/shard_map/all_gather | solution.py:841
  32.2 1.2 copy-start.1
  32.2 2.0 copy-start.2
  33.4 95.6 %all-gather.5.cloned.1.call-start = ((), (), s32[]{:S(2)}) async-start(), calls=%async_computation.6 | async-start | bytes 7077888 | tf_op jit(solution)/shard_map/all_gather | solution.py:841
  35.2 6.1 %copy-start.29 = (f32[48]{0:T(128)S(1)}, f32[48]{0:T(128)}, u32[]{:S(2)}) copy-start(f32[48]{0:T(128)} %param.19) | copy-start | bytes 580
  35.2 6.2 %copy-start.30 = (f32[48]{0:T(128)S(1)}, f32[48]{0:T(128)}, u32[]{:S(2)}) copy-start(f32[48]{0:T(128)} %param.20) | copy-start | bytes 580
  35.2 6.2 %copy-start.31 = (f32[48]{0:T(128)S(1)}, f32[48]{0:T(128)}, u32[]{:S(2)}) copy-start(f32[48]{0:T(128)} %param.21) | copy-start | bytes 580
  35.2 7.2 %slice-start.3 = ((f32[3328]{0:T(1024)}), f32[3072]{0:T(1024)S(1)}, s32[]{:S(2)}) async-start(f32[3328]{0:T(1024)} %param.18), calls=%async_computation.12 | async-start | bytes 24576 | tf_op jit(solution)/shard_map/slice | solution.py:886
  35.2 7.3 %slice-start.2 = ((f32[3328]{0:T(1024)}), f32[256]{0:T(256)S(1)}, s32[]{:S(2)}) async-start(f32[3328]{0:T(1024)} %param.18), calls=%async_computation.11 | async-start | bytes 2048 | tf_op jit(solution)/shard_map/slice | solution.py:886
  35.3 190.9 %reduce-scatter.3.cloned.1.call-start = ((), (), s32[]{:S(2)}) async-start(), calls=%async_computation.7 | async-start | bytes 7077888 | tf_op jit(solution)/shard_map/reduce_scatter | solution.py:844
  37.4 36.6 %slice-start.1 = ((f32[4,3328]{1,0:T(4,128)}), f32[4,3072]{1,0:T(4,128)S(1)}, s32[]{:S(2)}) async-start(f32[4,3328]{1,0:T(4,128)} %param.17), calls=%async_computation.10 | async-start | bytes 98304 | tf_op jit(solution)/shard_map/slice | solution.py:884
  37.4 36.6 %slice-start = ((f32[4,3328]{1,0:T(4,128)}), f32[4,256]{1,0:T(4,128)S(1)}, s32[]{:S(2)}) async-start(f32[4,3328]{1,0:T(4,128)} %param.17), calls=%async_computation.9 | async-start | bytes 8192 | tf_op jit(solution)/shard_map/slice | solution.py:884
  37.4 30.1 %collective-permute-start.2 = (bf16[400,512]{1,0:T(8,128)(2,1)}, bf16[400,512]{1,0:T(8,128)(2,1)S(1)}, u32[]{:S(2)}, u32[]{:S(2)}) collective-permute-start(bf16[400,512]{1,0:T(8,128)(2,1)} %shard_map.205.refs_1_), channel_id=1, source_target_pairs={{0,12},{4,8},{8,4},{12,0},{1,13},{5,9},{9,5},{13,1},{2,14},{6,10},... | collective-permute-start | bytes 1228808 | tf_op jit(solution)/shard_map/ppermute | solution.py:26
  37.8 35.2 %collective-permute-start.1 = (bf16[400,512]{1,0:T(8,128)(2,1)}, bf16[400,512]{1,0:T(8,128)(2,1)S(1)}, u32[]{:S(2)}, u32[]{:S(2)}) collective-permute-start(bf16[400,512]{1,0:T(8,128)(2,1)} %shard_map.205.refs_1_), channel_id=1, source_target_pairs={{0,8},{4,12},{8,0},{12,4},{1,9},{5,13},{9,1},{13,5},{2,10},{6,14},... | collective-permute-start | bytes 1228808 | tf_op jit(solution)/shard_map/ppermute | solution.py:26
  41.3 31.7 %collective-permute-start = (bf16[400,512]{1,0:T(8,128)(2,1)}, bf16[400,512]{1,0:T(8,128)(2,1)S(1)}, u32[]{:S(2)}, u32[]{:S(2)}) collective-permute-start(bf16[400,512]{1,0:T(8,128)(2,1)} %shard_map.205.refs_1_), channel_id=1, source_target_pairs={{0,4},{4,0},{8,12},{12,8},{1,5},{5,1},{9,13},{13,9},{2,6},{6,2},{1... | collective-permute-start | bytes 1228808 | tf_op jit(solution)/shard_map/ppermute | solution.py:26
  67.5 6.5 %copy-start.12 = (bf16[400,512]{1,0:T(8,128)(2,1)}, bf16[400,512]{1,0:T(8,128)(2,1)S(1)}, u32[]{:S(2)}) copy-start(bf16[400,512]{1,0:T(8,128)(2,1)S(1)} %collective-permute-done.2.refs_4_.refs_2_) | copy-start | bytes 1228804
  73.0 1.0 copy-start.14
  73.0 1.0 copy-start.16
  73.9 7.8 %collective-permute-start.3 = (bf16[1536,128]{1,0:T(8,128)(2,1)}, bf16[1536,128]{1,0:T(8,128)(2,1)}, u32[]{:S(2)}, u32[]{:S(2)}) collective-permute-start(bf16[1536,128]{1,0:T(8,128)(2,1)} %pad_maximum_fusion), channel_id=1, source_target_pairs={{0,1},{1,0},{2,3},{3,2},{4,5},{5,4},{6,7},{7,6},{8,9},{9,8},{10,11... | collective-permute-start | bytes 1179656 | tf_op jit(solution)/shard_map/ppermute | solution.py:22
  74.0 7.7 %copy-start.11 = (bf16[400,512]{1,0:T(8,128)(2,1)S(1)}, bf16[400,512]{1,0:T(8,128)(2,1)}, u32[]{:S(2)}) copy-start(bf16[400,512]{1,0:T(8,128)(2,1)} %shard_map.205.refs_1_) | copy-start | bytes 1228804
  76.0 41.7 %collective-permute-start.6 = (bf16[384,768]{1,0:T(8,128)(2,1)}, bf16[384,768]{1,0:T(8,128)(2,1)}, u32[]{:S(2)}, u32[]{:S(2)}) collective-permute-start(bf16[384,768]{1,0:T(8,128)(2,1)} %shard_map.207.refs_3_), channel_id=1, source_target_pairs={{0,12},{4,8},{8,4},{12,0},{1,13},{5,9},{9,5},{13,1},{2,14},{6,10},... | collective-permute-start | bytes 1769480 | tf_op jit(solution)/shard_map/ppermute | solution.py:26
  77.6 51.5 %collective-permute-start.5 = (bf16[384,768]{1,0:T(8,128)(2,1)}, bf16[384,768]{1,0:T(8,128)(2,1)}, u32[]{:S(2)}, u32[]{:S(2)}) collective-permute-start(bf16[384,768]{1,0:T(8,128)(2,1)} %shard_map.207.refs_3_), channel_id=1, source_target_pairs={{0,8},{4,12},{8,0},{12,4},{1,9},{5,13},{9,1},{13,5},{2,10},{6,14},... | collective-permute-start | bytes 1769480 | tf_op jit(solution)/shard_map/ppermute | solution.py:26
  81.8 47.3 %collective-permute-start.4 = (bf16[384,768]{1,0:T(8,128)(2,1)}, bf16[384,768]{1,0:T(8,128)(2,1)}, u32[]{:S(2)}, u32[]{:S(2)}) collective-permute-start(bf16[384,768]{1,0:T(8,128)(2,1)} %shard_map.207.refs_3_), channel_id=1, source_target_pairs={{0,4},{4,0},{8,12},{12,8},{1,5},{5,1},{9,13},{13,9},{2,6},{6,2},{1... | collective-permute-start | bytes 1769480 | tf_op jit(solution)/shard_map/ppermute | solution.py:26
  81.8 1.0 copy-start.13
  82.8 1.0 copy-start.15
  83.8 1.0 copy-start.17
  129.1 1.1 copy-start.18
  146.1 0.7 copy-start.27
  146.1 143.3 %reduce-scatter.5.cloned.1.call-start = ((), (), s32[]{:S(2)}) async-start(), calls=%async_computation.8 | async-start | bytes 7077888 | tf_op jit(solution)/shard_map/reduce_scatter | solution.py:844
  146.8 1.2 collective-permute-start.7
  148.0 3.7 %collective-permute-start.10 = (f32[16,256]{1,0:T(8,128)S(1)}, f32[16,256]{1,0:T(8,128)S(1)}, u32[]{:S(2)}, u32[]{:S(2)}) collective-permute-start(f32[16,256]{1,0:T(8,128)S(1)} %add.93), channel_id=1, source_target_pairs={{0,16},{2,18},{16,0},{18,2},{1,17},{3,19},{17,1},{19,3},{4,20},{6,... | collective-permute-start | bytes 49160 | tf_op jit(solution)/shard_map/ppermute | solution.py:26
  148.7 3.7 %collective-permute-start.9 = (f32[16,256]{1,0:T(8,128)S(1)}, f32[16,256]{1,0:T(8,128)S(1)}, u32[]{:S(2)}, u32[]{:S(2)}) collective-permute-start(f32[16,256]{1,0:T(8,128)S(1)} %add.93), channel_id=1, source_target_pairs={{0,2},{2,0},{16,18},{18,16},{1,3},{3,1},{17,19},{19,17},{4,6},{6,4... | collective-permute-start | bytes 49160 | tf_op jit(solution)/shard_map/ppermute | solution.py:26
  150.0 4.6 %collective-permute-start.8 = (f32[16,256]{1,0:T(8,128)S(1)}, f32[16,256]{1,0:T(8,128)S(1)}, u32[]{:S(2)}, u32[]{:S(2)}) collective-permute-start(f32[16,256]{1,0:T(8,128)S(1)} %add.93), channel_id=1, source_target_pairs={{0,18},{2,16},{16,2},{18,0},{1,19},{3,17},{17,3},{19,1},{4,22},{6,... | collective-permute-start | bytes 49160 | tf_op jit(solution)/shard_map/ppermute | solution.py:26
  154.7 22.9 %copy-start.20 = (bf16[1536,768]{1,0:T(8,128)(2,1)S(1)}, bf16[1536,768]{1,0:T(8,128)(2,1)}, u32[]{:S(2)}) copy-start(bf16[1536,768]{1,0:T(8,128)(2,1)} %get-tuple-element.57.refs_5_) | copy-start | bytes 7077892
  154.7 22.9 %copy-start.21 = (bf16[1536,384]{1,0:T(8,128)(2,1)S(1)}, bf16[1536,384]{1,0:T(8,128)(2,1)}, u32[]{:S(2)}) copy-start(bf16[1536,384]{1,0:T(8,128)(2,1)} %get-tuple-element.58.refs_6_) | copy-start | bytes 3538948
  172.8 44.7 %collective-permute-start.11 = (bf16[384,768]{1,0:T(8,128)(2,1)}, bf16[384,768]{1,0:T(8,128)(2,1)S(1)}, u32[]{:S(2)}, u32[]{:S(2)}) collective-permute-start(bf16[384,768]{1,0:T(8,128)(2,1)} %get-tuple-element.66), channel_id=1, source_target_pairs={{0,8},{4,12},{8,0},{12,4},{1,9},{5,13},{9,1},{13,5},{2,10},{6,14},... | collective-permute-start | bytes 1769480 | tf_op jit(solution)/shard_map/ppermute | solution.py:26
  176.1 50.1 %collective-permute-start.12 = (bf16[384,768]{1,0:T(8,128)(2,1)}, bf16[384,768]{1,0:T(8,128)(2,1)S(1)}, u32[]{:S(2)}, u32[]{:S(2)}) collective-permute-start(bf16[384,768]{1,0:T(8,128)(2,1)} %get-tuple-element.67), channel_id=1, source_target_pairs={{0,12},{4,8},{8,4},{12,0},{1,13},{5,9},{9,5},{13,1},{2,14},{6,10},... | collective-permute-start | bytes 1769480 | tf_op jit(solution)/shard_map/ppermute | solution.py:26
  176.6 49.6 %collective-permute-start.13 = (bf16[384,768]{1,0:T(8,128)(2,1)}, bf16[384,768]{1,0:T(8,128)(2,1)}, u32[]{:S(2)}, u32[]{:S(2)}) collective-permute-start(bf16[384,768]{1,0:T(8,128)(2,1)} %get-tuple-element.68), channel_id=1, source_target_pairs={{0,4},{4,0},{8,12},{12,8},{1,5},{5,1},{9,13},{13,9},{2,6},{6,2},{1... | collective-permute-start | bytes 1769480 | tf_op jit(solution)/shard_map/ppermute | solution.py:26
  177.6 0.7 copy-start.22
  217.5 8.7 %copy-start.6 = (bf16[384,768]{1,0:T(8,128)(2,1)}, bf16[384,768]{1,0:T(8,128)(2,1)S(1)}, u32[]{:S(2)}) copy-start(bf16[384,768]{1,0:T(8,128)(2,1)S(1)} %collective-permute-done.11.refs_6_.refs_1_) | copy-start | bytes 1769476
  226.2 0.8 copy-start.8
  227.0 1.0 copy-start.24
  228.0 1.7 collective-permute-start.14
  229.7 0.7 copy-start.28
  230.4 2.1 copy-start.7
  230.4 2.1 copy-start.9
  232.6 1.0 copy-start.10
  233.6 1.2 copy-start.19
  237.1 46.0 %all-to-all-start.1 = ((bf16[8,48,768]{2,1,0:T(8,128)(2,1)}), bf16[8,48,768]{2,1,0:T(8,128)(2,1)S(1)}, u32[]{:S(2)}, u32[]{:S(2)}) async-start(bf16[8,48,768]{2,1,0:T(8,128)(2,1)} %shard_map.213), calls=%async_computation.3 | async-start | bytes 1179648 | tf_op jit(solution)/shard_map/all_to_all | solution.py:838
  240.6 19.2 %collective-permute-start.15 = (bf16[432,512]{1,0:T(8,128)(2,1)}, bf16[432,512]{1,0:T(8,128)(2,1)S(1)}, u32[]{:S(2)}, u32[]{:S(2)}) collective-permute-start(bf16[432,512]{1,0:T(8,128)(2,1)} %get-tuple-element.77), channel_id=1, source_target_pairs={{0,4},{4,0},{8,12},{12,8},{1,5},{5,1},{9,13},{13,9},{2,6},{6,2},{1... | collective-permute-start | bytes 1327112 | tf_op jit(solution)/shard_map/ppermute | solution.py:26
  240.7 32.1 %collective-permute-start.16 = (bf16[432,512]{1,0:T(8,128)(2,1)}, bf16[432,512]{1,0:T(8,128)(2,1)S(1)}, u32[]{:S(2)}, u32[]{:S(2)}) collective-permute-start(bf16[432,512]{1,0:T(8,128)(2,1)} %get-tuple-element.78), channel_id=1, source_target_pairs={{0,8},{4,12},{8,0},{12,4},{1,9},{5,13},{9,1},{13,5},{2,10},{6,14},... | collective-permute-start | bytes 1327112 | tf_op jit(solution)/shard_map/ppermute | solution.py:26
  242.9 40.1 %collective-permute-start.17 = (bf16[432,512]{1,0:T(8,128)(2,1)}, bf16[432,512]{1,0:T(8,128)(2,1)}, u32[]{:S(2)}, u32[]{:S(2)}) collective-permute-start(bf16[432,512]{1,0:T(8,128)(2,1)} %get-tuple-element.79), channel_id=1, source_target_pairs={{0,12},{4,8},{8,4},{12,0},{1,13},{5,9},{9,5},{13,1},{2,14},{6,10},... | collective-permute-start | bytes 1327112 | tf_op jit(solution)/shard_map/ppermute | solution.py:26
  283.1 2.4 copy-start.4
  285.5 15.9 %all-to-all-start.2 = ((bf16[8,80,640]{2,1,0:T(8,128)(2,1)}), bf16[8,80,640]{2,1,0:T(8,128)(2,1)S(1)}, u32[]{:S(2)}, u32[]{:S(2)}) async-start(bf16[8,80,640]{2,1,0:T(8,128)(2,1)} %shard_map.214), calls=%async_computation.4 | async-start | bytes 1638400 | tf_op jit(solution)/shard_map/all_to_all | solution.py:838
  289.4 1.7 copy-start.23
  293.9 10.2 %copy-start.3 = (bf16[256,1536]{1,0:T(8,128)(2,1)}, bf16[256,1536]{1,0:T(8,128)(2,1)S(1)}, u32[]{:S(2)}) copy-start(bf16[256,1536]{1,0:T(8,128)(2,1)S(1)} %get-tuple-element.90.refs_0_) | copy-start | bytes 2359300
  301.4 1.1 copy-start.5
Sparse Core Ops, SparseCore 0:
  33.6 45.6 all-gather.2
  81.7 45.5 all-gather.4
  146.3 62.6 reduce-scatter.2
  227.1 61.0 reduce-scatter.4

commit v5 on v4

--- a/solution.py
+++ b/solution.py
@@ -728,6 +728,36 @@
     )(early, owned, *waits)
 
 
+def pack_weights(in_weight, out_weight, ranks, heads):
+    rows, inner_all = out_weight.shape
+    inner = inner_all // ranks
+    first_step = in_weight.shape[1] - ranks * heads
+    states = (first_step - 2 * inner_all) // 2
+
+    def run(in_ref, weight_ref, conv_ref, late_ref):
+        steps = in_ref[:, first_step:].astype(jnp.float32)
+        steps = jnp.concatenate([steps, jnp.zeros((rows, LANES - steps.shape[1]), jnp.float32)], axis=1)
+        lane = lax.broadcasted_iota(jnp.int32, (rows, LANES), 1)
+        for rank in range(ranks):
+            own = slice(rank * inner, (rank + 1) * inner)
+            late_ref[rank, :, :inner] = in_ref[:, own]
+            late_ref[rank, :, inner:] = weight_ref[:, own]
+            conv_ref[rank, :, :inner] = in_ref[:, inner_all + rank * inner : inner_all + (rank + 1) * inner]
+            state = 2 * inner_all + (rank % 2) * states
+            conv_ref[rank, :, inner : inner + states] = in_ref[:, state : state + states]
+            moved = pltpu.roll(steps, (LANES - rank * heads) % LANES, 1)
+            conv_ref[rank, :, inner + states :] = jnp.where(lane < heads, moved, 0.0).astype(LOW)
+
+    return pl.pallas_call(
+        run,
+        out_shape=[
+            jax.ShapeDtypeStruct((ranks, rows, inner + states + LANES), LOW),
+            jax.ShapeDtypeStruct((ranks, rows, 2 * inner), LOW),
+        ],
+        cost_estimate=pl.CostEstimate(flops=int(1e9), bytes_accessed=1 << 20, transcendentals=0),
+    )(in_weight, out_weight)
+
+
 def pack_steps(value, start, width):
     rows = value.shape[0]
 
@@ -843,37 +873,25 @@
     def scatter_far(value):
         return lax.psum_scatter(value, PLANE, scatter_dimension=0, tiled=True)
 
-    def by_rank(columns):
-        return columns.reshape(rows, ranks, -1).transpose(1, 0, 2)
-
-    first_state = 2 * inner_all
-    first_step = first_state + 2 * states
-    state_columns = in_weight[:, first_state:first_step].reshape(rows, 2, states).transpose(1, 0, 2)
-    packed = jnp.concatenate(
-        [
-            by_rank(in_weight[:, :inner_all]),
-            by_rank(out_weight),
-            by_rank(in_weight[:, inner_all:first_state]),
-            jnp.tile(state_columns, (ranks // 2, 1, 1)),
-            jnp.pad(by_rank(in_weight[:, first_step:]), ((0, 0), (0, 0), (0, LANES - heads))),
-        ],
-        axis=2,
-    )
-    plane_weights = exchange(packed).reshape(ranks * rows, -1)
+    packed_conv, packed_late = pack_weights(in_weight, out_weight, ranks, heads)
+    conv_plane = exchange(packed_conv).reshape(ranks * rows, -1)
+    (late_packed,) = hold([packed_late], [conv_plane])
+    late_plane = exchange(late_packed).reshape(ranks * rows, -1)
     if direct:
-        conv_pieces = gather_rows(pack_steps(plane_weights, 2 * inner, inner + states))
+        conv_pieces = gather_rows(pack_steps(conv_plane, 0, inner + states))
     else:
-        conv_pieces = [pack_steps(piece, 0, inner + states) for piece in gather_rows(plane_weights[:, 2 * inner :])]
+        conv_pieces = [pack_steps(piece, 0, inner + states) for piece in gather_rows(conv_plane)]
     other_states = swap(
         jnp.concatenate([piece[:piece_rows, inner : inner + states] for piece in conv_pieces], axis=0)
     )
-    late_pieces = gather_rows(columns_of(plane_weights, 0, 2 * inner, conv_pieces[1:]))
+    (late_columns,) = hold([late_plane], conv_pieces[1:2])
+    late_pieces = gather_rows(late_columns)
 
     stream = hidden_in.astype(jnp.float32)
     scale = lax.rsqrt(jnp.mean(stream * stream, axis=-1, keepdims=True) + EPSILON)
     valid = (jnp.arange(length) < lengths[0])[:, None]
     own_upstream = jnp.where(valid, cotangent, jnp.zeros_like(cotangent))
-    own_normed = copies(norm_kernel, (), hidden_in, (pre_gain[None],), 1, (plane_weights,))
+    own_normed = copies(norm_kernel, (), hidden_in, (pre_gain[None],), 1, (conv_plane,))
     normed = gather_tokens(own_normed)
     upstream = gather_tokens(copies(mask_kernel, (lengths,), cotangent, (), 1, (own_normed,)))
 

time: 314 us -> 307 us (0.978)
  local copies, waits for them, and re-layouts: 20.5 us -> 13.3 us
  waiting for transfers between devices: 131 us -> 127 us
  starting transfers between devices: 33 us -> 36.7 us
    all_to_all x3 -> x4, waiting for transfers between devices: 22.2 us -> 15.9 us  [exchange(): return lax.all_to_all(value, PLANE, split_axis=0, concat_axis=0, tiled=True)]
    unnamed x69 -> x58, local copies, waits for them, and re-layouts: 14.2 us -> 8.78 us
    all_gather x2, waiting for transfers between devices: 0.01 us -> 5.28 us  [gather_tokens(): return lax.all_gather(value, PLANE, axis=0, tiled=True)]
    all_to_all x3 -> x4, starting transfers between devices: 11.1 us -> 14.8 us  [exchange(): return lax.all_to_all(value, PLANE, split_axis=0, concat_axis=0, tiled=True)]
  transfers between devices with their start and end apart: 25 -> 26, of which waited for: 15 -> 17; matrix products, arithmetic and copies ran while one was open for 2% -> 3% of each run, Pallas kernels for 28% -> 28%
where the time goes in v5:
time: 307 us; the launch traced here: 305 us
  waiting for transfers between devices  127 us (41%)
  Pallas kernels  107 us (35%)
  starting transfers between devices  36.7 us (12%)
  between operations  14.7 us (5%)
  local copies, waits for them, and re-layouts  13.3 us (4%)
  other arithmetic  6.68 us (2%)
    ppermute x15, waiting for transfers between devices, cross(): return lax.ppermute(value, axes, [(i, i ^ distance) for i in range(count)])  103 us
    pallas_call x4, Pallas kernels, run_slots(): pl.pallas_call(run, grid_spec=pltpu.PrefetchScalarGridSpec(num_scalar_pre...  92.2 us
    ppermute x15, starting transfers between devices, cross(): return lax.ppermute(value, axes, [(i, i ^ distance) for i in range(count)])  21.3 us
    all_to_all x4, waiting for transfers between devices, exchange(): return lax.all_to_all(value, PLANE, split_axis=0, concat_axis=0, tiled=True)  15.9 us
    all_to_all x4, starting transfers between devices, exchange(): return lax.all_to_all(value, PLANE, split_axis=0, concat_axis=0, tiled=True)  14.8 us
    unnamed x58, local copies, waits for them, and re-layouts  8.78 us
  transfers between devices with their start and end apart: 26, of which 17 were waited for; matrix products, arithmetic and copies ran while one was open for 3% of the time, Pallas kernels for 28%

profile of v5, /device:TPU:16, one launch (start us, length us, event | category | flops | bytes accessed | tf_op | source)
XLA Modules:
  0.0 305.4 jit_solution(131904609163279203)
XLA Ops:
  7.2 2.3 shard_map.203
  9.5 3.7 %all-to-all-start = ((bf16[8,48,640]{2,1,0:T(8,128)(2,1)}), bf16[8,48,640]{2,1,0:T(8,128)(2,1)S(1)}, u32[]{:S(2)}, u32[]{:S(2)}) async-start(bf16[8,48,640]{2,1,0:T(8,128)(2,1)} %get-tuple-element.51), calls=%async_computation | async-start | bytes 983040 | tf_op jit(solution)/shard_map/all_to_all | solution.py:868
  13.3 8.4 %all-to-all-done = bf16[8,48,640]{2,1,0:T(8,128)(2,1)S(1)} async-done(((bf16[8,48,640]{2,1,0:T(8,128)(2,1)}), bf16[8,48,640]{2,1,0:T(8,128)(2,1)S(1)}, u32[]{:S(2)}, u32[]{:S(2)}) %all-to-all-start) | async-done | bytes 491552 | tf_op jit(solution)/shard_map/all_to_all | solution.py:868
  21.7 1.2 shard_map.204.refs_0_
  23.6 1.0 shard_map.205
  24.7 1.9 shard_map.206.refs_1_
  26.5 0.4 collective-permute-start.2
  27.0 3.5 %collective-permute-start.1 = (bf16[400,512]{1,0:T(8,128)(2,1)}, bf16[400,512]{1,0:T(8,128)(2,1)}, u32[]{:S(2)}, u32[]{:S(2)}) collective-permute-start(bf16[400,512]{1,0:T(8,128)(2,1)} %shard_map.206.refs_1_), channel_id=1, source_target_pairs={{0,8},{4,12},{8,0},{12,4},{1,9},{5,13},{9,1},{13,5},{2,10},{6,14},... | collective-permute-start | bytes 1228808 | tf_op jit(solution)/shard_map/ppermute | solution.py:26
  30.6 0.9 slice.44
  31.6 3.7 %all-to-all-start.1 = ((bf16[8,48,768]{2,1,0:T(8,128)(2,1)}), bf16[8,48,768]{2,1,0:T(8,128)(2,1)S(1)}, u32[]{:S(2)}, u32[]{:S(2)}) async-start(bf16[8,48,768]{2,1,0:T(8,128)(2,1)} %shard_map.208), calls=%async_computation.1 | async-start | bytes 1179648 | tf_op jit(solution)/shard_map/all_to_all | solution.py:868
  35.3 21.4 %collective-permute-done.2.refs_4_ = bf16[400,512]{1,0:T(8,128)(2,1)S(1)} collective-permute-done((bf16[400,512]{1,0:T(8,128)(2,1)}, bf16[400,512]{1,0:T(8,128)(2,1)S(1)}, u32[]{:S(2)}, u32[]{:S(2)}) %collective-permute-start.2) | collective-permute-done | bytes 409632 | tf_op jit(solution)/shard_map/ppermute | solution.py:26
  56.7 5.5 %collective-permute-done.1.refs_3_ = bf16[400,512]{1,0:T(8,128)(2,1)} collective-permute-done((bf16[400,512]{1,0:T(8,128)(2,1)}, bf16[400,512]{1,0:T(8,128)(2,1)}, u32[]{:S(2)}, u32[]{:S(2)}) %collective-permute-start.1) | collective-permute-done | bytes 409632 | tf_op jit(solution)/shard_map/ppermute | solution.py:26
  62.2 0.9 slice.46
  63.1 0.9 pad_maximum_fusion
  64.0 0.8 slice.37
  65.0 0.8 dynamic_slice.27
  66.1 0.8 copy-done.1
  66.9 1.6 collective-permute-start.6
  68.5 4.3 %collective-permute-start.5 = (bf16[384,768]{1,0:T(8,128)(2,1)}, bf16[384,768]{1,0:T(8,128)(2,1)}, u32[]{:S(2)}, u32[]{:S(2)}) collective-permute-start(bf16[384,768]{1,0:T(8,128)(2,1)} %shard_map.209.refs_3_), channel_id=1, source_target_pairs={{0,8},{4,12},{8,0},{12,4},{1,9},{5,13},{9,1},{13,5},{2,10},{6,14},... | collective-permute-start | bytes 1769480 | tf_op jit(solution)/shard_map/ppermute | solution.py:26
  72.8 2.2 all-gather.3.cloned.1.call-done.refs_0_.refs_4_
  75.0 1.0 copy-done.7
  76.0 19.1 %shard_map.207 = (f32[2048,768]{1,0:T(8,128)}, f32[2048,384]{1,0:T(8,128)}, bf16[1536,768]{1,0:T(8,128)(2,1)}) custom-call(s32[9]{0:T(128)S(1)} %stack.39.place_ref, bf16[2048,1536]{1,0:T(8,128)(2,1)} %all-gather.3.cloned.1.call-done.refs_0_.refs_4_, bf16[400,512]{1,0:T(8,128)(2,1)S(1)} %copy-done.16, bf16[400,512]{1,0:T(8,128)(2,1)S(1)} %copy-done.7, ...), custom_call_target="tpu_custom_call" | custom-call | flops 12000000000 | bytes 1048576 | tf_op jit(solution)/shard_map/pallas_call | solution.py:569
  95.1 13.5 %collective-permute-done.6.refs_6_ = bf16[384,768]{1,0:T(8,128)(2,1)} collective-permute-done((bf16[384,768]{1,0:T(8,128)(2,1)}, bf16[384,768]{1,0:T(8,128)(2,1)}, u32[]{:S(2)}, u32[]{:S(2)}) %collective-permute-start.6) | collective-permute-done | bytes 589856 | tf_op jit(solution)/shard_map/ppermute | solution.py:26
  108.6 11.4 %collective-permute-done.5.refs_5_ = bf16[384,768]{1,0:T(8,128)(2,1)} collective-permute-done((bf16[384,768]{1,0:T(8,128)(2,1)}, bf16[384,768]{1,0:T(8,128)(2,1)}, u32[]{:S(2)}, u32[]{:S(2)}) %collective-permute-start.5) | collective-permute-done | bytes 589856 | tf_op jit(solution)/shard_map/ppermute | solution.py:26
  120.0 3.0 all-gather.5.cloned.1.call-done.refs_1_
  123.0 16.0 %shard_map.210 = (f32[2048,384]{1,0:T(8,128)}, f32[2048,384]{1,0:T(8,128)}, bf16[2048,1536]{1,0:T(8,128)(2,1)}, f32[16,256]{1,0:T(8,128)}, bf16[1536,384]{1,0:T(8,128)(2,1)}) custom-call(s32[9]{0:T(128)S(1)} %stack.39.place_ref, bf16[2048,1536]{1,0:T(8,128)(2,1)} %all-gather.3.cloned.1.call-done.refs_0_.refs_4_, ...), custom_call_target="tpu_custom_call" | custom-call | flops 14000000000 | bytes 1048576 | tf_op jit(solution)/shard_map/pallas_call | solution.py:569
  139.3 0.5 copy-done.24
  140.0 0.9 collective-permute-done.7
  140.9 1.5 collective-permute-start.10
  142.4 0.6 collective-permute-start.9
  142.9 1.5 collective-permute-start.8
  144.7 1.5 collective-permute-done.9
  146.1 1.5 collective-permute-done.8
  147.6 18.0 %shard_map.211 = (bf16[2048,384]{1,0:T(8,128)(2,1)}, f32[2048,384]{1,0:T(8,128)}, f32[8,384]{1,0:T(8,128)}, bf16[384,768]{1,0:T(8,128)(2,1)}, bf16[384,768]{1,0:...) custom-call(s32[9]{0:T(128)S(1)} %stack.39.place_ref, ...), custom_call_target="tpu_custom_call" | custom-call | flops 16000000000 | bytes 1048576 | tf_op jit(solution)/shard_map/pallas_call | solution.py:569
  165.6 0.6 collective-permute-start.11
  166.1 2.5 collective-permute-start.12
  168.6 1.4 collective-permute-start.13
  170.0 0.7 copy-done.20
  170.7 39.1 %shard_map.212 = (bf16[2048,1536]{1,0:T(8,128)(2,1)}, bf16[1536,128]{1,0:T(8,128)(2,1)}, bf16[432,512]{1,0:T(8,128)(2,1)}, bf16[432,512]{1,0:T(8,128)(2,1)}, bf1...) custom-call(s32[9]{0:T(128)S(1)} %stack.39.place_ref, f32[2048,768]{1,0:T(8,128)} %get-tuple-element.56.refs_0_, ...), custom_call_target="tpu_custom_call" | custom-call | flops 30000001024 | bytes 1048576 | tf_op jit(solution)/shard_map/pallas_call | solution.py:569
  209.9 9.1 %collective-permute-done.12.refs_7_.refs_2_ = bf16[384,768]{1,0:T(8,128)(2,1)S(1)} collective-permute-done((bf16[384,768]{1,0:T(8,128)(2,1)}, bf16[384,768]{1,0:T(8,128)(2,1)S(1)}, u32[]{:S(2)}, u32[]{:S(2)}) %collective-permute-start.12) | collective-permute-done | bytes 589856 | tf_op jit(solution)/shard_map/ppermute | solution.py:26
  219.0 0.8 copy-done.12
  219.9 1.0 copy-done.22
  220.9 1.7 collective-permute-done.14.refs_4_
  222.6 0.7 copy-done.25
  223.3 2.1 shard_map.214
  225.4 1.0 copy-done.14
  226.5 1.1 copy-done.17
  227.6 2.3 shard_map.215
  229.9 3.6 %all-to-all-start.2 = ((bf16[8,48,768]{2,1,0:T(8,128)(2,1)}), bf16[8,48,768]{2,1,0:T(8,128)(2,1)S(1)}, u32[]{:S(2)}, u32[]{:S(2)}) async-start(bf16[8,48,768]{2,1,0:T(8,128)(2,1)} %shard_map.215), calls=%async_computation.4 | async-start | bytes 1179648 | tf_op jit(solution)/shard_map/all_to_all | solution.py:868
  233.5 1.2 collective-permute-start.16
  234.7 2.3 collective-permute-start.17
  237.0 14.5 %collective-permute-done.15.refs_1_ = bf16[432,512]{1,0:T(8,128)(2,1)S(1)} collective-permute-done((bf16[432,512]{1,0:T(8,128)(2,1)}, bf16[432,512]{1,0:T(8,128)(2,1)S(1)}, u32[]{:S(2)}, u32[]{:S(2)}) %collective-permute-start.15) | collective-permute-done | bytes 442400 | tf_op jit(solution)/shard_map/ppermute | solution.py:26
  251.5 4.0 %collective-permute-done.16.refs_2_ = bf16[432,512]{1,0:T(8,128)(2,1)} collective-permute-done((bf16[432,512]{1,0:T(8,128)(2,1)}, bf16[432,512]{1,0:T(8,128)(2,1)}, u32[]{:S(2)}, u32[]{:S(2)}) %collective-permute-start.16) | collective-permute-done | bytes 442400 | tf_op jit(solution)/shard_map/ppermute | solution.py:26
  255.5 20.4 %collective-permute-done.17.refs_3_ = bf16[432,512]{1,0:T(8,128)(2,1)} collective-permute-done((bf16[432,512]{1,0:T(8,128)(2,1)}, bf16[432,512]{1,0:T(8,128)(2,1)}, u32[]{:S(2)}, u32[]{:S(2)}) %collective-permute-start.17) | collective-permute-done | bytes 442400 | tf_op jit(solution)/shard_map/ppermute | solution.py:26
  275.9 2.6 shard_map.216
  278.4 3.9 %all-to-all-start.3 = ((bf16[8,80,640]{2,1,0:T(8,128)(2,1)}), bf16[8,80,640]{2,1,0:T(8,128)(2,1)S(1)}, u32[]{:S(2)}, u32[]{:S(2)}) async-start(bf16[8,80,640]{2,1,0:T(8,128)(2,1)} %shard_map.216), calls=%async_computation.5 | async-start | bytes 1638400 | tf_op jit(solution)/shard_map/all_to_all | solution.py:868
  282.3 1.6 fusion.2
  284.0 2.8 fusion.6
  286.9 7.4 %all-to-all-done.3.ref = bf16[8,80,640]{2,1,0:T(8,128)(2,1)S(1)} async-done(((bf16[8,80,640]{2,1,0:T(8,128)(2,1)}), bf16[8,80,640]{2,1,0:T(8,128)(2,1)S(1)}, u32[]{:S(2)}, u32[]{:S(2)}) %all-to-all-start.3) | async-done | bytes 819232 | tf_op jit(solution)/shard_map/all_to_all | solution.py:868
  294.3 1.1 copy-done.9
  295.4 1.7 shard_map.217
  297.1 0.5 slice_bitcast_fusion
  297.6 0.6 div.19
  298.2 0.6 reduce.1
  (103 shorter events, 1.8 us)
Async XLA Ops:
  7.2 6.1 %copy-start.23 = (f32[1536]{0:T(1024)S(1)}, f32[1536]{0:T(1024)}, u32[]{:S(2)}) copy-start(f32[1536]{0:T(1024)} %param.15) | copy-start | bytes 18436
  7.2 14.5 %copy-start = (bf16[256,1536]{1,0:T(8,128)(2,1)S(1)}, bf16[256,1536]{1,0:T(8,128)(2,1)}, u32[]{:S(2)}) copy-start(bf16[256,1536]{1,0:T(8,128)(2,1)} %hidden_ref.1) | copy-start | bytes 2359300
  9.5 12.2 %all-to-all-start = ((bf16[8,48,640]{2,1,0:T(8,128)(2,1)}), bf16[8,48,640]{2,1,0:T(8,128)(2,1)S(1)}, u32[]{:S(2)}, u32[]{:S(2)}) async-start(bf16[8,48,640]{2,1,0:T(8,128)(2,1)} %get-tuple-element.51), calls=%async_computation | async-start | bytes 983040 | tf_op jit(solution)/shard_map/all_to_all | solution.py:868
  13.2 61.8 %all-gather.3.cloned.1.call-start = ((), (), s32[]{:S(2)}) async-start(), calls=%async_computation.6 | async-start | bytes 7077888 | tf_op jit(solution)/shard_map/all_gather | solution.py:871
  21.7 1.2 copy-start.3
  21.7 1.9 copy-start.4
  22.9 100.1 %all-gather.5.cloned.1.call-start = ((), (), s32[]{:S(2)}) async-start(), calls=%async_computation.7 | async-start | bytes 7077888 | tf_op jit(solution)/shard_map/all_gather | solution.py:871
  24.7 5.8 %slice-start.2 = ((f32[3328]{0:T(1024)}), f32[3072]{0:T(1024)S(1)}, s32[]{:S(2)}) async-start(f32[3328]{0:T(1024)} %param.18), calls=%async_computation.12 | async-start | bytes 24576 | tf_op jit(solution)/shard_map/slice | solution.py:904
  26.5 30.1 %collective-permute-start.2 = (bf16[400,512]{1,0:T(8,128)(2,1)}, bf16[400,512]{1,0:T(8,128)(2,1)S(1)}, u32[]{:S(2)}, u32[]{:S(2)}) collective-permute-start(bf16[400,512]{1,0:T(8,128)(2,1)} %shard_map.206.refs_1_), channel_id=1, source_target_pairs={{0,12},{4,8},{8,4},{12,0},{1,13},{5,9},{9,5},{13,1},{2,14},{6,10},... | collective-permute-start | bytes 1228808 | tf_op jit(solution)/shard_map/ppermute | solution.py:26
  27.0 35.2 %collective-permute-start.1 = (bf16[400,512]{1,0:T(8,128)(2,1)}, bf16[400,512]{1,0:T(8,128)(2,1)}, u32[]{:S(2)}, u32[]{:S(2)}) collective-permute-start(bf16[400,512]{1,0:T(8,128)(2,1)} %shard_map.206.refs_1_), channel_id=1, source_target_pairs={{0,8},{4,12},{8,0},{12,4},{1,9},{5,13},{9,1},{13,5},{2,10},{6,14},... | collective-permute-start | bytes 1228808 | tf_op jit(solution)/shard_map/ppermute | solution.py:26
  30.5 32.6 %collective-permute-start = (bf16[400,512]{1,0:T(8,128)(2,1)}, bf16[400,512]{1,0:T(8,128)(2,1)S(1)}, u32[]{:S(2)}, u32[]{:S(2)}) collective-permute-start(bf16[400,512]{1,0:T(8,128)(2,1)} %shard_map.206.refs_1_), channel_id=1, source_target_pairs={{0,4},{4,0},{8,12},{12,8},{1,5},{5,1},{9,13},{13,9},{2,6},{6,2},{1... | collective-permute-start | bytes 1228808 | tf_op jit(solution)/shard_map/ppermute | solution.py:26
  31.5 32.5 %slice-start.1 = ((f32[3328]{0:T(1024)}), f32[256]{0:T(256)S(1)}, s32[]{:S(2)}) async-start(f32[3328]{0:T(1024)} %param.18), calls=%async_computation.11 | async-start | bytes 2048 | tf_op jit(solution)/shard_map/slice | solution.py:904
  31.5 33.3 %copy-start.26 = (f32[48]{0:T(128)S(1)}, f32[48]{0:T(128)}, u32[]{:S(2)}) copy-start(f32[48]{0:T(128)} %param.19) | copy-start | bytes 580
  31.5 33.4 %copy-start.27 = (f32[48]{0:T(128)S(1)}, f32[48]{0:T(128)}, u32[]{:S(2)}) copy-start(f32[48]{0:T(128)} %param.20) | copy-start | bytes 580
  31.5 33.4 %copy-start.28 = (f32[48]{0:T(128)S(1)}, f32[48]{0:T(128)}, u32[]{:S(2)}) copy-start(f32[48]{0:T(128)} %param.21) | copy-start | bytes 580
  31.5 34.5 %slice-start = ((f32[4,3328]{1,0:T(4,128)}), f32[4,256]{1,0:T(4,128)S(1)}, s32[]{:S(2)}) async-start(f32[4,3328]{1,0:T(4,128)} %param.17), calls=%async_computation.10 | async-start | bytes 8192 | tf_op jit(solution)/shard_map/slice | solution.py:902
  31.6 34.5 %all-to-all-start.1 = ((bf16[8,48,768]{2,1,0:T(8,128)(2,1)}), bf16[8,48,768]{2,1,0:T(8,128)(2,1)S(1)}, u32[]{:S(2)}, u32[]{:S(2)}) async-start(bf16[8,48,768]{2,1,0:T(8,128)(2,1)} %shard_map.208), calls=%async_computation.1 | async-start | bytes 1179648 | tf_op jit(solution)/shard_map/all_to_all | solution.py:868
  35.2 39.8 %copy-start.16 = (bf16[400,512]{1,0:T(8,128)(2,1)S(1)}, bf16[400,512]{1,0:T(8,128)(2,1)}, u32[]{:S(2)}) copy-start(bf16[400,512]{1,0:T(8,128)(2,1)} %shard_map.206.refs_1_) | copy-start | bytes 1228804
  35.3 183.8 %reduce-scatter.3.cloned.1.call-start = ((), (), s32[]{:S(2)}) async-start(), calls=%async_computation.8 | async-start | bytes 7077888 | tf_op jit(solution)/shard_map/reduce_scatter | solution.py:874
  63.1 3.0 copy-start.6
  64.0 8.8 %collective-permute-start.3 = (bf16[1536,128]{1,0:T(8,128)(2,1)}, bf16[1536,128]{1,0:T(8,128)(2,1)}, u32[]{:S(2)}, u32[]{:S(2)}) collective-permute-start(bf16[1536,128]{1,0:T(8,128)(2,1)} %pad_maximum_fusion), channel_id=1, source_target_pairs={{0,1},{1,0},{2,3},{3,2},{4,5},{5,4},{6,7},{7,6},{8,9},{9,8},{10,11... | collective-permute-start | bytes 1179656 | tf_op jit(solution)/shard_map/ppermute | solution.py:22
  66.1 0.8 copy-start.1
  66.9 41.7 %collective-permute-start.6 = (bf16[384,768]{1,0:T(8,128)(2,1)}, bf16[384,768]{1,0:T(8,128)(2,1)}, u32[]{:S(2)}, u32[]{:S(2)}) collective-permute-start(bf16[384,768]{1,0:T(8,128)(2,1)} %shard_map.209.refs_3_), channel_id=1, source_target_pairs={{0,12},{4,8},{8,4},{12,0},{1,13},{5,9},{9,5},{13,1},{2,14},{6,10},... | collective-permute-start | bytes 1769480 | tf_op jit(solution)/shard_map/ppermute | solution.py:26
  68.5 51.5 %collective-permute-start.5 = (bf16[384,768]{1,0:T(8,128)(2,1)}, bf16[384,768]{1,0:T(8,128)(2,1)}, u32[]{:S(2)}, u32[]{:S(2)}) collective-permute-start(bf16[384,768]{1,0:T(8,128)(2,1)} %shard_map.209.refs_3_), channel_id=1, source_target_pairs={{0,8},{4,12},{8,0},{12,4},{1,9},{5,13},{9,1},{13,5},{2,10},{6,14},... | collective-permute-start | bytes 1769480 | tf_op jit(solution)/shard_map/ppermute | solution.py:26
  72.8 47.2 %collective-permute-start.4 = (bf16[384,768]{1,0:T(8,128)(2,1)}, bf16[384,768]{1,0:T(8,128)(2,1)}, u32[]{:S(2)}, u32[]{:S(2)}) collective-permute-start(bf16[384,768]{1,0:T(8,128)(2,1)} %shard_map.209.refs_3_), channel_id=1, source_target_pairs={{0,4},{4,0},{8,12},{12,8},{1,5},{5,1},{9,13},{13,9},{2,6},{6,2},{1... | collective-permute-start | bytes 1769480 | tf_op jit(solution)/shard_map/ppermute | solution.py:26
  75.0 1.0 copy-start.7
  76.0 47.0 %copy-start.2 = (bf16[384,768]{1,0:T(8,128)(2,1)S(1)}, bf16[384,768]{1,0:T(8,128)(2,1)}, u32[]{:S(2)}) copy-start(bf16[384,768]{1,0:T(8,128)(2,1)} %shard_map.209.refs_3_) | copy-start | bytes 1769476
  139.0 0.7 copy-start.24
  139.0 143.3 %reduce-scatter.5.cloned.1.call-start = ((), (), s32[]{:S(2)}) async-start(), calls=%async_computation.9 | async-start | bytes 7077888 | tf_op jit(solution)/shard_map/reduce_scatter | solution.py:874
  139.7 1.2 collective-permute-start.7
  140.9 3.7 %collective-permute-start.10 = (f32[16,256]{1,0:T(8,128)S(1)}, f32[16,256]{1,0:T(8,128)S(1)}, u32[]{:S(2)}, u32[]{:S(2)}) collective-permute-start(f32[16,256]{1,0:T(8,128)S(1)} %add.91), channel_id=1, source_target_pairs={{0,16},{2,18},{16,0},{18,2},{1,17},{3,19},{17,1},{19,3},{4,20},{6,... | collective-permute-start | bytes 49160 | tf_op jit(solution)/shard_map/ppermute | solution.py:26
  142.4 3.7 %collective-permute-start.9 = (f32[16,256]{1,0:T(8,128)S(1)}, f32[16,256]{1,0:T(8,128)S(1)}, u32[]{:S(2)}, u32[]{:S(2)}) collective-permute-start(f32[16,256]{1,0:T(8,128)S(1)} %add.91), channel_id=1, source_target_pairs={{0,2},{2,0},{16,18},{18,16},{1,3},{3,1},{17,19},{19,17},{4,6},{6,4... | collective-permute-start | bytes 49160 | tf_op jit(solution)/shard_map/ppermute | solution.py:26
  142.9 4.6 %collective-permute-start.8 = (f32[16,256]{1,0:T(8,128)S(1)}, f32[16,256]{1,0:T(8,128)S(1)}, u32[]{:S(2)}, u32[]{:S(2)}) collective-permute-start(f32[16,256]{1,0:T(8,128)S(1)} %add.91), channel_id=1, source_target_pairs={{0,18},{2,16},{16,2},{18,0},{1,19},{3,17},{17,3},{19,1},{4,22},{6,... | collective-permute-start | bytes 49160 | tf_op jit(solution)/shard_map/ppermute | solution.py:26
  147.6 22.4 %copy-start.18 = (bf16[1536,768]{1,0:T(8,128)(2,1)S(1)}, bf16[1536,768]{1,0:T(8,128)(2,1)}, u32[]{:S(2)}) copy-start(bf16[1536,768]{1,0:T(8,128)(2,1)} %get-tuple-element.61.refs_5_) | copy-start | bytes 7077892
  147.6 22.4 %copy-start.19 = (bf16[1536,384]{1,0:T(8,128)(2,1)S(1)}, bf16[1536,384]{1,0:T(8,128)(2,1)}, u32[]{:S(2)}) copy-start(bf16[1536,384]{1,0:T(8,128)(2,1)} %get-tuple-element.62.refs_6_) | copy-start | bytes 3538948
  165.6 44.3 %collective-permute-start.11 = (bf16[384,768]{1,0:T(8,128)(2,1)}, bf16[384,768]{1,0:T(8,128)(2,1)S(1)}, u32[]{:S(2)}, u32[]{:S(2)}) collective-permute-start(bf16[384,768]{1,0:T(8,128)(2,1)} %get-tuple-element.70), channel_id=1, source_target_pairs={{0,8},{4,12},{8,0},{12,4},{1,9},{5,13},{9,1},{13,5},{2,10},{6,14},... | collective-permute-start | bytes 1769480 | tf_op jit(solution)/shard_map/ppermute | solution.py:26
  166.1 52.9 %collective-permute-start.12 = (bf16[384,768]{1,0:T(8,128)(2,1)}, bf16[384,768]{1,0:T(8,128)(2,1)S(1)}, u32[]{:S(2)}, u32[]{:S(2)}) collective-permute-start(bf16[384,768]{1,0:T(8,128)(2,1)} %get-tuple-element.71), channel_id=1, source_target_pairs={{0,12},{4,8},{8,4},{12,0},{1,13},{5,9},{9,5},{13,1},{2,14},{6,10},... | collective-permute-start | bytes 1769480 | tf_op jit(solution)/shard_map/ppermute | solution.py:26
  168.6 50.5 %collective-permute-start.13 = (bf16[384,768]{1,0:T(8,128)(2,1)}, bf16[384,768]{1,0:T(8,128)(2,1)}, u32[]{:S(2)}, u32[]{:S(2)}) collective-permute-start(bf16[384,768]{1,0:T(8,128)(2,1)} %get-tuple-element.72), channel_id=1, source_target_pairs={{0,4},{4,0},{8,12},{12,8},{1,5},{5,1},{9,13},{13,9},{2,6},{6,2},{1... | collective-permute-start | bytes 1769480 | tf_op jit(solution)/shard_map/ppermute | solution.py:26
  170.0 0.7 copy-start.20
  209.9 9.2 %copy-start.10 = (bf16[384,768]{1,0:T(8,128)(2,1)}, bf16[384,768]{1,0:T(8,128)(2,1)S(1)}, u32[]{:S(2)}) copy-start(bf16[384,768]{1,0:T(8,128)(2,1)S(1)} %collective-permute-done.11.refs_6_.refs_1_) | copy-start | bytes 1769476
  219.0 0.8 copy-start.12
  219.8 1.0 copy-start.22
  220.8 1.7 collective-permute-start.14
  222.6 0.7 copy-start.25
  223.3 2.1 copy-start.11
  223.3 2.1 copy-start.13
  225.4 1.0 copy-start.14
  226.5 1.1 copy-start.17
  227.6 48.3 %copy-start.15 = (bf16[432,512]{1,0:T(8,128)(2,1)S(1)}, bf16[432,512]{1,0:T(8,128)(2,1)}, u32[]{:S(2)}) copy-start(bf16[432,512]{1,0:T(8,128)(2,1)} %get-tuple-element.80.refs_4_.refs_0_) | copy-start | bytes 1327108
  229.9 46.0 %all-to-all-start.2 = ((bf16[8,48,768]{2,1,0:T(8,128)(2,1)}), bf16[8,48,768]{2,1,0:T(8,128)(2,1)S(1)}, u32[]{:S(2)}, u32[]{:S(2)}) async-start(bf16[8,48,768]{2,1,0:T(8,128)(2,1)} %shard_map.215), calls=%async_computation.4 | async-start | bytes 1179648 | tf_op jit(solution)/shard_map/all_to_all | solution.py:868
  233.4 18.1 %collective-permute-start.15 = (bf16[432,512]{1,0:T(8,128)(2,1)}, bf16[432,512]{1,0:T(8,128)(2,1)S(1)}, u32[]{:S(2)}, u32[]{:S(2)}) collective-permute-start(bf16[432,512]{1,0:T(8,128)(2,1)} %get-tuple-element.81), channel_id=1, source_target_pairs={{0,4},{4,0},{8,12},{12,8},{1,5},{5,1},{9,13},{13,9},{2,6},{6,2},{1... | collective-permute-start | bytes 1327112 | tf_op jit(solution)/shard_map/ppermute | solution.py:26
  233.5 22.0 %collective-permute-start.16 = (bf16[432,512]{1,0:T(8,128)(2,1)}, bf16[432,512]{1,0:T(8,128)(2,1)}, u32[]{:S(2)}, u32[]{:S(2)}) collective-permute-start(bf16[432,512]{1,0:T(8,128)(2,1)} %get-tuple-element.82), channel_id=1, source_target_pairs={{0,8},{4,12},{8,0},{12,4},{1,9},{5,13},{9,1},{13,5},{2,10},{6,14},... | collective-permute-start | bytes 1327112 | tf_op jit(solution)/shard_map/ppermute | solution.py:26
  234.7 41.2 %collective-permute-start.17 = (bf16[432,512]{1,0:T(8,128)(2,1)}, bf16[432,512]{1,0:T(8,128)(2,1)}, u32[]{:S(2)}, u32[]{:S(2)}) collective-permute-start(bf16[432,512]{1,0:T(8,128)(2,1)} %get-tuple-element.83), channel_id=1, source_target_pairs={{0,12},{4,8},{8,4},{12,0},{1,13},{5,9},{9,5},{13,1},{2,14},{6,10},... | collective-permute-start | bytes 1327112 | tf_op jit(solution)/shard_map/ppermute | solution.py:26
  275.9 2.6 copy-start.8
  278.4 15.9 %all-to-all-start.3 = ((bf16[8,80,640]{2,1,0:T(8,128)(2,1)}), bf16[8,80,640]{2,1,0:T(8,128)(2,1)S(1)}, u32[]{:S(2)}, u32[]{:S(2)}) async-start(bf16[8,80,640]{2,1,0:T(8,128)(2,1)} %shard_map.216), calls=%async_computation.5 | async-start | bytes 1638400 | tf_op jit(solution)/shard_map/all_to_all | solution.py:868
  282.3 1.7 copy-start.21
  286.9 10.2 %copy-start.5 = (bf16[256,1536]{1,0:T(8,128)(2,1)}, bf16[256,1536]{1,0:T(8,128)(2,1)S(1)}, u32[]{:S(2)}) copy-start(bf16[256,1536]{1,0:T(8,128)(2,1)S(1)} %get-tuple-element.94.refs_0_) | copy-start | bytes 2359300
  294.3 1.1 copy-start.9
Sparse Core Ops, SparseCore 0:
  23.0 51.9 all-gather.2
  77.5 45.5 all-gather.4
  139.2 61.7 reduce-scatter.2
  220.0 60.9 reduce-scatter.4

commit v6 on v5

--- a/solution.py
+++ b/solution.py
@@ -148,6 +148,28 @@
     row = lax.broadcasted_iota(jnp.int32, cotangent_ref.shape, 0)
     own = cotangent_ref[...].astype(jnp.float32)
     refs[-1][...] = jnp.where(row < lengths_ref[0], own, 0.0).astype(LOW)
+
+
+def hidden_kernel(grad_ref, hidden_ref, upstream_ref, gain_ref, out_ref):
+    stream = hidden_ref[...].astype(jnp.float32)
+    scale = lax.rsqrt(jnp.mean(stream * stream, axis=-1, keepdims=True) + EPSILON)
+    grad = grad_ref[...].astype(jnp.float32) * gain_ref[...]
+    along = jnp.mean(grad * stream, axis=-1, keepdims=True)
+    grad_stream = grad * scale - stream * (scale * scale * scale * along)
+    out_ref[...] = (upstream_ref[...].astype(jnp.float32) + grad_stream).astype(LOW)
+
+
+def hidden_gradient(grad, hidden, upstream, gain):
+    length, width = hidden.shape
+    block = pl.BlockSpec((length // 2, width), lambda index: (index, 0))
+    return pl.pallas_call(
+        hidden_kernel,
+        grid=(2,),
+        in_specs=[block] * 3 + [pl.BlockSpec(gain.shape, lambda index: (0, 0))],
+        out_specs=block,
+        out_shape=jax.ShapeDtypeStruct((length, width), LOW),
+        cost_estimate=pl.CostEstimate(flops=int(2e9), bytes_accessed=1 << 20, transcendentals=0),
+    )(grad, hidden, upstream, gain)
 
 
 def copy_kernel(value_ref, *refs):
@@ -668,12 +690,12 @@
     )(*terms, *waits)
 
 
-def owner_outputs(early, owned, rows, heads, states, sizes, waits):
+def owner_outputs(early, owned, gain, rows, heads, states, sizes, waits):
     proj, inner_all, taps_shape, model = sizes
     ranks = owned.shape[0]
     inner = inner_all // ranks
 
-    def blocks(early_ref, ref, store):
+    def blocks(early_ref, ref, divisor_ref, store):
         def lanes_of(value, rank):
             lane = lax.broadcasted_iota(jnp.int32, value.shape, 1)
             value = jnp.where(lane < heads, value, 0.0)
@@ -712,20 +734,22 @@
         bias_ref[:, inner_all + states :] = shared[11:12, :states]
         wide = inner + states
         for part in range(3):
-            pre_ref[:, part * wide : (part + 1) * wide] = shared[7 + part : 8 + part]
+            lanes = slice(part * wide, (part + 1) * wide)
+            pre_ref[:, lanes] = shared[7 + part : 8 + part] / divisor_ref[:, lanes]
         head_ref[0:1, :] = dt_sum
         head_ref[1:2, :] = alog_sum
         head_ref[2:3, :] = skip_sum
 
     shapes = [(rows, proj), (rows, inner_all), taps_shape, (1, taps_shape[1]), (1, inner_all), (1, model), (8, LANES)]
     return pl.pallas_call(
-        lambda early_ref, ref, *refs: blocks(early_ref, ref, refs[len(waits) :]),
+        lambda early_ref, ref, divisor_ref, *refs: blocks(early_ref, ref, divisor_ref, refs[len(waits) :]),
         in_specs=[pl.BlockSpec(array.shape, lambda: (0, 0, 0)) for array in (early, owned)]
+        + [pl.BlockSpec(gain.shape, lambda: (0, 0))]
         + [pl.BlockSpec(memory_space=pl.ANY)] * len(waits),
         out_shape=[jax.ShapeDtypeStruct(shape, jnp.float32) for shape in shapes],
         compiler_params=pltpu.CompilerParams(vmem_limit_bytes=24 << 20),
         cost_estimate=pl.CostEstimate(flops=int(3e9), bytes_accessed=1 << 20, transcendentals=0),
-    )(early, owned, *waits)
+    )(early, owned, gain, *waits)
 
 
 def pack_weights(in_weight, out_weight, ranks, heads):
@@ -888,12 +912,11 @@
     late_pieces = gather_rows(late_columns)
 
     stream = hidden_in.astype(jnp.float32)
-    scale = lax.rsqrt(jnp.mean(stream * stream, axis=-1, keepdims=True) + EPSILON)
     valid = (jnp.arange(length) < lengths[0])[:, None]
-    own_upstream = jnp.where(valid, cotangent, jnp.zeros_like(cotangent))
     own_normed = copies(norm_kernel, (), hidden_in, (pre_gain[None],), 1, (conv_plane,))
     normed = gather_tokens(own_normed)
-    upstream = gather_tokens(copies(mask_kernel, (lengths,), cotangent, (), 1, (own_normed,)))
+    own_masked = copies(mask_kernel, (lengths,), cotangent, (), 1, (own_normed,))
+    upstream = gather_tokens(own_masked)
 
     def of_rank(value, count):
         return lax.dynamic_slice_in_dim(value, rank * count, count, axis=-1)
@@ -996,10 +1019,7 @@
         conv_moved = [cross(pieces[away], LINE, away, 4) for away in (1, 2, 3)]
     else:
         conv_moved = []
-    grad_own = scatter_far(grad_normed) * pre_gain
-    along = jnp.mean(grad_own * stream, axis=-1, keepdims=True)
-    grad_stream = grad_own * scale - stream * (scale**3 * along)
-    grad_hidden = (own_upstream.astype(jnp.float32) + grad_stream).astype(LOW)
+    grad_hidden = hidden_gradient(scatter_far(grad_normed), hidden_in, own_masked, pre_gain[None])
 
     if direct:
         early_owned = exchange(side_sums([early[0], *early_moved], ranks, False, pieces[:1]))
@@ -1020,12 +1040,12 @@
         owned = exchange(jnp.concatenate([conv, below], axis=1))
     sizes_out = (in_weight.shape[1], inner_all, conv_weight.shape, model)
     owned_in, owned_out, taps_grad, bias_grad, gain_grads, pre_grad, head_grads = owner_outputs(
-        early_owned, owned, rows + -rows % 16, heads, states, sizes_out, (output,)
+        early_owned, owned, pre_gain[None], rows + -rows % 16, heads, states, sizes_out, (output,)
     )
     return (
         output,
         grad_hidden,
-        pre_grad[0] / pre_gain,
+        pre_grad[0],
         owned_in[:rows],
         taps_grad,
         bias_grad[0],

time: 307 us -> 305 us (level)
    ppermute x15, waiting for transfers between devices: 103 us -> 99.7 us  [cross(): return lax.ppermute(value, axes, [(i, i ^ distance) for i in range(count)])]
  transfers between devices with their start and end apart: 26 -> 26, of which waited for: 17 -> 17; matrix products, arithmetic and copies ran while one was open for 3% -> 2% of each run, Pallas kernels for 28% -> 29%
where the time goes in v6:
time: 305 us; the launch traced here: 304 us
  waiting for transfers between devices  129 us (42%)
  Pallas kernels  109 us (36%)
  starting transfers between devices  36.7 us (12%)
  between operations  14.8 us (5%)
  local copies, waits for them, and re-layouts  10.7 us (4%)
  other arithmetic  3.64 us (1%)
    ppermute x15, waiting for transfers between devices, cross(): return lax.ppermute(value, axes, [(i, i ^ distance) for i in range(count)])  99.7 us
    pallas_call x4, Pallas kernels, run_slots(): pl.pallas_call(run, grid_spec=pltpu.PrefetchScalarGridSpec(num_scalar_pre...  93.9 us
    ppermute x15, starting transfers between devices, cross(): return lax.ppermute(value, axes, [(i, i ^ distance) for i in range(count)])  21.3 us
    all_to_all x4, waiting for transfers between devices, exchange(): return lax.all_to_all(value, PLANE, split_axis=0, concat_axis=0, tiled=True)  18.9 us
    all_to_all x4, starting transfers between devices, exchange(): return lax.all_to_all(value, PLANE, split_axis=0, concat_axis=0, tiled=True)  14.8 us
    unnamed x58, local copies, waits for them, and re-layouts  7.87 us
    all_gather x2, waiting for transfers between devices, gather_tokens(): return lax.all_gather(value, PLANE, axis=0, tiled=True)  7.85 us
  transfers between devices with their start and end apart: 26, of which 17 were waited for; matrix products, arithmetic and copies ran while one was open for 2% of the time, Pallas kernels for 29%

profile of v6, /device:TPU:16, one launch (start us, length us, event | category | flops | bytes accessed | tf_op | source)
XLA Modules:
  0.0 304.0 jit_solution(9802913192961397787)
XLA Ops:
  7.2 2.3 shard_map.203
  9.5 3.7 %all-to-all-start = ((bf16[8,48,640]{2,1,0:T(8,128)(2,1)}), bf16[8,48,640]{2,1,0:T(8,128)(2,1)S(1)}, u32[]{:S(2)}, u32[]{:S(2)}) async-start(bf16[8,48,640]{2,1,0:T(8,128)(2,1)} %get-tuple-element.51), calls=%async_computation | async-start | bytes 983040 | tf_op jit(solution)/shard_map/all_to_all | solution.py:892
  13.3 8.4 %all-to-all-done = bf16[8,48,640]{2,1,0:T(8,128)(2,1)S(1)} async-done(((bf16[8,48,640]{2,1,0:T(8,128)(2,1)}), bf16[8,48,640]{2,1,0:T(8,128)(2,1)S(1)}, u32[]{:S(2)}, u32[]{:S(2)}) %all-to-all-start) | async-done | bytes 491552 | tf_op jit(solution)/shard_map/all_to_all | solution.py:892
  21.7 1.2 shard_map.204.refs_0_
  23.6 1.0 shard_map.205.upstream_ref
  24.7 1.9 shard_map.206.refs_1_
  26.6 0.5 collective-permute-start.2
  27.1 3.5 %collective-permute-start.1 = (bf16[400,512]{1,0:T(8,128)(2,1)}, bf16[400,512]{1,0:T(8,128)(2,1)S(1)}, u32[]{:S(2)}, u32[]{:S(2)}) collective-permute-start(bf16[400,512]{1,0:T(8,128)(2,1)} %shard_map.206.refs_1_), channel_id=1, source_target_pairs={{0,8},{4,12},{8,0},{12,4},{1,9},{5,13},{9,1},{13,5},{2,10},{6,14},... | collective-permute-start | bytes 1228808 | tf_op jit(solution)/shard_map/ppermute | solution.py:26
  30.7 0.9 slice.44
  31.6 3.7 %all-to-all-start.1 = ((bf16[8,48,768]{2,1,0:T(8,128)(2,1)}), bf16[8,48,768]{2,1,0:T(8,128)(2,1)S(1)}, u32[]{:S(2)}, u32[]{:S(2)}) async-start(bf16[8,48,768]{2,1,0:T(8,128)(2,1)} %shard_map.208), calls=%async_computation.1 | async-start | bytes 1179648 | tf_op jit(solution)/shard_map/all_to_all | solution.py:892
  35.4 21.5 %collective-permute-done.2.refs_4_ = bf16[400,512]{1,0:T(8,128)(2,1)S(1)} collective-permute-done((bf16[400,512]{1,0:T(8,128)(2,1)}, bf16[400,512]{1,0:T(8,128)(2,1)S(1)}, u32[]{:S(2)}, u32[]{:S(2)}) %collective-permute-start.2) | collective-permute-done | bytes 409632 | tf_op jit(solution)/shard_map/ppermute | solution.py:26
  56.8 5.5 %collective-permute-done.1.refs_3_ = bf16[400,512]{1,0:T(8,128)(2,1)S(1)} collective-permute-done((bf16[400,512]{1,0:T(8,128)(2,1)}, bf16[400,512]{1,0:T(8,128)(2,1)S(1)}, u32[]{:S(2)}, u32[]{:S(2)}) %collective-permute-start.1) | collective-permute-done | bytes 409632 | tf_op jit(solution)/shard_map/ppermute | solution.py:26
  62.4 0.9 pad_maximum_fusion
  63.5 0.8 dynamic_slice.27
  64.6 0.8 copy-done
  65.4 1.6 collective-permute-start.6
  67.0 4.2 %collective-permute-start.5 = (bf16[384,768]{1,0:T(8,128)(2,1)}, bf16[384,768]{1,0:T(8,128)(2,1)}, u32[]{:S(2)}, u32[]{:S(2)}) collective-permute-start(bf16[384,768]{1,0:T(8,128)(2,1)} %shard_map.209.refs_3_), channel_id=1, source_target_pairs={{0,8},{4,12},{8,0},{12,4},{1,9},{5,13},{9,1},{13,5},{2,10},{6,14},... | collective-permute-start | bytes 1769480 | tf_op jit(solution)/shard_map/ppermute | solution.py:26
  71.2 3.9 %all-gather.3.cloned.1.call-done.refs_0_.refs_4_ = bf16[2048,1536]{1,0:T(8,128)(2,1)} async-done(((bf16[256,1536]{1,0:T(8,128)(2,1)}), bf16[2048,1536]{1,0:T(8,128)(2,1)}) %all-gather.3.cloned.1.call-update) | async-done | bytes 6291472 | tf_op jit(solution)/shard_map/all_gather | solution.py:895
  75.0 1.0 copy-done.6
  76.0 18.9 %shard_map.207 = (f32[2048,768]{1,0:T(8,128)}, f32[2048,384]{1,0:T(8,128)}, bf16[1536,768]{1,0:T(8,128)(2,1)}) custom-call(s32[9]{0:T(128)S(1)} %stack.39.place_ref, bf16[2048,1536]{1,0:T(8,128)(2,1)} %all-gather.3.cloned.1.call-done.refs_0_.refs_4_, bf16[400,512]{1,0:T(8,128)(2,1)S(1)} %copy-done.15, bf16[400,512]{1,0:T(8,128)(2,1)S(1)} %copy-done.6, ...), custom_call_target="tpu_custom_call" | custom-call | flops 12000000000 | bytes 1048576 | tf_op jit(solution)/shard_map/pallas_call | solution.py:591
  94.9 12.2 %collective-permute-done.6.refs_6_ = bf16[384,768]{1,0:T(8,128)(2,1)} collective-permute-done((bf16[384,768]{1,0:T(8,128)(2,1)}, bf16[384,768]{1,0:T(8,128)(2,1)}, u32[]{:S(2)}, u32[]{:S(2)}) %collective-permute-start.6) | collective-permute-done | bytes 589856 | tf_op jit(solution)/shard_map/ppermute | solution.py:26
  107.1 11.4 %collective-permute-done.5.refs_5_ = bf16[384,768]{1,0:T(8,128)(2,1)} collective-permute-done((bf16[384,768]{1,0:T(8,128)(2,1)}, bf16[384,768]{1,0:T(8,128)(2,1)}, u32[]{:S(2)}, u32[]{:S(2)}) %collective-permute-start.5) | collective-permute-done | bytes 589856 | tf_op jit(solution)/shard_map/ppermute | solution.py:26
  118.5 4.0 %all-gather.5.cloned.1.call-done.refs_1_ = bf16[2048,1536]{1,0:T(8,128)(2,1)} async-done(((bf16[256,1536]{1,0:T(8,128)(2,1)}), bf16[2048,1536]{1,0:T(8,128)(2,1)}) %all-gather.5.cloned.1.call-update) | async-done | bytes 6291472 | tf_op jit(solution)/shard_map/all_gather | solution.py:895
  122.5 16.0 %shard_map.210 = (f32[2048,384]{1,0:T(8,128)}, f32[2048,384]{1,0:T(8,128)}, bf16[2048,1536]{1,0:T(8,128)(2,1)}, f32[16,256]{1,0:T(8,128)}, bf16[1536,384]{1,0:T(8,128)(2,1)}) custom-call(s32[9]{0:T(128)S(1)} %stack.39.place_ref, bf16[2048,1536]{1,0:T(8,128)(2,1)} %all-gather.3.cloned.1.call-done.refs_0_.refs_4_, ...), custom_call_target="tpu_custom_call" | custom-call | flops 14000000000 | bytes 1048576 | tf_op jit(solution)/shard_map/pallas_call | solution.py:591
  138.5 0.2 reduce-scatter.5.cloned.1.call-start
  138.7 0.5 copy-done.23
  139.1 0.3 collective-permute-start.7
  139.4 0.9 collective-permute-done.7
  140.3 1.5 collective-permute-start.10
  141.8 0.6 collective-permute-start.9
  142.4 1.5 collective-permute-start.8
  143.8 0.2 collective-permute-done.10
  144.1 1.5 collective-permute-done.9
  145.5 1.5 collective-permute-done.8
  147.0 17.9 %shard_map.211 = (bf16[2048,384]{1,0:T(8,128)(2,1)}, f32[2048,384]{1,0:T(8,128)}, f32[8,384]{1,0:T(8,128)}, bf16[384,768]{1,0:T(8,128)(2,1)}, bf16[384,768]{1,0:...) custom-call(s32[9]{0:T(128)S(1)} %stack.39.place_ref, ...), custom_call_target="tpu_custom_call" | custom-call | flops 16000000000 | bytes 1048576 | tf_op jit(solution)/shard_map/pallas_call | solution.py:591
  164.9 0.6 collective-permute-start.11
  165.5 2.4 collective-permute-start.12
  167.9 1.4 collective-permute-start.13
  169.4 0.7 copy-done.21
  170.1 41.1 %shard_map.212 = (bf16[2048,1536]{1,0:T(8,128)(2,1)}, bf16[1536,128]{1,0:T(8,128)(2,1)}, bf16[432,512]{1,0:T(8,128)(2,1)}, bf16[432,512]{1,0:T(8,128)(2,1)}, bf1...) custom-call(s32[9]{0:T(128)S(1)} %stack.39.place_ref, f32[2048,768]{1,0:T(8,128)} %get-tuple-element.56.refs_0_, ...), custom_call_target="tpu_custom_call" | custom-call | flops 30000001024 | bytes 1048576 | tf_op jit(solution)/shard_map/pallas_call | solution.py:591
  211.2 7.2 %collective-permute-done.12.refs_7_.refs_2_ = bf16[384,768]{1,0:T(8,128)(2,1)S(1)} collective-permute-done((bf16[384,768]{1,0:T(8,128)(2,1)}, bf16[384,768]{1,0:T(8,128)(2,1)S(1)}, u32[]{:S(2)}, u32[]{:S(2)}) %collective-permute-start.12) | collective-permute-done | bytes 589856 | tf_op jit(solution)/shard_map/ppermute | solution.py:26
  218.5 0.8 copy-done.9
  219.5 0.9 copy-done.22
  220.5 1.7 collective-permute-done.14.refs_4_
  222.2 0.8 copy-done.25
  222.9 2.0 shard_map.215
  225.0 1.0 copy-done.13
  226.0 1.1 copy-done.18
  227.1 1.1 shard_map.216
  228.2 3.5 %all-to-all-start.2 = ((bf16[8,48,768]{2,1,0:T(8,128)(2,1)}), bf16[8,48,768]{2,1,0:T(8,128)(2,1)S(1)}, u32[]{:S(2)}, u32[]{:S(2)}) async-start(bf16[8,48,768]{2,1,0:T(8,128)(2,1)} %shard_map.216), calls=%async_computation.4 | async-start | bytes 1179648 | tf_op jit(solution)/shard_map/all_to_all | solution.py:892
  231.9 1.1 collective-permute-start.16
  232.9 2.4 collective-permute-start.17
  235.3 14.5 %collective-permute-done.15.refs_1_ = bf16[432,512]{1,0:T(8,128)(2,1)S(1)} collective-permute-done((bf16[432,512]{1,0:T(8,128)(2,1)}, bf16[432,512]{1,0:T(8,128)(2,1)S(1)}, u32[]{:S(2)}, u32[]{:S(2)}) %collective-permute-start.15) | collective-permute-done | bytes 442400 | tf_op jit(solution)/shard_map/ppermute | solution.py:26
  249.8 3.9 %collective-permute-done.16.refs_2_ = bf16[432,512]{1,0:T(8,128)(2,1)S(1)} collective-permute-done((bf16[432,512]{1,0:T(8,128)(2,1)}, bf16[432,512]{1,0:T(8,128)(2,1)S(1)}, u32[]{:S(2)}, u32[]{:S(2)}) %collective-permute-start.16) | collective-permute-done | bytes 442400 | tf_op jit(solution)/shard_map/ppermute | solution.py:26
  253.7 20.5 %collective-permute-done.17.refs_3_ = bf16[432,512]{1,0:T(8,128)(2,1)S(1)} collective-permute-done((bf16[432,512]{1,0:T(8,128)(2,1)}, bf16[432,512]{1,0:T(8,128)(2,1)S(1)}, u32[]{:S(2)}, u32[]{:S(2)}) %collective-permute-start.17) | collective-permute-done | bytes 442400 | tf_op jit(solution)/shard_map/ppermute | solution.py:26
  274.1 1.2 shard_map.217
  275.3 3.9 %all-to-all-start.3 = ((bf16[8,80,640]{2,1,0:T(8,128)(2,1)}), bf16[8,80,640]{2,1,0:T(8,128)(2,1)S(1)}, u32[]{:S(2)}, u32[]{:S(2)}) async-start(bf16[8,80,640]{2,1,0:T(8,128)(2,1)} %shard_map.217), calls=%async_computation.5 | async-start | bytes 1638400 | tf_op jit(solution)/shard_map/all_to_all | solution.py:892
  279.2 1.5 select_convert_fusion.refs_0_
  280.7 10.5 %all-to-all-done.3.ref = bf16[8,80,640]{2,1,0:T(8,128)(2,1)S(1)} async-done(((bf16[8,80,640]{2,1,0:T(8,128)(2,1)}), bf16[8,80,640]{2,1,0:T(8,128)(2,1)S(1)}, u32[]{:S(2)}, u32[]{:S(2)}) %all-to-all-start.3) | async-done | bytes 819232 | tf_op jit(solution)/shard_map/all_to_all | solution.py:892
  291.2 1.7 shard_map.218
  292.9 0.6 reduce
  293.5 0.6 reduce.1
  294.2 0.5 slice_bitcast_fusion
  294.7 2.7 shard_map.214
  (102 shorter events, 1.3 us)
Async XLA Ops:
  7.2 6.1 %copy-start.24 = (f32[1536]{0:T(1024)S(1)}, f32[1536]{0:T(1024)}, u32[]{:S(2)}) copy-start(f32[1536]{0:T(1024)} %param.15) | copy-start | bytes 18436
  7.2 14.5 %copy-start.3 = (bf16[256,1536]{1,0:T(8,128)(2,1)S(1)}, bf16[256,1536]{1,0:T(8,128)(2,1)}, u32[]{:S(2)}) copy-start(bf16[256,1536]{1,0:T(8,128)(2,1)} %hidden_ref.3) | copy-start | bytes 2359300
  9.5 12.2 %all-to-all-start = ((bf16[8,48,640]{2,1,0:T(8,128)(2,1)}), bf16[8,48,640]{2,1,0:T(8,128)(2,1)S(1)}, u32[]{:S(2)}, u32[]{:S(2)}) async-start(bf16[8,48,640]{2,1,0:T(8,128)(2,1)} %get-tuple-element.51), calls=%async_computation | async-start | bytes 983040 | tf_op jit(solution)/shard_map/all_to_all | solution.py:892
  13.2 61.8 %all-gather.3.cloned.1.call-start = ((), (), s32[]{:S(2)}) async-start(), calls=%async_computation.6 | async-start | bytes 7077888 | tf_op jit(solution)/shard_map/all_gather | solution.py:895
  13.3 277.9 %copy-start.16 = (f32[1,1536]{1,0:T(1,128)}, f32[1,1536]{1,0:T(1,128)S(1)}, u32[]{:S(2)}) copy-start(f32[1,1536]{1,0:T(1,128)S(1)} %broadcast_in_dim.35.gain_ref.divisor_ref) | copy-start | bytes 18436
  21.7 1.2 copy-start.2
  21.7 1.9 copy-start.17
  22.9 99.5 %all-gather.5.cloned.1.call-start = ((), (), s32[]{:S(2)}) async-start(), calls=%async_computation.7 | async-start | bytes 7077888 | tf_op jit(solution)/shard_map/all_gather | solution.py:895
  24.7 5.9 %slice-start.3 = ((f32[3328]{0:T(1024)}), f32[3072]{0:T(1024)S(1)}, s32[]{:S(2)}) async-start(f32[3328]{0:T(1024)} %param.18), calls=%async_computation.13 | async-start | bytes 24576 | tf_op jit(solution)/shard_map/slice | solution.py:927
  26.6 36.6 %slice-start.2 = ((f32[3328]{0:T(1024)}), f32[256]{0:T(256)S(1)}, s32[]{:S(2)}) async-start(f32[3328]{0:T(1024)} %param.18), calls=%async_computation.12 | async-start | bytes 2048 | tf_op jit(solution)/shard_map/slice | solution.py:927
  26.6 36.7 %copy-start.26 = (f32[48]{0:T(128)S(1)}, f32[48]{0:T(128)}, u32[]{:S(2)}) copy-start(f32[48]{0:T(128)} %param.19) | copy-start | bytes 580
  26.6 36.8 %copy-start.27 = (f32[48]{0:T(128)S(1)}, f32[48]{0:T(128)}, u32[]{:S(2)}) copy-start(f32[48]{0:T(128)} %param.20) | copy-start | bytes 580
  26.6 36.8 %copy-start.28 = (f32[48]{0:T(128)S(1)}, f32[48]{0:T(128)}, u32[]{:S(2)}) copy-start(f32[48]{0:T(128)} %param.21) | copy-start | bytes 580
  26.6 37.9 %slice-start.1 = ((f32[4,3328]{1,0:T(4,128)}), f32[4,3072]{1,0:T(4,128)S(1)}, s32[]{:S(2)}) async-start(f32[4,3328]{1,0:T(4,128)} %param.17), calls=%async_computation.11 | async-start | bytes 98304 | tf_op jit(solution)/shard_map/slice | solution.py:925
  26.6 37.9 %slice-start = ((f32[4,3328]{1,0:T(4,128)}), f32[4,256]{1,0:T(4,128)S(1)}, s32[]{:S(2)}) async-start(f32[4,3328]{1,0:T(4,128)} %param.17), calls=%async_computation.10 | async-start | bytes 8192 | tf_op jit(solution)/shard_map/slice | solution.py:925
  26.6 30.2 %collective-permute-start.2 = (bf16[400,512]{1,0:T(8,128)(2,1)}, bf16[400,512]{1,0:T(8,128)(2,1)S(1)}, u32[]{:S(2)}, u32[]{:S(2)}) collective-permute-start(bf16[400,512]{1,0:T(8,128)(2,1)} %shard_map.206.refs_1_), channel_id=1, source_target_pairs={{0,12},{4,8},{8,4},{12,0},{1,13},{5,9},{9,5},{13,1},{2,14},{6,10},... | collective-permute-start | bytes 1228808 | tf_op jit(solution)/shard_map/ppermute | solution.py:26
  27.1 35.2 %collective-permute-start.1 = (bf16[400,512]{1,0:T(8,128)(2,1)}, bf16[400,512]{1,0:T(8,128)(2,1)S(1)}, u32[]{:S(2)}, u32[]{:S(2)}) collective-permute-start(bf16[400,512]{1,0:T(8,128)(2,1)} %shard_map.206.refs_1_), channel_id=1, source_target_pairs={{0,8},{4,12},{8,0},{12,4},{1,9},{5,13},{9,1},{13,5},{2,10},{6,14},... | collective-permute-start | bytes 1228808 | tf_op jit(solution)/shard_map/ppermute | solution.py:26
  30.6 31.7 %collective-permute-start = (bf16[400,512]{1,0:T(8,128)(2,1)}, bf16[400,512]{1,0:T(8,128)(2,1)S(1)}, u32[]{:S(2)}, u32[]{:S(2)}) collective-permute-start(bf16[400,512]{1,0:T(8,128)(2,1)} %shard_map.206.refs_1_), channel_id=1, source_target_pairs={{0,4},{4,0},{8,12},{12,8},{1,5},{5,1},{9,13},{13,9},{2,6},{6,2},{1... | collective-permute-start | bytes 1228808 | tf_op jit(solution)/shard_map/ppermute | solution.py:26
  31.6 43.4 %copy-start.15 = (bf16[400,512]{1,0:T(8,128)(2,1)S(1)}, bf16[400,512]{1,0:T(8,128)(2,1)}, u32[]{:S(2)}) copy-start(bf16[400,512]{1,0:T(8,128)(2,1)} %shard_map.206.refs_1_) | copy-start | bytes 1228804
  31.6 32.9 %all-to-all-start.1 = ((bf16[8,48,768]{2,1,0:T(8,128)(2,1)}), bf16[8,48,768]{2,1,0:T(8,128)(2,1)S(1)}, u32[]{:S(2)}, u32[]{:S(2)}) async-start(bf16[8,48,768]{2,1,0:T(8,128)(2,1)} %shard_map.208), calls=%async_computation.1 | async-start | bytes 1179648 | tf_op jit(solution)/shard_map/all_to_all | solution.py:892
  35.3 183.2 %reduce-scatter.3.cloned.1.call-start = ((), (), s32[]{:S(2)}) async-start(), calls=%async_computation.8 | async-start | bytes 7077888 | tf_op jit(solution)/shard_map/reduce_scatter | solution.py:898
  62.3 2.3 copy-start.5
  63.2 7.9 %collective-permute-start.3 = (bf16[1536,128]{1,0:T(8,128)(2,1)}, bf16[1536,128]{1,0:T(8,128)(2,1)S(1)}, u32[]{:S(2)}, u32[]{:S(2)}) collective-permute-start(bf16[1536,128]{1,0:T(8,128)(2,1)} %pad_maximum_fusion), channel_id=1, source_target_pairs={{0,1},{1,0},{2,3},{3,2},{4,5},{5,4},{6,7},{7,6},{8,9},{9,8},{10,11... | collective-permute-start | bytes 1179656 | tf_op jit(solution)/shard_map/ppermute | solution.py:22
  64.6 0.8 copy-start
  65.4 41.7 %collective-permute-start.6 = (bf16[384,768]{1,0:T(8,128)(2,1)}, bf16[384,768]{1,0:T(8,128)(2,1)}, u32[]{:S(2)}, u32[]{:S(2)}) collective-permute-start(bf16[384,768]{1,0:T(8,128)(2,1)} %shard_map.209.refs_3_), channel_id=1, source_target_pairs={{0,12},{4,8},{8,4},{12,0},{1,13},{5,9},{9,5},{13,1},{2,14},{6,10},... | collective-permute-start | bytes 1769480 | tf_op jit(solution)/shard_map/ppermute | solution.py:26
  67.0 51.5 %collective-permute-start.5 = (bf16[384,768]{1,0:T(8,128)(2,1)}, bf16[384,768]{1,0:T(8,128)(2,1)}, u32[]{:S(2)}, u32[]{:S(2)}) collective-permute-start(bf16[384,768]{1,0:T(8,128)(2,1)} %shard_map.209.refs_3_), channel_id=1, source_target_pairs={{0,8},{4,12},{8,0},{12,4},{1,9},{5,13},{9,1},{13,5},{2,10},{6,14},... | collective-permute-start | bytes 1769480 | tf_op jit(solution)/shard_map/ppermute | solution.py:26
  71.1 47.3 %collective-permute-start.4 = (bf16[384,768]{1,0:T(8,128)(2,1)}, bf16[384,768]{1,0:T(8,128)(2,1)}, u32[]{:S(2)}, u32[]{:S(2)}) collective-permute-start(bf16[384,768]{1,0:T(8,128)(2,1)} %shard_map.209.refs_3_), channel_id=1, source_target_pairs={{0,4},{4,0},{8,12},{12,8},{1,5},{5,1},{9,13},{13,9},{2,6},{6,2},{1... | collective-permute-start | bytes 1769480 | tf_op jit(solution)/shard_map/ppermute | solution.py:26
  75.0 1.0 copy-start.6
  76.0 46.4 %copy-start.1 = (bf16[384,768]{1,0:T(8,128)(2,1)S(1)}, bf16[384,768]{1,0:T(8,128)(2,1)}, u32[]{:S(2)}) copy-start(bf16[384,768]{1,0:T(8,128)(2,1)} %shard_map.209.refs_3_) | copy-start | bytes 1769476
  138.4 0.7 copy-start.23
  138.5 156.2 %reduce-scatter.5.cloned.1.call-start = ((), (), s32[]{:S(2)}) async-start(), calls=%async_computation.9 | async-start | bytes 7077888 | tf_op jit(solution)/shard_map/reduce_scatter | solution.py:898
  139.1 1.2 collective-permute-start.7
  140.3 3.7 %collective-permute-start.10 = (f32[16,256]{1,0:T(8,128)S(1)}, f32[16,256]{1,0:T(8,128)S(1)}, u32[]{:S(2)}, u32[]{:S(2)}) collective-permute-start(f32[16,256]{1,0:T(8,128)S(1)} %add.74), channel_id=1, source_target_pairs={{0,16},{2,18},{16,0},{18,2},{1,17},{3,19},{17,1},{19,3},{4,20},{6,... | collective-permute-start | bytes 49160 | tf_op jit(solution)/shard_map/ppermute | solution.py:26
  141.8 3.7 %collective-permute-start.9 = (f32[16,256]{1,0:T(8,128)S(1)}, f32[16,256]{1,0:T(8,128)S(1)}, u32[]{:S(2)}, u32[]{:S(2)}) collective-permute-start(f32[16,256]{1,0:T(8,128)S(1)} %add.74), channel_id=1, source_target_pairs={{0,2},{2,0},{16,18},{18,16},{1,3},{3,1},{17,19},{19,17},{4,6},{6,4... | collective-permute-start | bytes 49160 | tf_op jit(solution)/shard_map/ppermute | solution.py:26
  142.4 4.6 %collective-permute-start.8 = (f32[16,256]{1,0:T(8,128)S(1)}, f32[16,256]{1,0:T(8,128)S(1)}, u32[]{:S(2)}, u32[]{:S(2)}) collective-permute-start(f32[16,256]{1,0:T(8,128)S(1)} %add.74), channel_id=1, source_target_pairs={{0,18},{2,16},{16,2},{18,0},{1,19},{3,17},{17,3},{19,1},{4,22},{6,... | collective-permute-start | bytes 49160 | tf_op jit(solution)/shard_map/ppermute | solution.py:26
  147.0 22.4 %copy-start.19 = (bf16[1536,768]{1,0:T(8,128)(2,1)S(1)}, bf16[1536,768]{1,0:T(8,128)(2,1)}, u32[]{:S(2)}) copy-start(bf16[1536,768]{1,0:T(8,128)(2,1)} %get-tuple-element.61.refs_5_) | copy-start | bytes 7077892
  147.0 22.4 %copy-start.20 = (bf16[1536,384]{1,0:T(8,128)(2,1)S(1)}, bf16[1536,384]{1,0:T(8,128)(2,1)}, u32[]{:S(2)}) copy-start(bf16[1536,384]{1,0:T(8,128)(2,1)} %get-tuple-element.62.refs_6_) | copy-start | bytes 3538948
  164.9 46.3 %collective-permute-start.11 = (bf16[384,768]{1,0:T(8,128)(2,1)}, bf16[384,768]{1,0:T(8,128)(2,1)S(1)}, u32[]{:S(2)}, u32[]{:S(2)}) collective-permute-start(bf16[384,768]{1,0:T(8,128)(2,1)} %get-tuple-element.70), channel_id=1, source_target_pairs={{0,8},{4,12},{8,0},{12,4},{1,9},{5,13},{9,1},{13,5},{2,10},{6,14},... | collective-permute-start | bytes 1769480 | tf_op jit(solution)/shard_map/ppermute | solution.py:26
  165.5 52.9 %collective-permute-start.12 = (bf16[384,768]{1,0:T(8,128)(2,1)}, bf16[384,768]{1,0:T(8,128)(2,1)S(1)}, u32[]{:S(2)}, u32[]{:S(2)}) collective-permute-start(bf16[384,768]{1,0:T(8,128)(2,1)} %get-tuple-element.71), channel_id=1, source_target_pairs={{0,12},{4,8},{8,4},{12,0},{1,13},{5,9},{9,5},{13,1},{2,14},{6,10},... | collective-permute-start | bytes 1769480 | tf_op jit(solution)/shard_map/ppermute | solution.py:26
  167.9 50.5 %collective-permute-start.13 = (bf16[384,768]{1,0:T(8,128)(2,1)}, bf16[384,768]{1,0:T(8,128)(2,1)S(1)}, u32[]{:S(2)}, u32[]{:S(2)}) collective-permute-start(bf16[384,768]{1,0:T(8,128)(2,1)} %get-tuple-element.72), channel_id=1, source_target_pairs={{0,4},{4,0},{8,12},{12,8},{1,5},{5,1},{9,13},{13,9},{2,6},{6,2},{1... | collective-permute-start | bytes 1769480 | tf_op jit(solution)/shard_map/ppermute | solution.py:26
  169.4 0.7 copy-start.21
  211.2 7.2 %copy-start.7 = (bf16[384,768]{1,0:T(8,128)(2,1)}, bf16[384,768]{1,0:T(8,128)(2,1)S(1)}, u32[]{:S(2)}) copy-start(bf16[384,768]{1,0:T(8,128)(2,1)S(1)} %collective-permute-done.11.refs_6_.refs_1_) | copy-start | bytes 1769476
  218.4 0.8 copy-start.9
  218.4 1.0 copy-start.11
  219.5 1.0 copy-start.22
  219.5 5.5 %copy-start.8 = (bf16[384,768]{1,0:T(8,128)(2,1)S(1)}, bf16[384,768]{1,0:T(8,128)(2,1)}, u32[]{:S(2)}) copy-start(bf16[384,768]{1,0:T(8,128)(2,1)} %copy-done.7) | copy-start | bytes 1769476
  219.5 5.5 %copy-start.10 = (bf16[384,768]{1,0:T(8,128)(2,1)S(1)}, bf16[384,768]{1,0:T(8,128)(2,1)}, u32[]{:S(2)}) copy-start(bf16[384,768]{1,0:T(8,128)(2,1)} %copy-done.9) | copy-start | bytes 1769476
  219.5 5.5 %copy-start.12 = (bf16[384,768]{1,0:T(8,128)(2,1)S(1)}, bf16[384,768]{1,0:T(8,128)(2,1)}, u32[]{:S(2)}) copy-start(bf16[384,768]{1,0:T(8,128)(2,1)} %copy-done.11) | copy-start | bytes 1769476
  220.4 1.7 collective-permute-start.14
  222.2 0.8 copy-start.25
  225.0 1.0 copy-start.13
  226.0 1.1 copy-start.18
  227.1 47.0 %copy-start.14 = (bf16[432,512]{1,0:T(8,128)(2,1)S(1)}, bf16[432,512]{1,0:T(8,128)(2,1)}, u32[]{:S(2)}) copy-start(bf16[432,512]{1,0:T(8,128)(2,1)} %get-tuple-element.80.refs_4_.refs_0_) | copy-start | bytes 1327108
  228.2 45.9 %all-to-all-start.2 = ((bf16[8,48,768]{2,1,0:T(8,128)(2,1)}), bf16[8,48,768]{2,1,0:T(8,128)(2,1)S(1)}, u32[]{:S(2)}, u32[]{:S(2)}) async-start(bf16[8,48,768]{2,1,0:T(8,128)(2,1)} %shard_map.216), calls=%async_computation.4 | async-start | bytes 1179648 | tf_op jit(solution)/shard_map/all_to_all | solution.py:892
  231.8 18.0 %collective-permute-start.15 = (bf16[432,512]{1,0:T(8,128)(2,1)}, bf16[432,512]{1,0:T(8,128)(2,1)S(1)}, u32[]{:S(2)}, u32[]{:S(2)}) collective-permute-start(bf16[432,512]{1,0:T(8,128)(2,1)} %get-tuple-element.81), channel_id=1, source_target_pairs={{0,4},{4,0},{8,12},{12,8},{1,5},{5,1},{9,13},{13,9},{2,6},{6,2},{1... | collective-permute-start | bytes 1327112 | tf_op jit(solution)/shard_map/ppermute | solution.py:26
  231.9 21.8 %collective-permute-start.16 = (bf16[432,512]{1,0:T(8,128)(2,1)}, bf16[432,512]{1,0:T(8,128)(2,1)S(1)}, u32[]{:S(2)}, u32[]{:S(2)}) collective-permute-start(bf16[432,512]{1,0:T(8,128)(2,1)} %get-tuple-element.82), channel_id=1, source_target_pairs={{0,8},{4,12},{8,0},{12,4},{1,9},{5,13},{9,1},{13,5},{2,10},{6,14},... | collective-permute-start | bytes 1327112 | tf_op jit(solution)/shard_map/ppermute | solution.py:26
  232.9 41.2 %collective-permute-start.17 = (bf16[432,512]{1,0:T(8,128)(2,1)}, bf16[432,512]{1,0:T(8,128)(2,1)S(1)}, u32[]{:S(2)}, u32[]{:S(2)}) collective-permute-start(bf16[432,512]{1,0:T(8,128)(2,1)} %get-tuple-element.83), channel_id=1, source_target_pairs={{0,12},{4,8},{8,4},{12,0},{1,13},{5,9},{9,5},{13,1},{2,14},{6,10},... | collective-permute-start | bytes 1327112 | tf_op jit(solution)/shard_map/ppermute | solution.py:26
  275.3 15.9 %all-to-all-start.3 = ((bf16[8,80,640]{2,1,0:T(8,128)(2,1)}), bf16[8,80,640]{2,1,0:T(8,128)(2,1)S(1)}, u32[]{:S(2)}, u32[]{:S(2)}) async-start(bf16[8,80,640]{2,1,0:T(8,128)(2,1)} %shard_map.217), calls=%async_computation.5 | async-start | bytes 1638400 | tf_op jit(solution)/shard_map/all_to_all | solution.py:892
  280.7 12.2 %copy-start.4 = (bf16[256,1536]{1,0:T(8,128)(2,1)}, bf16[256,1536]{1,0:T(8,128)(2,1)S(1)}, u32[]{:S(2)}) copy-start(bf16[256,1536]{1,0:T(8,128)(2,1)S(1)} %select_convert_fusion.refs_0_) | copy-start | bytes 2359300
Sparse Core Ops, SparseCore 0:
  23.0 51.9 all-gather.2
  76.9 45.5 all-gather.4
  138.6 61.7 reduce-scatter.2
  219.6 60.8 reduce-scatter.4
